TPU v7x, 32 devices: a whole 2x2x4 slice. The times are simulated.
32 devices in a mesh: seq: 8 (over y, x, core), dp: 4 (over z).
Axes of the slice: x: 2, y: 2, z: 4, core: 2. Of those that a mesh axis runs over, the one named last changes fastest.
Arguments:
- query: bfloat16 [4, 1024, 2048], P('dp', 'seq'), may hold values from -6 to 6
- keys: bfloat16 [4, 1024, 512], P('dp', 'seq'), may hold values from -6 to 6
- values: bfloat16 [4, 1024, 512], P('dp', 'seq'), may hold values from -6 to 6
- out_grad: bfloat16 [4, 1024, 2048], P('dp', 'seq'), may hold values from -16 to 16
- normed_input: bfloat16 [4, 1024, 4096], P('dp', 'seq'), may hold values from -6 to 6
- q_start: int32 [8], P('dp'), may hold values from 256 to 383, as said below
- q_len: int32 [8], P('dp'), may hold values from 1 to 64, as said below
Outputs:
- q_grad: bfloat16 [4, 1024, 2048], P('dp', 'seq')
- k_grad: bfloat16 [4, 1024, 512], P('dp', 'seq')
- v_grad: bfloat16 [4, 1024, 512], P('dp', 'seq')
- kv_weight_grad: float32 [4096, 1024], P(('seq', 'dp'))
Inputs may be any that keep to these rules, and one draw needn't show every extreme that they name: `q_start`: the visual part of each sequence ends here. `q_len`: tokens after the question are padding.
All inputs are finite; a program needn't handle non-finite values.
Results may differ from a plain program's by a relative error of at most 0.013.
Values may be sent and summed in bfloat16 or wider, within the bound.
No kernel may reach another device: no remote copies, remote signals or barrier semaphores. Data moves between devices by JAX's collectives and lax.ppermute only.
A program may use at most 128 MiB of HBM per device.

v0:
```python
import math

import jax
import jax.numpy as jnp
from jax import lax
from jax.sharding import PartitionSpec as P

HEADS = 16
KV_HEADS = 4
HEAD_DIM = 128


def local(query, keys, values, out_grad, normed_input, q_start, q_len):
    seq_count = lax.axis_size("seq")
    tokens_dev = query.shape[1]
    repeat_by = HEADS // KV_HEADS
    classes = max(1, seq_count // HEADS)
    heads_dev = HEADS * classes // seq_count
    head_groups = seq_count // classes
    class_tokens = tokens_dev // classes
    seq_len = tokens_dev * seq_count // 2
    group_tokens = tokens_dev * seq_count
    width_dev = heads_dev * HEAD_DIM
    my_class = lax.axis_index("seq") // head_groups
    score_scale = 1.0 / math.sqrt(HEAD_DIM)

    def to_units(array):
        return array.reshape(class_tokens, seq_count, width_dev)

    query_units = to_units(query[0])
    grad_units = to_units(out_grad[0])
    key_wide = jnp.repeat(
        keys[0].reshape(tokens_dev, KV_HEADS, HEAD_DIM), repeat_by, axis=1
    ).reshape(tokens_dev, HEADS * HEAD_DIM)
    value_wide = jnp.repeat(
        values[0].reshape(tokens_dev, KV_HEADS, HEAD_DIM), repeat_by, axis=1
    ).reshape(tokens_dev, HEADS * HEAD_DIM)
    wide_shape = (tokens_dev, classes, head_groups, width_dev)
    key_units = jnp.broadcast_to(
        key_wide.reshape(tokens_dev, 1, head_groups, width_dev), wide_shape
    ).reshape(tokens_dev, seq_count, width_dev)
    value_units = jnp.broadcast_to(
        value_wide.reshape(tokens_dev, 1, head_groups, width_dev), wide_shape
    ).reshape(tokens_dev, seq_count, width_dev)
    query_got, grad_got, key_got, value_got = (
        lax.all_to_all(query_units, "seq", split_axis=1, concat_axis=0, tiled=True),
        lax.all_to_all(grad_units, "seq", split_axis=1, concat_axis=0, tiled=True),
        lax.all_to_all(key_units, "seq", split_axis=1, concat_axis=0, tiled=True),
        lax.all_to_all(value_units, "seq", split_axis=1, concat_axis=0, tiled=True),
    )
    key_rows = key_got.reshape(group_tokens, heads_dev, HEAD_DIM)
    value_rows = value_got.reshape(group_tokens, heads_dev, HEAD_DIM)
    query_rows = query_got.reshape(seq_count * class_tokens, heads_dev, HEAD_DIM)
    grad_rows = grad_got.reshape(seq_count * class_tokens, heads_dev, HEAD_DIM)
    block_rows = min(512, seq_len // classes)
    blocks_seq = seq_len // classes // block_rows
    key_pos = jnp.arange(seq_len, dtype=jnp.int32)

    def one_block(block_idx, carry):
        query_acc, key_acc, value_acc = carry
        seq_idx = block_idx // blocks_seq
        first_row = block_idx * block_rows
        key_first = seq_idx * seq_len
        query_block = lax.dynamic_slice_in_dim(query_rows, first_row, block_rows, 0)
        grad_block = lax.dynamic_slice_in_dim(grad_rows, first_row, block_rows, 0)
        key_block = lax.dynamic_slice_in_dim(key_rows, key_first, seq_len, 0)
        value_block = lax.dynamic_slice_in_dim(value_rows, key_first, seq_len, 0)
        start_pos = lax.dynamic_index_in_dim(q_start, seq_idx, 0, keepdims=False)
        end_pos = start_pos + lax.dynamic_index_in_dim(q_len, seq_idx, 0, keepdims=False)
        query_pos = (
            (first_row + jnp.arange(block_rows, dtype=jnp.int32)) * classes + my_class - key_first
        )
        visible = (key_pos[None, :] < end_pos) & (
            (key_pos[None, :] <= query_pos[:, None]) | (key_pos[None, :] < start_pos)
        )
        scores = (
            jnp.einsum("qhd,khd->hqk", query_block, key_block, preferred_element_type=jnp.float32)
            * score_scale
        )
        scores = jnp.where(visible[None], scores, -jnp.inf)
        row_max = jnp.max(scores, axis=-1, keepdims=True)
        exponent = jnp.where(visible[None], jnp.exp(scores - row_max), 0.0)
        probability = exponent / jnp.sum(exponent, axis=-1, keepdims=True)
        prob_low = probability.astype(jnp.bfloat16)
        dprob = jnp.einsum(
            "qhd,khd->hqk", grad_block, value_block, preferred_element_type=jnp.float32
        )
        row_delta = jnp.sum(probability * dprob, axis=-1, keepdims=True)
        dscore = (probability * (dprob - row_delta) * score_scale).astype(jnp.bfloat16)
        query_grad = jnp.einsum(
            "hqk,khd->qhd", dscore, key_block, preferred_element_type=jnp.float32
        ).astype(jnp.bfloat16)
        query_acc = lax.dynamic_update_slice_in_dim(query_acc, query_grad, first_row, 0)
        key_part = lax.dynamic_slice_in_dim(key_acc, key_first, seq_len, 0) + jnp.einsum(
            "hqk,qhd->khd", dscore, query_block, preferred_element_type=jnp.float32
        )
        value_part = lax.dynamic_slice_in_dim(value_acc, key_first, seq_len, 0) + jnp.einsum(
            "hqk,qhd->khd", prob_low, grad_block, preferred_element_type=jnp.float32
        )
        key_acc = lax.dynamic_update_slice_in_dim(key_acc, key_part, key_first, 0)
        value_acc = lax.dynamic_update_slice_in_dim(value_acc, value_part, key_first, 0)
        return (query_acc, key_acc, value_acc)

    start_state = (
        jnp.zeros((seq_count * class_tokens, heads_dev, HEAD_DIM), jnp.bfloat16),
        jnp.zeros((group_tokens, heads_dev, HEAD_DIM), jnp.float32),
        jnp.zeros((group_tokens, heads_dev, HEAD_DIM), jnp.float32),
    )
    query_acc, key_acc, value_acc = lax.fori_loop(0, 2 * blocks_seq, one_block, start_state)
    query_back = lax.all_to_all(
        query_acc.reshape(seq_count, class_tokens, 1, width_dev),
        "seq",
        split_axis=0,
        concat_axis=2,
        tiled=True,
    )
    query_grad_out = query_back.reshape(tokens_dev, HEADS * HEAD_DIM)
    key_back, value_back = (
        lax.all_to_all(
            key_acc.reshape(seq_count, tokens_dev, 1, width_dev).astype(jnp.bfloat16),
            "seq",
            split_axis=0,
            concat_axis=2,
            tiled=True,
        ).astype(jnp.float32),
        lax.all_to_all(
            value_acc.reshape(seq_count, tokens_dev, 1, width_dev).astype(jnp.bfloat16),
            "seq",
            split_axis=0,
            concat_axis=2,
            tiled=True,
        ).astype(jnp.float32),
    )
    key_grad_out = (
        key_back.reshape(tokens_dev, classes, KV_HEADS, repeat_by, HEAD_DIM)
        .sum(axis=(1, 3))
        .astype(jnp.bfloat16)
        .reshape(tokens_dev, KV_HEADS * HEAD_DIM)
    )
    value_grad_out = (
        value_back.reshape(tokens_dev, classes, KV_HEADS, repeat_by, HEAD_DIM)
        .sum(axis=(1, 3))
        .astype(jnp.bfloat16)
        .reshape(tokens_dev, KV_HEADS * HEAD_DIM)
    )
    joined = jnp.concatenate([key_grad_out, value_grad_out], axis=1)
    hidden_rows = normed_input[0]
    weight_out = lax.psum_scatter(
        jnp.einsum("tr,tc->rc", hidden_rows, joined, preferred_element_type=jnp.float32),
        ("seq", "dp"),
        scatter_dimension=0,
        tiled=True,
    )
    return (query_grad_out[None], key_grad_out[None], value_grad_out[None], weight_out)


def solution(mesh):
    in_specs = (
        P("dp", "seq", None),
        P("dp", "seq", None),
        P("dp", "seq", None),
        P("dp", "seq", None),
        P("dp", "seq", None),
        P("dp"),
        P("dp"),
    )
    out_specs = (
        P("dp", "seq", None),
        P("dp", "seq", None),
        P("dp", "seq", None),
        P(("seq", "dp"), None),
    )
    return jax.shard_map(local, mesh=mesh, in_specs=in_specs, out_specs=out_specs, check_vma=False)
```

profile of v0, /device:TPU:0, one launch (start us, length us, event | category | flops | bytes accessed | tf_op | source)
XLA Modules:
  0.0 517.7 jit_solution(14875414930006477504)
XLA Ops:
  7.2 1.1 copy.110
  9.2 5.2 all-to-all-start.3
  15.5 8.7 %all-to-all-done.3 = bf16[128,8,256]{0,2,1:T(8,128)(2,1)S(1)} async-done(((bf16[128,8,256]{0,2,1:T(8,128)(2,1)}), bf16[128,8,256]{0,2,1:T(8,128)(2,1)S(1)}, u32[]{:S(2)}, u32[]{:S(2)}) %all-to-all-start.3) | async-done | bytes 524320 | tf_op jit(solution)/shard_map/all_to_all | solution.py:49
  25.0 3.5 all-to-all-start
  29.6 8.7 %all-to-all-done = bf16[128,8,256]{0,2,1:T(8,128)(2,1)S(1)} async-done(((bf16[128,8,256]{0,2,1:T(8,128)(2,1)}), bf16[128,8,256]{0,2,1:T(8,128)(2,1)S(1)}, u32[]{:S(2)}, u32[]{:S(2)}) %all-to-all-start) | async-done | bytes 524320 | tf_op jit(solution)/shard_map/all_to_all | solution.py:48
  38.2 3.5 all-to-all-start.1
  42.7 8.7 %all-to-all-done.1 = bf16[128,8,256]{0,2,1:T(8,128)(2,1)S(1)} async-done(((bf16[128,8,256]{0,2,1:T(8,128)(2,1)}), bf16[128,8,256]{0,2,1:T(8,128)(2,1)S(1)}, u32[]{:S(2)}, u32[]{:S(2)}) %all-to-all-start.1) | async-done | bytes 524320 | tf_op jit(solution)/shard_map/all_to_all | solution.py:46
  51.4 3.5 all-to-all-start.2
  54.9 1.1 copy.90
  56.1 2.1 reshape.215
  60.9 3.7 all-to-all-done.2
  67.9 1.1 broadcast.126
  69.1 39.2 %while.21 = (s32[]{:T(128)}, bf16[1024,2,128]{0,2,1:T(8,128)(2,1)}, f32[1024,2,128]{0,2,1:T(8,128)}, f32[1024,2,128]{0,2,1:T(8,128)}, bf16[1024,2,128]{0,2,1:T(8...) while((s32[]{:T(128)}, bf16[1024,2,128]{0,2,1:T(8,128)(2,1)}, ...), condition=%wide.region_4.5_spmd.clone.clone, body=%wide.region_0.4_spmd.clone.clone.sunk | while | flops 683284480 | bytes 30182676 | solution.py:109
  72.4 3.5 fusion.114
  75.9 3.1 fusion.117
  79.1 1.4 fusion.112
  80.5 4.0 fusion.115
  84.5 4.1 fusion.116
  91.9 3.5 fusion.114
  95.5 3.1 fusion.117
  98.6 1.4 fusion.112
  100.1 4.0 fusion.115
  104.1 4.2 fusion.116
  108.2 1.4 convert_element_type.153
  110.6 3.5 all-to-all-start.6
  115.2 8.6 %all-to-all-done.6 = bf16[8,128,1,256]{1,3,2,0:T(8,128)(2,1)S(1)} async-done(((bf16[8,128,1,256]{1,3,2,0:T(8,128)(2,1)}), bf16[8,128,1,256]{1,3,2,0:T(8,128)(2,1)S(1)}, u32[]{:S(2)}, u32[]{:S(2)}) %all-to-all-start.6) | async-done | bytes 524320 | tf_op jit(solution)/shard_map/all_to_all | solution.py:126
  123.8 3.5 all-to-all-start.5
  127.4 9.5 %all-to-all-done.5 = bf16[8,128,1,256]{1,3,2,0:T(8,128)(2,1)S(1)} async-done(((bf16[8,128,1,256]{1,3,2,0:T(8,128)(2,1)}), bf16[8,128,1,256]{1,3,2,0:T(8,128)(2,1)S(1)}, u32[]{:S(2)}, u32[]{:S(2)}) %all-to-all-start.5) | async-done | bytes 524320 | tf_op jit(solution)/shard_map/all_to_all | solution.py:119
  137.1 8.0 %convolution_bitcast_fusion.1 = f32[4096,1024]{0,1:T(8,128)} fusion(bf16[1,128,4096]{2,1,0:T(8,128)(2,1)S(1)} %copy-done, bf16[128,512]{0,1:T(8,128)(2,1)S(1)} %bitcast.117, bf16[128,512]{0,1:T(8,128)(2,1)S(1)} %bitcast.119), kind=kOutput, calls=%fused_computation.54 | convolution fusion | flops 1074266112 | bytes 18087936 | tf_op jit(solution)/shard_map/tr,tc->rc/dot_general | solution.py:149
  146.6 13.2 %all_to_all.93 = bf16[8,128,1,256]{3,1,2,0:T(8,128)(2,1)S(1)} all-to-all(bf16[8,128,1,256]{3,1,2,0:T(8,128)(2,1)S(1)} %copy.111), channel_id=1, replica_groups=mesh['seq'=8,'dp'=4] {'seq'}, dimensions={0} | all-to-all | bytes 1048576 | tf_op jit(solution)/shard_map/all_to_all | solution.py:110
  162.7 346.2 %reduce-scatter.2.cloned.1.call-done = f32[128,1024]{0,1:T(8,128)} async-done(((f32[4096,1024]{0,1:T(8,128)}), f32[128,1024]{0,1:T(8,128)}) %reduce-scatter.2.cloned.1.call-update) | async-done | bytes 524304 | tf_op jit(solution)/shard_map/reduce_scatter | solution.py:148
  508.9 2.0 copy.102
  (56 shorter events, 21.6 us)
Async XLA Ops:
  7.2 129.9 %copy-start = (bf16[1,128,4096]{2,1,0:T(8,128)(2,1)S(1)}, bf16[1,128,4096]{2,1,0:T(8,128)(2,1)}, u32[]{:S(2)}) copy-start(bf16[1,128,4096]{2,1,0:T(8,128)(2,1)} %param.13) | copy-start | bytes 3145732
  7.2 21.4 %copy-start.4 = (bf16[1,128,2048]{2,1,0:T(8,128)(2,1)S(1)}, bf16[1,128,2048]{2,1,0:T(8,128)(2,1)}, u32[]{:S(2)}) copy-start(bf16[1,128,2048]{2,1,0:T(8,128)(2,1)} %param.9) | copy-start | bytes 1572868
  9.2 14.9 %all-to-all-start.3 = ((bf16[128,8,256]{0,2,1:T(8,128)(2,1)}), bf16[128,8,256]{0,2,1:T(8,128)(2,1)S(1)}, u32[]{:S(2)}, u32[]{:S(2)}) async-start(bf16[128,8,256]{0,2,1:T(8,128)(2,1)} %bitcast.11), calls=%async_computation.3 | async-start | bytes 1048576 | tf_op jit(solution)/shard_map/all_to_all | solution.py:49
  14.4 27.3 %copy-start.5 = (bf16[1,128,2048]{2,1,0:T(8,128)(2,1)S(1)}, bf16[1,128,2048]{2,1,0:T(8,128)(2,1)}, u32[]{:S(2)}) copy-start(bf16[1,128,2048]{2,1,0:T(8,128)(2,1)} %param.12) | copy-start | bytes 1572868
  25.0 13.2 %all-to-all-start = ((bf16[128,8,256]{0,2,1:T(8,128)(2,1)}), bf16[128,8,256]{0,2,1:T(8,128)(2,1)S(1)}, u32[]{:S(2)}, u32[]{:S(2)}) async-start(bf16[128,8,256]{0,2,1:T(8,128)(2,1)} %bitcast.1), calls=%async_computation | async-start | bytes 1048576 | tf_op jit(solution)/shard_map/all_to_all | solution.py:48
  38.2 13.2 %all-to-all-start.1 = ((bf16[128,8,256]{0,2,1:T(8,128)(2,1)}), bf16[128,8,256]{0,2,1:T(8,128)(2,1)S(1)}, u32[]{:S(2)}, u32[]{:S(2)}) async-start(bf16[128,8,256]{0,2,1:T(8,128)(2,1)} %bitcast.4), calls=%async_computation.1 | async-start | bytes 1048576 | tf_op jit(solution)/shard_map/all_to_all | solution.py:46
  51.4 13.2 %all-to-all-start.2 = ((bf16[128,8,256]{0,2,1:T(8,128)(2,1)}), bf16[128,8,256]{0,2,1:T(8,128)(2,1)S(1)}, u32[]{:S(2)}, u32[]{:S(2)}) async-start(bf16[128,8,256]{0,2,1:T(8,128)(2,1)} %bitcast.7), calls=%async_computation.2 | async-start | bytes 1048576 | tf_op jit(solution)/shard_map/all_to_all | solution.py:47
  64.9 4.1 copy-start.6
  64.9 4.1 copy-start.7
  75.9 3.1 copy-start.1
  95.5 3.1 copy-start.1
  108.2 5.9 %copy-start.2 = (f32[1024,2,128]{0,2,1:T(8,128)S(1)}, f32[1024,2,128]{0,2,1:T(8,128)}, u32[]{:S(2)}) copy-start(f32[1024,2,128]{0,2,1:T(8,128)} %get-tuple-element.301) | copy-start | bytes 3145732
  110.6 13.2 %all-to-all-start.6 = ((bf16[8,128,1,256]{1,3,2,0:T(8,128)(2,1)}), bf16[8,128,1,256]{1,3,2,0:T(8,128)(2,1)S(1)}, u32[]{:S(2)}, u32[]{:S(2)}) async-start(bf16[8,128,1,256]{1,3,2,0:T(8,128)(2,1)} %copy.98), calls=%async_computation.6 | async-start | bytes 1048576 | tf_op jit(solution)/shard_map/all_to_all | solution.py:126
  123.8 13.2 %all-to-all-start.5 = ((bf16[8,128,1,256]{1,3,2,0:T(8,128)(2,1)}), bf16[8,128,1,256]{1,3,2,0:T(8,128)(2,1)S(1)}, u32[]{:S(2)}, u32[]{:S(2)}) async-start(bf16[8,128,1,256]{1,3,2,0:T(8,128)(2,1)} %copy.97), calls=%async_computation.5 | async-start | bytes 1048576 | tf_op jit(solution)/shard_map/all_to_all | solution.py:119
  127.3 381.6 %reduce-scatter.2.cloned.1.call-start = ((), (), s32[]{:S(2)}) async-start(), calls=%async_computation.8 | async-start | bytes 17301504 | tf_op jit(solution)/shard_map/reduce_scatter | solution.py:148
  145.1 1.0 copy-start.3
Sparse Core Ops, SparseCore 0:
  145.3 363.5 reduce-scatter.1
where the time goes:
time: 519 us; the launch traced here: 518 us
  waiting for transfers between devices  394 us (76%)
  matrix products  40.5 us (8%)
  local copies, waits for them, and re-layouts  27.1 us (5%)
  starting transfers between devices  22.7 us (4%)
  between operations  14.2 us (3%)
  blocking collectives  13.2 us (3%)
    reduce_scatter x1, waiting for transfers between devices, local(): lax.psum_scatter(jnp.einsum('tr,tc->rc', hidden_rows, joined, preferred_e...  346 us
    all_to_all x1, blocking collectives, local(): lax.all_to_all(query_acc.reshape(seq_count, class_tokens, 1, width_dev),...  13.2 us
  transfers between devices with their start and end apart: 7, of which 7 were waited for; matrix products, arithmetic and copies ran while one was open for 3% of the time, Pallas kernels for 0%

commit v1 on v0

--- a/solution.py
+++ b/solution.py
@@ -1,8 +1,11 @@
+import functools
 import math
 
 import jax
 import jax.numpy as jnp
 from jax import lax
+from jax.experimental import pallas as pl
+from jax.experimental.pallas import tpu as pltpu
 from jax.sharding import PartitionSpec as P
 
 HEADS = 16
@@ -154,6 +157,262 @@
     return (query_grad_out[None], key_grad_out[None], value_grad_out[None], weight_out)
 
 
+def swap(array, axis, bit):
+    size = lax.axis_size(axis)
+    return lax.ppermute(array, axis, [(i, i ^ bit) for i in range(size)])
+
+
+def dot(left, right, dims):
+    return lax.dot_general(left, right, (dims, ((), ())), preferred_element_type=jnp.float32)
+
+
+def lanes(start, width):
+    return pl.ds(pl.multiple_of(start, 128), width)
+
+
+def call(body, outs, args, scratch=(), smem=0, flops=0, vmem=40):
+    specs = [pl.BlockSpec(memory_space=pltpu.VMEM)] * (len(args) - smem)
+    specs += [pl.BlockSpec(memory_space=pltpu.SMEM)] * smem
+    shapes = [jax.ShapeDtypeStruct(shape, dtype) for shape, dtype in outs]
+    moved = sum(math.prod(s.shape) * s.dtype.itemsize for s in [*shapes, *args])
+    return pl.pallas_call(
+        body,
+        out_shape=shapes,
+        in_specs=specs,
+        out_specs=[pl.BlockSpec(memory_space=pltpu.VMEM)] * len(shapes),
+        scratch_shapes=list(scratch),
+        compiler_params=pltpu.CompilerParams(vmem_limit_bytes=vmem * 2**20),
+        cost_estimate=pl.CostEstimate(flops=flops, bytes_accessed=moved, transcendentals=0),
+    )(*args)
+
+
+BF16, F32 = jnp.bfloat16, jnp.float32
+
+
+def local_pairs(query, keys, values, out_grad, normed_input, q_start, q_len):
+    tokens = query.shape[1]
+    width = HEADS * HEAD_DIM // 2
+    kv_width = KV_HEADS * HEAD_DIM // 2
+    own_heads = KV_HEADS // 2
+    repeat_by = HEADS // KV_HEADS
+    group_width = repeat_by * HEAD_DIM
+    seq_len = 4 * tokens
+    seen = seq_len * 7 // 8
+    model = normed_input.shape[2]
+    pair_rows = model // 4
+    planes = lax.axis_size("dp")
+    part_rows = pair_rows // 2 // planes
+    score_scale = 1.0 / math.sqrt(HEAD_DIM)
+    query, keys, values, out_grad, hidden = query[0], keys[0], values[0], out_grad[0], normed_input[0]
+
+    def place():
+        me = lax.axis_index("seq")
+        return me % 2, me % 4, me // 4
+
+    def split_heads(query_ref, grad_ref, key_ref, value_ref, kv_mine, kv_other, send):
+        core, _, _ = place()
+        for half, kv_out in ((core, kv_mine), (1 - core, kv_other)):
+            kv_out[:, :kv_width] = key_ref[:, lanes(half * kv_width, kv_width)]
+            kv_out[:, kv_width:] = value_ref[:, lanes(half * kv_width, kv_width)]
+        send[:, :width] = query_ref[:, lanes((1 - core) * width, width)]
+        send[:, width : 2 * width] = grad_ref[:, lanes((1 - core) * width, width)]
+        send[:, 2 * width :] = kv_other[...]
+
+    kv_mine, kv_other, core_send = call(
+        split_heads,
+        [((tokens, 2 * kv_width), BF16), ((tokens, 2 * kv_width), BF16), ((tokens, 2 * width + 2 * kv_width), BF16)],
+        (query, out_grad, keys, values),
+    )
+    kv_far = swap(kv_mine, "seq", 2)
+    kv_cross = swap(kv_other, "seq", 3)
+    core_got = swap(core_send, "seq", 1)
+
+    def split_hidden(hidden_ref, *outs):
+        pair = lax.axis_index("seq") // 2
+        for flip in range(4):
+            target = jnp.bitwise_xor(pair, flip)
+            outs[flip][...] = hidden_ref[:, lanes(target * pair_rows, pair_rows)]
+
+    hidden_mine, *hidden_send = call(split_hidden, [((tokens, pair_rows), BF16)] * 4, (hidden,))
+    hidden_got = [swap(hidden_send[flip - 1], "seq", 2 * flip) for flip in (1, 2, 3)]
+
+    def turn_hidden(mine, far, other, other_far, out):
+        half = place()[1] // 2
+        for block, (ref, spot) in enumerate(((mine, half), (far, 1 - half), (other, half), (other_far, 1 - half))):
+            out[:, lanes((block // 2) * 2 * tokens + spot * tokens, tokens)] = ref[...].T
+
+    (hidden_core,) = call(turn_hidden, [((pair_rows, 4 * tokens), BF16)], (hidden_mine, *hidden_got))
+    hidden_pair = swap(hidden_core, "seq", 1)
+
+    def attention(head, query_ref, grad_ref, kv0, got, kv2, kv3, start_ref, len_ref, part, part_low, mine, other, key_all, value_all):
+        core, spot, seq_idx = place()
+        base = 2 * width
+        for flip, ref, offset in ((0, kv0, 0), (1, got, base), (2, kv2, 0), (3, kv3, 0)):
+            rows = pl.ds(pl.multiple_of(jnp.bitwise_xor(spot, flip) * tokens, tokens), tokens)
+            key_all[rows, :] = ref[:, offset + head * HEAD_DIM : offset + (head + 1) * HEAD_DIM]
+            first = offset + kv_width + head * HEAD_DIM
+            value_all[rows, :] = ref[:, first : first + HEAD_DIM]
+        key = key_all[:seen, :]
+        value = value_all[:seen, :]
+        start = start_ref[seq_idx]
+        end = start + len_ref[seq_idx]
+        columns = repeat_by * tokens
+        row = lax.broadcasted_iota(jnp.int32, (1, columns), 1) % tokens
+        key_pos = lax.broadcasted_iota(jnp.int32, (seen, columns), 0)
+        for side, out in enumerate((mine, other)):
+            if side == 0:
+                blocks = [
+                    [ref[:, lanes(core * width + head * group_width + r * HEAD_DIM, HEAD_DIM)] for r in range(repeat_by)]
+                    for ref in (query_ref, grad_ref)
+                ]
+            else:
+                blocks = [
+                    [got[:, first + r * HEAD_DIM : first + (r + 1) * HEAD_DIM] for r in range(repeat_by)]
+                    for first in (head * group_width, width + head * group_width)
+                ]
+            query_rows = jnp.concatenate(blocks[0], axis=0)
+            grad_rows = jnp.concatenate(blocks[1], axis=0)
+            query_pos = jnp.bitwise_xor(spot, side) * tokens + row
+            limit = jnp.minimum(end, jnp.maximum(start, query_pos + 1))
+            scores = dot(key, query_rows, ((1,), (1,)))
+            scores = jnp.where(key_pos < limit, scores, -jnp.inf)
+            row_max = jnp.max(scores, axis=0, keepdims=True)
+            exponent = jnp.exp((scores - row_max) * score_scale)
+            probability = exponent * (1.0 / jnp.sum(exponent, axis=0, keepdims=True))
+            dprob = dot(value, grad_rows, ((1,), (1,)))
+            row_delta = jnp.sum(probability * dprob, axis=0, keepdims=True)
+            dscore = (probability * (dprob - row_delta)).astype(BF16)
+            key_part = dot(dscore, query_rows, ((1,), (0,))) * score_scale
+            value_part = dot(probability.astype(BF16), grad_rows, ((1,), (0,)))
+            if side == 0:
+                part[:, :HEAD_DIM] = key_part
+                part[:, HEAD_DIM:] = value_part
+            else:
+                part[:, :HEAD_DIM] += key_part
+                part[:, HEAD_DIM:] += value_part
+            query_grad = dot(key, dscore, ((0,), (0,))) * score_scale
+            for r in range(repeat_by):
+                out[:, r * HEAD_DIM : (r + 1) * HEAD_DIM] = query_grad[:, r * tokens : (r + 1) * tokens].T.astype(BF16)
+        part_low[...] = part[...].astype(BF16)
+
+    def add_parts(part, far, out):
+        out[...] = (part[...] + far[...].astype(F32)).astype(BF16)
+
+    def weight(core_ref, pair_ref, own, other, *outs_and_scratch):
+        *outs, rows_core, rows_pair = outs_and_scratch
+        core, _, _ = place()
+        plane = lax.axis_index("dp")
+        for seq, ref in enumerate((own, other)):
+            padded = jnp.concatenate([ref[...], jnp.zeros((seq_len - seen, 2 * HEAD_DIM), BF16)], axis=0)
+            for half in range(2):
+                first = jnp.where(core == 0, 0, 1)
+                low = padded[2 * half * tokens : (2 * half + 1) * tokens]
+                high = padded[(2 * half + 1) * tokens : (2 * half + 2) * tokens]
+                spot = (2 * seq + half) * tokens
+                rows_core[spot : spot + tokens, :] = jnp.where(first == 0, low, high)
+                rows_pair[spot : spot + tokens, :] = jnp.where(first == 0, high, low)
+        for flip, out in enumerate(outs):
+            target = jnp.bitwise_xor(plane, flip)
+            for owner in range(2):
+                rows = pl.ds(pl.multiple_of((owner * planes + target) * part_rows, part_rows), part_rows)
+                total = dot(core_ref[rows, :], rows_core[...], ((1,), (0,)))
+                total += dot(pair_ref[rows, :], rows_pair[...], ((1,), (0,)))
+                out[owner * part_rows : (owner + 1) * part_rows, :] = total.astype(out.dtype)
+
+    grads, query_parts, weight_parts = [], [], []
+    for head in range(own_heads):
+        part, part_low, query_mine, query_other = call(
+            functools.partial(attention, head),
+            [
+                ((seen, 2 * HEAD_DIM), F32),
+                ((seen, 2 * HEAD_DIM), BF16),
+                ((tokens, group_width), BF16),
+                ((tokens, group_width), BF16),
+            ],
+            (query, out_grad, kv_mine, core_got, kv_far, kv_cross, q_start, q_len),
+            scratch=[pltpu.VMEM((seq_len, HEAD_DIM), BF16)] * 2,
+            smem=2,
+            flops=10 * seen * 2 * group_width * tokens,
+        )
+        query_parts.append((query_mine, query_other))
+        far = swap(part_low, "seq", 2)
+        (grad,) = call(add_parts, [((seen, 2 * HEAD_DIM), BF16)], (part, far))
+        grads.append(grad)
+        grad_other = swap(grad, "seq", 4)
+        weight_own, *weight_send = call(
+            weight,
+            [((2 * part_rows, 2 * HEAD_DIM), F32 if flip == 0 else BF16) for flip in range(planes)],
+            (hidden_core, hidden_pair, grad, grad_other),
+            scratch=[pltpu.VMEM((4 * tokens, 2 * HEAD_DIM), BF16)] * 2,
+            flops=2 * pair_rows * 8 * tokens * 2 * HEAD_DIM,
+        )
+        weight_parts.append((weight_own, [swap(weight_send[flip - 1], "dp", flip) for flip in range(1, planes)]))
+
+    def pack(grad0, grad1, other0, other1, send, kept):
+        _, spot, _ = place()
+        for head, (grad, other) in enumerate(((grad0, other0), (grad1, other1))):
+            padded = jnp.concatenate([grad[...], jnp.zeros((seq_len - seen, 2 * HEAD_DIM), BF16)], axis=0)
+            for ref, wanted in ((kept, spot), (send, jnp.bitwise_xor(spot, 1))):
+                chosen = jnp.zeros((tokens, 2 * HEAD_DIM), BF16)
+                for block in range(4):
+                    chosen = jnp.where(wanted == block, padded[block * tokens : (block + 1) * tokens], chosen)
+                ref[:, head * 2 * HEAD_DIM : (head + 1) * 2 * HEAD_DIM] = chosen
+            send[:, 2 * kv_width + head * group_width : 2 * kv_width + (head + 1) * group_width] = other[...]
+
+    send, kept = call(
+        pack,
+        [((tokens, 2 * kv_width + width), BF16), ((tokens, 2 * kv_width), BF16)],
+        (*grads, query_parts[0][1], query_parts[1][1]),
+    )
+    got = swap(send, "seq", 1)
+
+    def unpack(kept_ref, got_ref, mine0, mine1, query_out, key_out, value_out):
+        core, _, _ = place()
+        for head, mine in enumerate((mine0, mine1)):
+            query_out[:, lanes(core * width + head * group_width, group_width)] = mine[...]
+            first = 2 * kv_width + head * group_width
+            query_out[:, lanes((1 - core) * width + head * group_width, group_width)] = got_ref[:, first : first + group_width]
+            for ref, side in ((kept_ref, core), (got_ref, 1 - core)):
+                spot = lanes(side * kv_width + head * HEAD_DIM, HEAD_DIM)
+                first = head * 2 * HEAD_DIM
+                key_out[:, spot] = ref[:, first : first + HEAD_DIM]
+                value_out[:, spot] = ref[:, first + HEAD_DIM : first + 2 * HEAD_DIM]
+
+    query_grad, key_grad, value_grad = call(
+        unpack,
+        [((tokens, 2 * width), BF16), ((tokens, 2 * kv_width), BF16), ((tokens, 2 * kv_width), BF16)],
+        (kept, got, query_parts[0][0], query_parts[1][0]),
+    )
+
+    def add_planes(own, *refs):
+        *got_refs, kept_ref, send_ref = refs
+        core, _, _ = place()
+        for ref, owner in ((kept_ref, core), (send_ref, 1 - core)):
+            rows = pl.ds(pl.multiple_of(owner * part_rows, part_rows), part_rows)
+            total = own[rows, :]
+            for got_ref in got_refs:
+                total += got_ref[rows, :].astype(F32)
+            ref[...] = total
+
+    pieces = []
+    for weight_own, weight_got in weight_parts:
+        kept_weight, send_weight = call(
+            add_planes, [((part_rows, 2 * HEAD_DIM), F32)] * 2, (weight_own, *weight_got)
+        )
+        pieces += [kept_weight, swap(send_weight, "seq", 1)]
+
+    def join(kept0, got0, kept1, got1, out):
+        core, _, _ = place()
+        for head, (kept_ref, got_ref) in enumerate(((kept0, got0), (kept1, got1))):
+            for ref, side in ((kept_ref, core), (got_ref, 1 - core)):
+                spot = side * kv_width + head * HEAD_DIM
+                out[:, lanes(spot, HEAD_DIM)] = ref[:, :HEAD_DIM]
+                out[:, lanes(2 * kv_width + spot, HEAD_DIM)] = ref[:, HEAD_DIM:]
+
+    (weight_grad,) = call(join, [((part_rows, 4 * kv_width), F32)], pieces)
+    return query_grad[None], key_grad[None], value_grad[None], weight_grad
+
+
 def solution(mesh):
     in_specs = (
         P("dp", "seq", None),
@@ -170,4 +429,5 @@
         P("dp", "seq", None),
         P(("seq", "dp"), None),
     )
-    return jax.shard_map(local, mesh=mesh, in_specs=in_specs, out_specs=out_specs, check_vma=False)
+    body = local_pairs if mesh.shape["seq"] == 2 * KV_HEADS else local
+    return jax.shard_map(body, mesh=mesh, in_specs=in_specs, out_specs=out_specs, check_vma=False)

time: 519 us -> 74 us (0.14)
  waiting for transfers between devices: 394 us -> 36.5 us
  matrix products: 40.5 us -> 0 us
  local copies, waits for them, and re-layouts: 27.1 us -> 3.05 us
  between operations: 14.2 us -> 0.79 us
  blocking collectives: 13.2 us -> 0 us
  Pallas kernels: 0 us -> 9.46 us
    reduce_scatter x1 -> x0, waiting for transfers between devices: 346 us -> none  [local(): lax.psum_scatter(jnp.einsum('tr,tc->rc', hidden_rows, joined, preferred_e...]
    all_to_all x6 -> x0, waiting for transfers between devices: 47.8 us -> none  [the longest x1 9.54 us: local(): lax.all_to_all(key_acc.reshape(seq_count, tokens_dev, 1, width_dev).astyp...]
    ppermute x0 -> x20, waiting for transfers between devices: none -> 36.5 us  [swap(): return lax.ppermute(array, axis, [(i, i ^ bit) for i in range(size)])]
    dot_general x9 -> x0, matrix products: 33.4 us -> none  [the longest x2 8.25 us: one_block(): jnp.einsum('hqk,qhd->khd', dscore, query_block, preferred_element_type=jn...]
    ppermute x0 -> x20, starting transfers between devices: none -> 23.5 us  [swap(): return lax.ppermute(array, axis, [(i, i ^ bit) for i in range(size)])]
    all_to_all x6 -> x0, starting transfers between devices: 22.6 us -> none  [the longest x1 5.17 us: local(): lax.all_to_all(value_units, 'seq', split_axis=1, concat_axis=0, tiled=True)]
    all_to_all x1 -> x0, blocking collectives: 13.2 us -> none  [local(): lax.all_to_all(query_acc.reshape(seq_count, class_tokens, 1, width_dev),...]
    pallas_call x0 -> x14, Pallas kernels: none -> 9.46 us  [call(): pl.pallas_call(body, out_shape=shapes, in_specs=specs, out_specs=[pl.Bloc...]
  transfers between devices with their start and end apart: 7 -> 20, of which waited for: 7 -> 10; matrix products, arithmetic and copies ran while one was open for 3% -> 0% of each run, Pallas kernels for 0% -> 12%
where the time goes in v1:
time: 74 us; the launch traced here: 73.3 us
  waiting for transfers between devices  36.5 us (49%)
  starting transfers between devices  23.5 us (32%)
  Pallas kernels  9.46 us (13%)
  local copies, waits for them, and re-layouts  3.05 us (4%)
  between operations  0.79 us (1%)
    ppermute x20, waiting for transfers between devices, swap(): return lax.ppermute(array, axis, [(i, i ^ bit) for i in range(size)])  36.5 us
    ppermute x20, starting transfers between devices, swap(): return lax.ppermute(array, axis, [(i, i ^ bit) for i in range(size)])  23.5 us
    pallas_call x14, Pallas kernels, call(): pl.pallas_call(body, out_shape=shapes, in_specs=specs, out_specs=[pl.Bloc...  9.46 us
    unnamed x14, local copies, waits for them, and re-layouts  3.05 us
  transfers between devices with their start and end apart: 20, of which 10 were waited for; matrix products, arithmetic and copies ran while one was open for 0% of the time, Pallas kernels for 12%

profile of v1, /device:TPU:0, one launch (start us, length us, event | category | flops | bytes accessed | tf_op | source)
XLA Modules:
  0.0 73.3 jit_solution(5555602777294914574)
XLA Ops:
  0.6 1.2 %copy-done = bf16[1,128,4096]{2,1,0:T(8,128)(2,1)S(1)} copy-done((bf16[1,128,4096]{2,1,0:T(8,128)(2,1)S(1)}, bf16[1,128,4096]{2,1,0:T(8,128)(2,1)}, u32[]{:S(2)}) %copy-start) | copy-done | bytes 1048600
  1.9 3.0 %collective-permute-start.6 = (bf16[128,1024]{1,0:T(8,128)(2,1)S(1)}, bf16[128,1024]{1,0:T(8,128)(2,1)S(1)}, u32[]{:S(2)}, u32[]{:S(2)}) collective-permute-start(bf16[128,1024]{1,0:T(8,128)(2,1)S(1)} %get-tuple-element.53), channel_id=1, source_target_pairs={{0,8},{4,12},{8,0},{12,4},{16,24},{20,28},{24,16},{28,20},{1,9},{5... | collective-permute-start | bytes 786440 | tf_op jit(solution)/shard_map/ppermute | solution.py:162
  4.9 1.5 %collective-permute-start.7 = (bf16[128,1024]{1,0:T(8,128)(2,1)S(1)}, bf16[128,1024]{1,0:T(8,128)(2,1)S(1)}, u32[]{:S(2)}, u32[]{:S(2)}) collective-permute-start(bf16[128,1024]{1,0:T(8,128)(2,1)S(1)} %get-tuple-element.54), channel_id=1, source_target_pairs={{0,16},{4,20},{8,24},{12,28},{16,0},{20,4},{24,8},{28,12},{1,17},{... | collective-permute-start | bytes 786440 | tf_op jit(solution)/shard_map/ppermute | solution.py:162
  6.5 0.9 %copy-done.3 = bf16[1,128,512]{2,1,0:T(8,128)(2,1)S(1)} copy-done((bf16[1,128,512]{2,1,0:T(8,128)(2,1)S(1)}, bf16[1,128,512]{2,1,0:T(8,128)(2,1)}, u32[]{:S(2)}) %copy-start.3) | copy-done | bytes 131096
  7.4 0.9 %copy-done.4 = bf16[1,128,512]{2,1,0:T(8,128)(2,1)S(1)} copy-done((bf16[1,128,512]{2,1,0:T(8,128)(2,1)S(1)}, bf16[1,128,512]{2,1,0:T(8,128)(2,1)}, u32[]{:S(2)}) %copy-start.4) | copy-done | bytes 131096
  8.4 3.6 %collective-permute-done.6.far = bf16[128,1024]{1,0:T(8,128)(2,1)S(1)} collective-permute-done((bf16[128,1024]{1,0:T(8,128)(2,1)S(1)}, bf16[128,1024]{1,0:T(8,128)(2,1)S(1)}, u32[]{:S(2)}, u32[]{:S(2)}) %collective-permute-start.6) | collective-permute-done | bytes 262176 | tf_op jit(solution)/shard_map/ppermute | solution.py:162
  12.1 6.2 %collective-permute-done.7.other = bf16[128,1024]{1,0:T(8,128)(2,1)S(1)} collective-permute-done((bf16[128,1024]{1,0:T(8,128)(2,1)S(1)}, bf16[128,1024]{1,0:T(8,128)(2,1)S(1)}, u32[]{:S(2)}, u32[]{:S(2)}) %collective-permute-start.7) | collective-permute-done | bytes 262176 | tf_op jit(solution)/shard_map/ppermute | solution.py:162
  18.8 1.3 %collective-permute-start.1 = (bf16[128,512]{1,0:T(8,128)(2,1)S(1)}, bf16[128,512]{1,0:T(8,128)(2,1)S(1)}, u32[]{:S(2)}, u32[]{:S(2)}) collective-permute-start(bf16[128,512]{1,0:T(8,128)(2,1)S(1)} %get-tuple-element.36.kv0), channel_id=1, source_target_pairs={{0,8},{4,12},{8,0},{12,4},{16,24},{20,28},{24,16},{28,20},{1,9},{5... | collective-permute-start | bytes 393224 | tf_op jit(solution)/shard_map/ppermute | solution.py:162
  20.1 0.5 collective-permute-start.2
  20.6 4.5 %collective-permute-done.1.kv2 = bf16[128,512]{1,0:T(8,128)(2,1)S(1)} collective-permute-done((bf16[128,512]{1,0:T(8,128)(2,1)S(1)}, bf16[128,512]{1,0:T(8,128)(2,1)S(1)}, u32[]{:S(2)}, u32[]{:S(2)}) %collective-permute-start.1) | collective-permute-done | bytes 131104 | tf_op jit(solution)/shard_map/ppermute | solution.py:162
  25.1 1.9 %collective-permute-done.2.kv3 = bf16[128,512]{1,0:T(8,128)(2,1)S(1)} collective-permute-done((bf16[128,512]{1,0:T(8,128)(2,1)S(1)}, bf16[128,512]{1,0:T(8,128)(2,1)S(1)}, u32[]{:S(2)}, u32[]{:S(2)}) %collective-permute-start.2) | collective-permute-done | bytes 131104 | tf_op jit(solution)/shard_map/ppermute | solution.py:162
  27.0 2.7 %shard_map.103 = (f32[448,256]{1,0:T(8,128)S(1)}, bf16[448,256]{1,0:T(8,128)(2,1)S(1)}, bf16[128,512]{1,0:T(8,128)(2,1)S(1)}, bf16[128,512]{1,0:T(8,128)(2,1)S(1)}) custom-call(bf16[128,2048]{1,0:T(8,128)(2,1)S(1)} %bitcast.10, bf16[128,2048]{1,0:T(8,128)(2,1)S(1)} %bitcast.13, bf16[128,512]{1,0:T(8,128)(2,1)S(1)} %get-tuple-element.36.kv0, ...), custom_call_target="tpu_custom_call" | custom-call | flops 587202560 | bytes 3047440 | tf_op jit(solution)/shard_map/pallas_call | solution.py:178
  29.7 1.3 %collective-permute-start.3 = (bf16[448,256]{1,0:T(8,128)(2,1)S(1)}, bf16[448,256]{1,0:T(8,128)(2,1)S(1)}, u32[]{:S(2)}, u32[]{:S(2)}) collective-permute-start(bf16[448,256]{1,0:T(8,128)(2,1)S(1)} %get-tuple-element.40), channel_id=1, source_target_pairs={{0,8},{4,12},{8,0},{12,4},{16,24},{20,28},{24,16},{28,20},{1,9},{5... | collective-permute-start | bytes 688136 | tf_op jit(solution)/shard_map/ppermute | solution.py:162
  31.0 2.7 %shard_map.105 = (f32[448,256]{1,0:T(8,128)S(1)}, bf16[448,256]{1,0:T(8,128)(2,1)S(1)}, bf16[128,512]{1,0:T(8,128)(2,1)S(1)}, bf16[128,512]{1,0:T(8,128)(2,1)S(1)}) custom-call(bf16[128,2048]{1,0:T(8,128)(2,1)S(1)} %bitcast.11, bf16[128,2048]{1,0:T(8,128)(2,1)S(1)} %bitcast.14, bf16[128,512]{1,0:T(8,128)(2,1)S(1)} %get-tuple-element.36.kv0, ...), custom_call_target="tpu_custom_call" | custom-call | flops 587202560 | bytes 3047440 | tf_op jit(solution)/shard_map/pallas_call | solution.py:178
  33.8 0.9 %collective-permute-start.4 = (bf16[448,256]{1,0:T(8,128)(2,1)S(1)}, bf16[448,256]{1,0:T(8,128)(2,1)S(1)}, u32[]{:S(2)}, u32[]{:S(2)}) collective-permute-start(bf16[448,256]{1,0:T(8,128)(2,1)S(1)} %get-tuple-element.42), channel_id=1, source_target_pairs={{0,8},{4,12},{8,0},{12,4},{16,24},{20,28},{24,16},{28,20},{1,9},{5... | collective-permute-start | bytes 688136 | tf_op jit(solution)/shard_map/ppermute | solution.py:162
  34.6 3.6 %collective-permute-done.3.far = bf16[448,256]{1,0:T(8,128)(2,1)S(1)} collective-permute-done((bf16[448,256]{1,0:T(8,128)(2,1)S(1)}, bf16[448,256]{1,0:T(8,128)(2,1)S(1)}, u32[]{:S(2)}, u32[]{:S(2)}) %collective-permute-start.3) | collective-permute-done | bytes 229408 | tf_op jit(solution)/shard_map/ppermute | solution.py:162
  38.3 1.6 %collective-permute-start.10 = (bf16[448,256]{1,0:T(8,128)(2,1)S(1)}, bf16[448,256]{1,0:T(8,128)(2,1)S(1)}, u32[]{:S(2)}, u32[]{:S(2)}) collective-permute-start(bf16[448,256]{1,0:T(8,128)(2,1)S(1)} %shard_map.104.grad0.own), channel_id=1, source_target_pairs={{0,16},{4,20},{8,24},{12,28},{16,0},{20,4},{24,8},{28,12},{1,17},{... | collective-permute-start | bytes 688136 | tf_op jit(solution)/shard_map/ppermute | solution.py:162
  39.9 2.7 %collective-permute-done.4.far = bf16[448,256]{1,0:T(8,128)(2,1)S(1)} collective-permute-done((bf16[448,256]{1,0:T(8,128)(2,1)S(1)}, bf16[448,256]{1,0:T(8,128)(2,1)S(1)}, u32[]{:S(2)}, u32[]{:S(2)}) %collective-permute-start.4) | collective-permute-done | bytes 229408 | tf_op jit(solution)/shard_map/ppermute | solution.py:162
  42.6 1.6 %collective-permute-start.15 = (bf16[448,256]{1,0:T(8,128)(2,1)S(1)}, bf16[448,256]{1,0:T(8,128)(2,1)S(1)}, u32[]{:S(2)}, u32[]{:S(2)}) collective-permute-start(bf16[448,256]{1,0:T(8,128)(2,1)S(1)} %shard_map.106.grad1.own), channel_id=1, source_target_pairs={{0,16},{4,20},{8,24},{12,28},{16,0},{20,4},{24,8},{28,12},{1,17},{... | collective-permute-start | bytes 688136 | tf_op jit(solution)/shard_map/ppermute | solution.py:162
  44.2 0.5 collective-permute-done.10.other
  44.7 0.7 shard_map.111
  45.4 1.6 %collective-permute-start.11 = (bf16[256,256]{1,0:T(8,128)(2,1)S(1)}, bf16[256,256]{1,0:T(8,128)(2,1)S(1)}, u32[]{:S(2)}, u32[]{:S(2)}) collective-permute-start(bf16[256,256]{1,0:T(8,128)(2,1)S(1)} %get-tuple-element.57), channel_id=1, source_target_pairs={{0,1},{1,0},{2,3},{3,2},{4,5},{5,4},{6,7},{7,6},{8,9},{9,8},{10,11... | collective-permute-start | bytes 393224 | tf_op jit(solution)/shard_map/ppermute | solution.py:162
  47.1 2.6 %collective-permute-start.12 = (bf16[256,256]{1,0:T(8,128)(2,1)S(1)}, bf16[256,256]{1,0:T(8,128)(2,1)S(1)}, u32[]{:S(2)}, u32[]{:S(2)}) collective-permute-start(bf16[256,256]{1,0:T(8,128)(2,1)S(1)} %get-tuple-element.58), channel_id=1, source_target_pairs={{0,2},{1,3},{2,0},{3,1},{4,6},{5,7},{6,4},{7,5},{8,10},{9,11},{10,... | collective-permute-start | bytes 393224 | tf_op jit(solution)/shard_map/ppermute | solution.py:162
  49.9 0.7 shard_map.113
  50.6 1.4 %collective-permute-start.16 = (bf16[256,256]{1,0:T(8,128)(2,1)S(1)}, bf16[256,256]{1,0:T(8,128)(2,1)S(1)}, u32[]{:S(2)}, u32[]{:S(2)}) collective-permute-start(bf16[256,256]{1,0:T(8,128)(2,1)S(1)} %get-tuple-element.63), channel_id=1, source_target_pairs={{0,1},{1,0},{2,3},{3,2},{4,5},{5,4},{6,7},{7,6},{8,9},{9,8},{10,11... | collective-permute-start | bytes 393224 | tf_op jit(solution)/shard_map/ppermute | solution.py:162
  52.0 2.8 %collective-permute-start.17 = (bf16[256,256]{1,0:T(8,128)(2,1)S(1)}, bf16[256,256]{1,0:T(8,128)(2,1)S(1)}, u32[]{:S(2)}, u32[]{:S(2)}) collective-permute-start(bf16[256,256]{1,0:T(8,128)(2,1)S(1)} %get-tuple-element.64), channel_id=1, source_target_pairs={{0,2},{1,3},{2,0},{3,1},{4,6},{5,7},{6,4},{7,5},{8,10},{9,11},{10,... | collective-permute-start | bytes 393224 | tf_op jit(solution)/shard_map/ppermute | solution.py:162
  54.9 4.8 %collective-permute-done.12.refs_1_ = bf16[256,256]{1,0:T(8,128)(2,1)S(1)} collective-permute-done((bf16[256,256]{1,0:T(8,128)(2,1)S(1)}, bf16[256,256]{1,0:T(8,128)(2,1)S(1)}, u32[]{:S(2)}, u32[]{:S(2)}) %collective-permute-start.12) | collective-permute-done | bytes 131104 | tf_op jit(solution)/shard_map/ppermute | solution.py:162
  59.7 2.8 %collective-permute-start.18 = (bf16[256,256]{1,0:T(8,128)(2,1)S(1)}, bf16[256,256]{1,0:T(8,128)(2,1)S(1)}, u32[]{:S(2)}, u32[]{:S(2)}) collective-permute-start(bf16[256,256]{1,0:T(8,128)(2,1)S(1)} %get-tuple-element.65), channel_id=1, source_target_pairs={{0,3},{1,2},{2,1},{3,0},{4,7},{5,6},{6,5},{7,4},{8,11},{9,10},{10,... | collective-permute-start | bytes 393224 | tf_op jit(solution)/shard_map/ppermute | solution.py:162
  62.6 8.3 %collective-permute-done.17.refs_1_ = bf16[256,256]{1,0:T(8,128)(2,1)S(1)} collective-permute-done((bf16[256,256]{1,0:T(8,128)(2,1)S(1)}, bf16[256,256]{1,0:T(8,128)(2,1)S(1)}, u32[]{:S(2)}, u32[]{:S(2)}) %collective-permute-start.17) | collective-permute-done | bytes 131104 | tf_op jit(solution)/shard_map/ppermute | solution.py:162
  71.1 1.0 %shard_map.108 = (bf16[128,2048]{1,0:T(8,128)(2,1)}, bf16[128,512]{1,0:T(8,128)(2,1)}, bf16[128,512]{1,0:T(8,128)(2,1)}) custom-call(bf16[128,512]{1,0:T(8,128)(2,1)S(1)} %get-tuple-element.45.kept_ref, bf16[128,1536]{1,0:T(8,128)(2,1)S(1)} %collective-permute-done.5.got_ref, bf16[128,512]{1,0:T(8,128)(2,1)S(1)} %get-tuple-element.47.mine0, ...), custom_call_target="tpu_custom_call" | custom-call | bytes 1572864 | tf_op jit(solution)/shard_map/pallas_call | solution.py:178
  72.0 0.4 collective-permute-done.19.got1
  72.4 0.9 %shard_map.115 = f32[128,1024]{1,0:T(8,128)} custom-call(f32[128,256]{1,0:T(8,128)S(1)} %get-tuple-element.60.kept0, f32[128,256]{1,0:T(8,128)S(1)} %collective-permute-done.14.got0, f32[128,256]{1,0:T(8,128)S(1)} %get-tuple-element.66.kept1, f32[128,256]{1,0:T(8,128)S(1)} %collective-permute-done.19.got1), custom_call_target="tpu_custom_call" | custom-call | bytes 1048576 | tf_op jit(solution)/shard_map/pallas_call | solution.py:178
  (36 shorter events, 1.3 us)
Async XLA Ops:
  0.6 1.2 %copy-start = (bf16[1,128,4096]{2,1,0:T(8,128)(2,1)S(1)}, bf16[1,128,4096]{2,1,0:T(8,128)(2,1)}, u32[]{:S(2)}) copy-start(bf16[1,128,4096]{2,1,0:T(8,128)(2,1)} %param.11) | copy-start | bytes 3145732
  1.9 4.6 %copy-start.1 = (bf16[1,128,2048]{2,1,0:T(8,128)(2,1)S(1)}, bf16[1,128,2048]{2,1,0:T(8,128)(2,1)}, u32[]{:S(2)}) copy-start(bf16[1,128,2048]{2,1,0:T(8,128)(2,1)} %param.7) | copy-start | bytes 1572868
  1.9 4.6 %copy-start.2 = (bf16[1,128,2048]{2,1,0:T(8,128)(2,1)S(1)}, bf16[1,128,2048]{2,1,0:T(8,128)(2,1)}, u32[]{:S(2)}) copy-start(bf16[1,128,2048]{2,1,0:T(8,128)(2,1)} %param.10) | copy-start | bytes 1572868
  1.9 10.1 %collective-permute-start.6 = (bf16[128,1024]{1,0:T(8,128)(2,1)S(1)}, bf16[128,1024]{1,0:T(8,128)(2,1)S(1)}, u32[]{:S(2)}, u32[]{:S(2)}) collective-permute-start(bf16[128,1024]{1,0:T(8,128)(2,1)S(1)} %get-tuple-element.53), channel_id=1, source_target_pairs={{0,8},{4,12},{8,0},{12,4},{16,24},{20,28},{24,16},{28,20},{1,9},{5... | collective-permute-start | bytes 786440 | tf_op jit(solution)/shard_map/ppermute | solution.py:162
  4.9 13.4 %collective-permute-start.7 = (bf16[128,1024]{1,0:T(8,128)(2,1)S(1)}, bf16[128,1024]{1,0:T(8,128)(2,1)S(1)}, u32[]{:S(2)}, u32[]{:S(2)}) collective-permute-start(bf16[128,1024]{1,0:T(8,128)(2,1)S(1)} %get-tuple-element.54), channel_id=1, source_target_pairs={{0,16},{4,20},{8,24},{12,28},{16,0},{20,4},{24,8},{28,12},{1,17},{... | collective-permute-start | bytes 786440 | tf_op jit(solution)/shard_map/ppermute | solution.py:162
  6.5 11.9 %collective-permute-start.8 = (bf16[128,1024]{1,0:T(8,128)(2,1)S(1)}, bf16[128,1024]{1,0:T(8,128)(2,1)S(1)}, u32[]{:S(2)}, u32[]{:S(2)}) collective-permute-start(bf16[128,1024]{1,0:T(8,128)(2,1)S(1)} %get-tuple-element.55), channel_id=1, source_target_pairs={{0,24},{4,28},{8,16},{12,20},{16,8},{20,12},{24,0},{28,4},{1,25},{... | collective-permute-start | bytes 786440 | tf_op jit(solution)/shard_map/ppermute | solution.py:162
  6.5 0.9 %copy-start.3 = (bf16[1,128,512]{2,1,0:T(8,128)(2,1)S(1)}, bf16[1,128,512]{2,1,0:T(8,128)(2,1)}, u32[]{:S(2)}) copy-start(bf16[1,128,512]{2,1,0:T(8,128)(2,1)} %param.8) | copy-start | bytes 393220
  7.4 0.9 %copy-start.4 = (bf16[1,128,512]{2,1,0:T(8,128)(2,1)S(1)}, bf16[1,128,512]{2,1,0:T(8,128)(2,1)}, u32[]{:S(2)}) copy-start(bf16[1,128,512]{2,1,0:T(8,128)(2,1)} %param.9) | copy-start | bytes 393220
  8.4 18.6 %collective-permute-start = (bf16[128,2560]{1,0:T(8,128)(2,1)S(1)}, bf16[128,2560]{1,0:T(8,128)(2,1)S(1)}, u32[]{:S(2)}, u32[]{:S(2)}) collective-permute-start(bf16[128,2560]{1,0:T(8,128)(2,1)S(1)} %get-tuple-element.37), channel_id=1, source_target_pairs={{0,4},{4,0},{8,12},{12,8},{16,20},{20,16},{24,28},{28,24},{1,5},{5... | collective-permute-start | bytes 1966088 | tf_op jit(solution)/shard_map/ppermute | solution.py:162
  18.7 26.1 %collective-permute-start.9 = (bf16[1024,512]{1,0:T(8,128)(2,1)S(1)}, bf16[1024,512]{1,0:T(8,128)(2,1)S(1)}, u32[]{:S(2)}, u32[]{:S(2)}) collective-permute-start(bf16[1024,512]{1,0:T(8,128)(2,1)S(1)} %shard_map.110.core_ref), channel_id=1, source_target_pairs={{0,4},{4,0},{8,12},{12,8},{16,20},{20,16},{24,28},{28,24},{1,5},{5... | collective-permute-start | bytes 3145736 | tf_op jit(solution)/shard_map/ppermute | solution.py:162
  18.7 8.3 %copy-start.5 = (s32[2]{0:T(128)S(1)}, s32[2]{0:T(128)}, u32[]{:S(2)}) copy-start(s32[2]{0:T(128)} %start_ref.3) | copy-start | bytes 28
  18.7 8.2 %copy-start.6 = (s32[2]{0:T(128)S(1)}, s32[2]{0:T(128)}, u32[]{:S(2)}) copy-start(s32[2]{0:T(128)} %len_ref.3) | copy-start | bytes 28
  18.8 6.4 %collective-permute-start.1 = (bf16[128,512]{1,0:T(8,128)(2,1)S(1)}, bf16[128,512]{1,0:T(8,128)(2,1)S(1)}, u32[]{:S(2)}, u32[]{:S(2)}) collective-permute-start(bf16[128,512]{1,0:T(8,128)(2,1)S(1)} %get-tuple-element.36.kv0), channel_id=1, source_target_pairs={{0,8},{4,12},{8,0},{12,4},{16,24},{20,28},{24,16},{28,20},{1,9},{5... | collective-permute-start | bytes 393224 | tf_op jit(solution)/shard_map/ppermute | solution.py:162
  20.1 6.9 %collective-permute-start.2 = (bf16[128,512]{1,0:T(8,128)(2,1)S(1)}, bf16[128,512]{1,0:T(8,128)(2,1)S(1)}, u32[]{:S(2)}, u32[]{:S(2)}) collective-permute-start(bf16[128,512]{1,0:T(8,128)(2,1)S(1)} %get-tuple-element.38), channel_id=1, source_target_pairs={{0,12},{4,8},{8,4},{12,0},{16,28},{20,24},{24,20},{28,16},{1,13},{... | collective-permute-start | bytes 393224 | tf_op jit(solution)/shard_map/ppermute | solution.py:162
  29.7 8.5 %collective-permute-start.3 = (bf16[448,256]{1,0:T(8,128)(2,1)S(1)}, bf16[448,256]{1,0:T(8,128)(2,1)S(1)}, u32[]{:S(2)}, u32[]{:S(2)}) collective-permute-start(bf16[448,256]{1,0:T(8,128)(2,1)S(1)} %get-tuple-element.40), channel_id=1, source_target_pairs={{0,8},{4,12},{8,0},{12,4},{16,24},{20,28},{24,16},{28,20},{1,9},{5... | collective-permute-start | bytes 688136 | tf_op jit(solution)/shard_map/ppermute | solution.py:162
  33.8 8.8 %collective-permute-start.4 = (bf16[448,256]{1,0:T(8,128)(2,1)S(1)}, bf16[448,256]{1,0:T(8,128)(2,1)S(1)}, u32[]{:S(2)}, u32[]{:S(2)}) collective-permute-start(bf16[448,256]{1,0:T(8,128)(2,1)S(1)} %get-tuple-element.42), channel_id=1, source_target_pairs={{0,8},{4,12},{8,0},{12,4},{16,24},{20,28},{24,16},{28,20},{1,9},{5... | collective-permute-start | bytes 688136 | tf_op jit(solution)/shard_map/ppermute | solution.py:162
  38.3 6.4 %collective-permute-start.10 = (bf16[448,256]{1,0:T(8,128)(2,1)S(1)}, bf16[448,256]{1,0:T(8,128)(2,1)S(1)}, u32[]{:S(2)}, u32[]{:S(2)}) collective-permute-start(bf16[448,256]{1,0:T(8,128)(2,1)S(1)} %shard_map.104.grad0.own), channel_id=1, source_target_pairs={{0,16},{4,20},{8,24},{12,28},{16,0},{20,4},{24,8},{28,12},{1,17},{... | collective-permute-start | bytes 688136 | tf_op jit(solution)/shard_map/ppermute | solution.py:162
  42.6 7.3 %collective-permute-start.15 = (bf16[448,256]{1,0:T(8,128)(2,1)S(1)}, bf16[448,256]{1,0:T(8,128)(2,1)S(1)}, u32[]{:S(2)}, u32[]{:S(2)}) collective-permute-start(bf16[448,256]{1,0:T(8,128)(2,1)S(1)} %shard_map.106.grad1.own), channel_id=1, source_target_pairs={{0,16},{4,20},{8,24},{12,28},{16,0},{20,4},{24,8},{28,12},{1,17},{... | collective-permute-start | bytes 688136 | tf_op jit(solution)/shard_map/ppermute | solution.py:162
  45.4 6.6 %collective-permute-start.11 = (bf16[256,256]{1,0:T(8,128)(2,1)S(1)}, bf16[256,256]{1,0:T(8,128)(2,1)S(1)}, u32[]{:S(2)}, u32[]{:S(2)}) collective-permute-start(bf16[256,256]{1,0:T(8,128)(2,1)S(1)} %get-tuple-element.57), channel_id=1, source_target_pairs={{0,1},{1,0},{2,3},{3,2},{4,5},{5,4},{6,7},{7,6},{8,9},{9,8},{10,11... | collective-permute-start | bytes 393224 | tf_op jit(solution)/shard_map/ppermute | solution.py:162
  47.1 24.0 %collective-permute-start.5 = (bf16[128,1536]{1,0:T(8,128)(2,1)S(1)}, bf16[128,1536]{1,0:T(8,128)(2,1)S(1)}, u32[]{:S(2)}, u32[]{:S(2)}) collective-permute-start(bf16[128,1536]{1,0:T(8,128)(2,1)S(1)} %get-tuple-element.46), channel_id=1, source_target_pairs={{0,4},{4,0},{8,12},{12,8},{16,20},{20,16},{24,28},{28,24},{1,5},{5... | collective-permute-start | bytes 1179656 | tf_op jit(solution)/shard_map/ppermute | solution.py:162
  47.1 12.6 %collective-permute-start.12 = (bf16[256,256]{1,0:T(8,128)(2,1)S(1)}, bf16[256,256]{1,0:T(8,128)(2,1)S(1)}, u32[]{:S(2)}, u32[]{:S(2)}) collective-permute-start(bf16[256,256]{1,0:T(8,128)(2,1)S(1)} %get-tuple-element.58), channel_id=1, source_target_pairs={{0,2},{1,3},{2,0},{3,1},{4,6},{5,7},{6,4},{7,5},{8,10},{9,11},{10,... | collective-permute-start | bytes 393224 | tf_op jit(solution)/shard_map/ppermute | solution.py:162
  49.7 12.8 %collective-permute-start.13 = (bf16[256,256]{1,0:T(8,128)(2,1)S(1)}, bf16[256,256]{1,0:T(8,128)(2,1)S(1)}, u32[]{:S(2)}, u32[]{:S(2)}) collective-permute-start(bf16[256,256]{1,0:T(8,128)(2,1)S(1)} %get-tuple-element.59), channel_id=1, source_target_pairs={{0,3},{1,2},{2,1},{3,0},{4,7},{5,6},{6,5},{7,4},{8,11},{9,10},{10,... | collective-permute-start | bytes 393224 | tf_op jit(solution)/shard_map/ppermute | solution.py:162
  50.6 12.0 %collective-permute-start.16 = (bf16[256,256]{1,0:T(8,128)(2,1)S(1)}, bf16[256,256]{1,0:T(8,128)(2,1)S(1)}, u32[]{:S(2)}, u32[]{:S(2)}) collective-permute-start(bf16[256,256]{1,0:T(8,128)(2,1)S(1)} %get-tuple-element.63), channel_id=1, source_target_pairs={{0,1},{1,0},{2,3},{3,2},{4,5},{5,4},{6,7},{7,6},{8,9},{9,8},{10,11... | collective-permute-start | bytes 393224 | tf_op jit(solution)/shard_map/ppermute | solution.py:162
  52.0 18.9 %collective-permute-start.17 = (bf16[256,256]{1,0:T(8,128)(2,1)S(1)}, bf16[256,256]{1,0:T(8,128)(2,1)S(1)}, u32[]{:S(2)}, u32[]{:S(2)}) collective-permute-start(bf16[256,256]{1,0:T(8,128)(2,1)S(1)} %get-tuple-element.64), channel_id=1, source_target_pairs={{0,2},{1,3},{2,0},{3,1},{4,6},{5,7},{6,4},{7,5},{8,10},{9,11},{10,... | collective-permute-start | bytes 393224 | tf_op jit(solution)/shard_map/ppermute | solution.py:162
  59.7 11.2 %collective-permute-start.18 = (bf16[256,256]{1,0:T(8,128)(2,1)S(1)}, bf16[256,256]{1,0:T(8,128)(2,1)S(1)}, u32[]{:S(2)}, u32[]{:S(2)}) collective-permute-start(bf16[256,256]{1,0:T(8,128)(2,1)S(1)} %get-tuple-element.65), channel_id=1, source_target_pairs={{0,3},{1,2},{2,1},{3,0},{4,7},{5,6},{6,5},{7,4},{8,11},{9,10},{10,... | collective-permute-start | bytes 393224 | tf_op jit(solution)/shard_map/ppermute | solution.py:162
  62.5 9.5 %collective-permute-start.14 = (f32[128,256]{1,0:T(8,128)S(1)}, f32[128,256]{1,0:T(8,128)S(1)}, u32[]{:S(2)}, u32[]{:S(2)}) collective-permute-start(f32[128,256]{1,0:T(8,128)S(1)} %get-tuple-element.61), channel_id=1, source_target_pairs={{0,4},{4,0},{8,12},{12,8},{16,20},{20,16},{24,28},{28,24},{1,5},{5... | collective-permute-start | bytes 393224 | tf_op jit(solution)/shard_map/ppermute | solution.py:162
  71.0 1.4 %collective-permute-start.19 = (f32[128,256]{1,0:T(8,128)S(1)}, f32[128,256]{1,0:T(8,128)S(1)}, u32[]{:S(2)}, u32[]{:S(2)}) collective-permute-start(f32[128,256]{1,0:T(8,128)S(1)} %get-tuple-element.67), channel_id=1, source_target_pairs={{0,4},{4,0},{8,12},{12,8},{16,20},{20,16},{24,28},{28,24},{1,5},{5... | collective-permute-start | bytes 393224 | tf_op jit(solution)/shard_map/ppermute | solution.py:162

commit v2 on v1

--- a/solution.py
+++ b/solution.py
@@ -170,20 +170,45 @@
     return pl.ds(pl.multiple_of(start, 128), width)
 
 
-def call(body, outs, args, scratch=(), smem=0, flops=0, vmem=40):
-    specs = [pl.BlockSpec(memory_space=pltpu.VMEM)] * (len(args) - smem)
-    specs += [pl.BlockSpec(memory_space=pltpu.SMEM)] * smem
+def call(body, outs, args, scratch=(), smem=0, held=0, flops=0, vmem=16, place=pltpu.VMEM):
+    near = len(args) - smem - held
+    specs = [pl.BlockSpec(memory_space=place)] * near
+    specs += [pl.BlockSpec(memory_space=pltpu.SMEM)] * smem + [pl.BlockSpec(memory_space=pl.ANY)] * held
     shapes = [jax.ShapeDtypeStruct(shape, dtype) for shape, dtype in outs]
-    moved = sum(math.prod(s.shape) * s.dtype.itemsize for s in [*shapes, *args])
+    moved = sum(math.prod(s.shape) * s.dtype.itemsize for s in [*shapes, *args[: near + smem]])
+
+    def run(*refs):
+        body(*refs[: near + smem], *refs[near + smem + held :])
+
     return pl.pallas_call(
-        body,
+        run,
         out_shape=shapes,
         in_specs=specs,
         out_specs=[pl.BlockSpec(memory_space=pltpu.VMEM)] * len(shapes),
         scratch_shapes=list(scratch),
         compiler_params=pltpu.CompilerParams(vmem_limit_bytes=vmem * 2**20),
-        cost_estimate=pl.CostEstimate(flops=flops, bytes_accessed=moved, transcendentals=0),
+        cost_estimate=pl.CostEstimate(flops=flops, bytes_accessed=0, transcendentals=0),
     )(*args)
+
+
+def after(array, *awaited):
+    return pl.pallas_call(
+        lambda *refs: None,
+        out_shape=jax.ShapeDtypeStruct(array.shape, array.dtype),
+        in_specs=[pl.BlockSpec(memory_space=pl.ANY)] * (1 + len(awaited)),
+        out_specs=pl.BlockSpec(memory_space=pl.ANY),
+        input_output_aliases={0: 0},
+        compiler_params=pltpu.CompilerParams(vmem_limit_bytes=2**20),
+        cost_estimate=pl.CostEstimate(flops=0, bytes_accessed=0, transcendentals=0),
+    )(array, *awaited)
+
+
+def copy_all(sems, pairs):
+    copies = [pltpu.make_async_copy(source, target, sems.at[n]) for n, (source, target) in enumerate(pairs)]
+    for copy in copies:
+        copy.start()
+    for copy in copies:
+        copy.wait()
 
 
 BF16, F32 = jnp.bfloat16, jnp.float32
@@ -209,48 +234,64 @@
         me = lax.axis_index("seq")
         return me % 2, me % 4, me // 4
 
-    def split_heads(query_ref, grad_ref, key_ref, value_ref, kv_mine, kv_other, send):
+    def split_pairs(key_ref, value_ref, kv_mine, kv_other, sems):
         core, _, _ = place()
-        for half, kv_out in ((core, kv_mine), (1 - core, kv_other)):
-            kv_out[:, :kv_width] = key_ref[:, lanes(half * kv_width, kv_width)]
-            kv_out[:, kv_width:] = value_ref[:, lanes(half * kv_width, kv_width)]
-        send[:, :width] = query_ref[:, lanes((1 - core) * width, width)]
-        send[:, width : 2 * width] = grad_ref[:, lanes((1 - core) * width, width)]
-        send[:, 2 * width :] = kv_other[...]
-
-    kv_mine, kv_other, core_send = call(
-        split_heads,
-        [((tokens, 2 * kv_width), BF16), ((tokens, 2 * kv_width), BF16), ((tokens, 2 * width + 2 * kv_width), BF16)],
-        (query, out_grad, keys, values),
+        copy_all(
+            sems,
+            [
+                (ref.at[:, lanes(half * kv_width, kv_width)], out.at[:, pl.ds(part * kv_width, kv_width)])
+                for half, out in ((core, kv_mine), (1 - core, kv_other))
+                for part, ref in enumerate((key_ref, value_ref))
+            ],
+        )
+
+    kv_mine, kv_other = call(
+        split_pairs,
+        [((tokens, 2 * kv_width), BF16)] * 2,
+        (keys, values),
+        scratch=[pltpu.SemaphoreType.DMA((4,))],
+        place=pl.ANY,
+        vmem=60,
     )
     kv_far = swap(kv_mine, "seq", 2)
     kv_cross = swap(kv_other, "seq", 3)
-    core_got = swap(core_send, "seq", 1)
+
+    kv_pair = swap(kv_other, "seq", 1)
+    query_pair = swap(query, "seq", 1)
+    grad_pair = swap(out_grad, "seq", 1)
 
     def split_hidden(hidden_ref, *outs):
+        *outs, sems = outs
         pair = lax.axis_index("seq") // 2
-        for flip in range(4):
-            target = jnp.bitwise_xor(pair, flip)
-            outs[flip][...] = hidden_ref[:, lanes(target * pair_rows, pair_rows)]
-
-    hidden_mine, *hidden_send = call(split_hidden, [((tokens, pair_rows), BF16)] * 4, (hidden,))
-    hidden_got = [swap(hidden_send[flip - 1], "seq", 2 * flip) for flip in (1, 2, 3)]
-
-    def turn_hidden(mine, far, other, other_far, out):
-        half = place()[1] // 2
-        for block, (ref, spot) in enumerate(((mine, half), (far, 1 - half), (other, half), (other_far, 1 - half))):
-            out[:, lanes((block // 2) * 2 * tokens + spot * tokens, tokens)] = ref[...].T
-
-    (hidden_core,) = call(turn_hidden, [((pair_rows, 4 * tokens), BF16)], (hidden_mine, *hidden_got))
-    hidden_pair = swap(hidden_core, "seq", 1)
-
-    def attention(head, query_ref, grad_ref, kv0, got, kv2, kv3, start_ref, len_ref, part, part_low, mine, other, key_all, value_all):
+        copy_all(
+            sems,
+            [
+                (hidden_ref.at[:, lanes(jnp.bitwise_xor(pair, flip) * pair_rows, pair_rows)], out)
+                for flip, out in enumerate(outs)
+            ],
+        )
+
+    hidden_send = call(
+        split_hidden,
+        [((tokens, pair_rows), BF16)] * 4,
+        (hidden, kv_mine),
+        scratch=[pltpu.SemaphoreType.DMA((4,))],
+        held=1,
+        place=pl.ANY,
+    )
+    hidden_core = {
+        0: hidden_send[0],
+        1: swap(after(hidden_send[1], query_pair), "seq", 2),
+        2: swap(after(hidden_send[2], query_pair), "seq", 4),
+        3: swap(after(hidden_send[3], query_pair), "seq", 6),
+    }
+
+    def attention(head, query_ref, grad_ref, query_far, grad_far, kv0, kv1, kv2, kv3, start_ref, len_ref, part, part_low, mine, other, key_all, value_all):
         core, spot, seq_idx = place()
-        base = 2 * width
-        for flip, ref, offset in ((0, kv0, 0), (1, got, base), (2, kv2, 0), (3, kv3, 0)):
+        for flip, ref in enumerate((kv0, kv1, kv2, kv3)):
             rows = pl.ds(pl.multiple_of(jnp.bitwise_xor(spot, flip) * tokens, tokens), tokens)
-            key_all[rows, :] = ref[:, offset + head * HEAD_DIM : offset + (head + 1) * HEAD_DIM]
-            first = offset + kv_width + head * HEAD_DIM
+            key_all[rows, :] = ref[:, head * HEAD_DIM : (head + 1) * HEAD_DIM]
+            first = kv_width + head * HEAD_DIM
             value_all[rows, :] = ref[:, first : first + HEAD_DIM]
         key = key_all[:seen, :]
         value = value_all[:seen, :]
@@ -260,16 +301,10 @@
         row = lax.broadcasted_iota(jnp.int32, (1, columns), 1) % tokens
         key_pos = lax.broadcasted_iota(jnp.int32, (seen, columns), 0)
         for side, out in enumerate((mine, other)):
-            if side == 0:
-                blocks = [
-                    [ref[:, lanes(core * width + head * group_width + r * HEAD_DIM, HEAD_DIM)] for r in range(repeat_by)]
-                    for ref in (query_ref, grad_ref)
-                ]
-            else:
-                blocks = [
-                    [got[:, first + r * HEAD_DIM : first + (r + 1) * HEAD_DIM] for r in range(repeat_by)]
-                    for first in (head * group_width, width + head * group_width)
-                ]
+            blocks = [
+                [ref[:, lanes(core * width + head * group_width + r * HEAD_DIM, HEAD_DIM)] for r in range(repeat_by)]
+                for ref in ((query_ref, grad_ref), (query_far, grad_far))[side]
+            ]
             query_rows = jnp.concatenate(blocks[0], axis=0)
             grad_rows = jnp.concatenate(blocks[1], axis=0)
             query_pos = jnp.bitwise_xor(spot, side) * tokens + row
@@ -298,29 +333,37 @@
     def add_parts(part, far, out):
         out[...] = (part[...] + far[...].astype(F32)).astype(BF16)
 
-    def weight(core_ref, pair_ref, own, other, *outs_and_scratch):
-        *outs, rows_core, rows_pair = outs_and_scratch
-        core, _, _ = place()
+    def weight(*refs):
+        *hidden_refs, own, other, kept, send = refs[:-2]
+        rows = refs[-2:]
+        _, spot, _ = place()
         plane = lax.axis_index("dp")
-        for seq, ref in enumerate((own, other)):
-            padded = jnp.concatenate([ref[...], jnp.zeros((seq_len - seen, 2 * HEAD_DIM), BF16)], axis=0)
-            for half in range(2):
-                first = jnp.where(core == 0, 0, 1)
-                low = padded[2 * half * tokens : (2 * half + 1) * tokens]
-                high = padded[(2 * half + 1) * tokens : (2 * half + 2) * tokens]
-                spot = (2 * seq + half) * tokens
-                rows_core[spot : spot + tokens, :] = jnp.where(first == 0, low, high)
-                rows_pair[spot : spot + tokens, :] = jnp.where(first == 0, high, low)
-        for flip, out in enumerate(outs):
+        padded, rows = rows[0], rows[1]
+        padded[seen:, :] = jnp.zeros((seq_len - seen, 2 * HEAD_DIM), BF16)
+        for flip in range(4):
+            if flip % 2 == 0:
+                padded[:seen, :] = (own, other)[flip // 2][...]
+            for core in range(2):
+                source = pl.multiple_of(jnp.bitwise_xor(spot, 2 * (flip % 2) + core) * tokens, tokens)
+                target = (2 * flip + core) * tokens
+                rows[target : target + tokens, :] = padded[pl.ds(source, tokens), :]
+        grads = rows[...]
+        for flip, out, half in ((1, send, 0), (3, send, 1), (0, kept, 0), (2, kept, 1)):
             target = jnp.bitwise_xor(plane, flip)
             for owner in range(2):
-                rows = pl.ds(pl.multiple_of((owner * planes + target) * part_rows, part_rows), part_rows)
-                total = dot(core_ref[rows, :], rows_core[...], ((1,), (0,)))
-                total += dot(pair_ref[rows, :], rows_pair[...], ((1,), (0,)))
-                out[owner * part_rows : (owner + 1) * part_rows, :] = total.astype(out.dtype)
+                spot = lanes((owner * planes + target) * part_rows, part_rows)
+                hidden_part = jnp.concatenate([ref[:, spot] for ref in hidden_refs], axis=0)
+                total = dot(hidden_part, grads, ((0,), (0,)))
+                first = (2 * half + owner) * part_rows
+                out[first : first + part_rows, :] = total.astype(out.dtype)
+
+    def add_near(kept, near, out):
+        out[...] = (kept[2 * part_rows :, :] + near[2 * part_rows :, :].astype(F32)).astype(BF16)
 
     grads, query_parts, weight_parts = [], [], []
+    sums = []
     for head in range(own_heads):
+        awaited = (hidden_core[1], hidden_core[2], query_parts[0][0]) if head else ()
         part, part_low, query_mine, query_other = call(
             functools.partial(attention, head),
             [
@@ -329,24 +372,45 @@
                 ((tokens, group_width), BF16),
                 ((tokens, group_width), BF16),
             ],
-            (query, out_grad, kv_mine, core_got, kv_far, kv_cross, q_start, q_len),
+            (query, out_grad, query_pair, grad_pair, kv_mine, kv_pair, kv_far, kv_cross, q_start, q_len, *awaited),
             scratch=[pltpu.VMEM((seq_len, HEAD_DIM), BF16)] * 2,
             smem=2,
-            flops=10 * seen * 2 * group_width * tokens,
+            held=len(awaited),
+            vmem=32,
+            flops=10 * seen * 2 * group_width * tokens * (0 if head else 20),
         )
         query_parts.append((query_mine, query_other))
-        far = swap(part_low, "seq", 2)
-        (grad,) = call(add_parts, [((seen, 2 * HEAD_DIM), BF16)], (part, far))
-        grads.append(grad)
-        grad_other = swap(grad, "seq", 4)
-        weight_own, *weight_send = call(
+        if head:
+            (grad,) = call(add_parts, [((seen, 2 * HEAD_DIM), BF16)], (*sums[0], query_mine, hidden_core[3]), held=2)
+            sums[0] = (grad, swap(grad, "seq", 4))
+        sums.append((part, swap(part_low, "seq", 2)))
+    hidden_blocks = []
+    for flip in range(4):
+        block = hidden_core[flip]
+        halves = (block[: tokens // 2], block[tokens // 2 :]) if flip == 3 else (block,)
+        hidden_blocks += [block, *[swap(half, "seq", 1) for half in halves]]
+    (grad,) = call(add_parts, [((seen, 2 * HEAD_DIM), BF16)], sums[1])
+    sums[1] = (grad, swap(grad, "seq", 4))
+    for head in range(own_heads):
+        grads.append(sums[head][0])
+        kept, send = call(
             weight,
-            [((2 * part_rows, 2 * HEAD_DIM), F32 if flip == 0 else BF16) for flip in range(planes)],
-            (hidden_core, hidden_pair, grad, grad_other),
-            scratch=[pltpu.VMEM((4 * tokens, 2 * HEAD_DIM), BF16)] * 2,
-            flops=2 * pair_rows * 8 * tokens * 2 * HEAD_DIM,
-        )
-        weight_parts.append((weight_own, [swap(weight_send[flip - 1], "dp", flip) for flip in range(1, planes)]))
+            [((4 * part_rows, 2 * HEAD_DIM), F32), ((4 * part_rows, 2 * HEAD_DIM), BF16)],
+            (*hidden_blocks, *sums[head]),
+            scratch=[pltpu.VMEM((seq_len, 2 * HEAD_DIM), BF16), pltpu.VMEM((8 * tokens, 2 * HEAD_DIM), BF16)],
+        )
+        weight_parts.append((kept, swap(send, "dp", 1)))
+    awaited = ()
+    for head, (kept, near) in enumerate(weight_parts):
+        (send,) = call(
+            add_near,
+            [((2 * part_rows, 2 * HEAD_DIM), BF16)],
+            (kept, near, *awaited),
+            held=len(awaited),
+            flops=0 if head else 2000000000,
+        )
+        awaited = (send,)
+        weight_parts[head] = (kept, near, swap(send, "dp", 2))
 
     def pack(grad0, grad1, other0, other1, send, kept):
         _, spot, _ = place()
@@ -384,21 +448,15 @@
         (kept, got, query_parts[0][0], query_parts[1][0]),
     )
 
-    def add_planes(own, *refs):
-        *got_refs, kept_ref, send_ref = refs
+    def add_planes(kept, near, far, kept_out, send_out):
         core, _, _ = place()
-        for ref, owner in ((kept_ref, core), (send_ref, 1 - core)):
+        for out, owner in ((kept_out, core), (send_out, 1 - core)):
             rows = pl.ds(pl.multiple_of(owner * part_rows, part_rows), part_rows)
-            total = own[rows, :]
-            for got_ref in got_refs:
-                total += got_ref[rows, :].astype(F32)
-            ref[...] = total
+            out[...] = kept[rows, :] + (near[rows, :].astype(F32) + far[rows, :].astype(F32))
 
     pieces = []
-    for weight_own, weight_got in weight_parts:
-        kept_weight, send_weight = call(
-            add_planes, [((part_rows, 2 * HEAD_DIM), F32)] * 2, (weight_own, *weight_got)
-        )
+    for parts in weight_parts:
+        kept_weight, send_weight = call(add_planes, [((part_rows, 2 * HEAD_DIM), F32)] * 2, parts)
         pieces += [kept_weight, swap(send_weight, "seq", 1)]
 
     def join(kept0, got0, kept1, got1, out):
@@ -429,5 +487,5 @@
         P("dp", "seq", None),
         P(("seq", "dp"), None),
     )
-    body = local_pairs if mesh.shape["seq"] == 2 * KV_HEADS else local
+    body = local_pairs if (mesh.shape["seq"], mesh.shape["dp"]) == (2 * KV_HEADS, 4) else local
     return jax.shard_map(body, mesh=mesh, in_specs=in_specs, out_specs=out_specs, check_vma=False)

time: 74 us -> 64.7 us (0.87)
  waiting for transfers between devices: 36.5 us -> 25.1 us
  starting transfers between devices: 23.5 us -> 25.3 us
  Pallas kernels: 9.46 us -> 11.1 us
  local copies, waits for them, and re-layouts: 3.05 us -> 2.17 us
    ppermute x20 -> x24, waiting for transfers between devices: 36.5 us -> 25.1 us  [swap(): return lax.ppermute(array, axis, [(i, i ^ bit) for i in range(size)])]
    ppermute x20 -> x24, starting transfers between devices: 23.5 us -> 25.3 us  [swap(): return lax.ppermute(array, axis, [(i, i ^ bit) for i in range(size)])]
    pallas_call x14 -> x18, Pallas kernels: 9.46 us -> 11.1 us  [the longest x15 11.1 us: call(): pl.pallas_call(run, out_shape=shapes, in_specs=specs, out_specs=[pl.Block...]
    unnamed x14, local copies, waits for them, and re-layouts: 3.05 us -> 2.15 us
  transfers between devices with their start and end apart: 20 -> 24, of which waited for: 10 -> 9; matrix products, arithmetic and copies ran while one was open for 0% -> 0% of each run, Pallas kernels for 12% -> 16%
where the time goes in v2:
time: 64.7 us; the launch traced here: 64.5 us
  starting transfers between devices  25.3 us (39%)
  waiting for transfers between devices  25.1 us (39%)
  Pallas kernels  11.1 us (17%)
  local copies, waits for them, and re-layouts  2.17 us (3%)
  between operations  0.86 us (1%)
    ppermute x24, starting transfers between devices, swap(): return lax.ppermute(array, axis, [(i, i ^ bit) for i in range(size)])  25.3 us
    ppermute x24, waiting for transfers between devices, swap(): return lax.ppermute(array, axis, [(i, i ^ bit) for i in range(size)])  25.1 us
    pallas_call x15, Pallas kernels, call(): pl.pallas_call(run, out_shape=shapes, in_specs=specs, out_specs=[pl.Block...  11.1 us
    unnamed x14, local copies, waits for them, and re-layouts  2.15 us
  transfers between devices with their start and end apart: 24, of which 9 were waited for; matrix products, arithmetic and copies ran while one was open for 0% of the time, Pallas kernels for 16%

profile of v2, /device:TPU:0, one launch (start us, length us, event | category | flops | bytes accessed | tf_op | source)
XLA Modules:
  0.0 64.5 jit_solution(6397161038958550105)
XLA Ops:
  0.6 0.5 collective-permute-start
  1.2 1.7 %shard_map.102 = (bf16[128,512]{1,0:T(8,128)(2,1)}, bf16[128,512]{1,0:T(8,128)(2,1)}) custom-call(bf16[128,512]{1,0:T(8,128)(2,1)} %bitcast.15, bf16[128,512]{1,0:T(8,128)(2,1)} %bitcast.16), custom_call_target="tpu_custom_call" | custom-call | tf_op jit(solution)/shard_map/pallas_call | solution.py:183
  2.9 0.5 collective-permute-start.2
  3.4 2.6 %collective-permute-start.3 = (bf16[128,512]{1,0:T(8,128)(2,1)}, bf16[128,512]{1,0:T(8,128)(2,1)S(1)}, u32[]{:S(2)}, u32[]{:S(2)}) collective-permute-start(bf16[128,512]{1,0:T(8,128)(2,1)} %get-tuple-element.31.refs_4_.refs_1_), channel_id=1, source_target_pairs={{0,8},{4,12},{8,0},{12,4},{16,24},{20,28},{24,16},{28,20},{1,9},{5... | collective-permute-start | bytes 393224 | tf_op jit(solution)/shard_map/ppermute | solution.py:162
  6.0 1.2 %copy-done = bf16[1,128,4096]{2,1,0:T(8,128)(2,1)S(1)} copy-done((bf16[1,128,4096]{2,1,0:T(8,128)(2,1)S(1)}, bf16[1,128,4096]{2,1,0:T(8,128)(2,1)}, u32[]{:S(2)}) %copy-start) | copy-done | bytes 1048600
  7.3 0.9 %copy-done.1 = bf16[128,512]{1,0:T(8,128)(2,1)S(1)} copy-done((bf16[128,512]{1,0:T(8,128)(2,1)S(1)}, bf16[128,512]{1,0:T(8,128)(2,1)}, u32[]{:S(2)}) %copy-start.1) | copy-done | bytes 131096
  8.3 1.8 %collective-permute-start.6 = (bf16[128,1024]{1,0:T(8,128)(2,1)S(1)}, bf16[128,1024]{1,0:T(8,128)(2,1)S(1)}, u32[]{:S(2)}, u32[]{:S(2)}) collective-permute-start(bf16[128,1024]{1,0:T(8,128)(2,1)S(1)} %shard_map.105), channel_id=1, source_target_pairs={{0,8},{4,12},{8,0},{12,4},{16,24},{20,28},{24,16},{28,20},{1,9},{5... | collective-permute-start | bytes 786440 | tf_op jit(solution)/shard_map/ppermute | solution.py:162
  10.1 1.6 %collective-permute-start.7 = (bf16[128,1024]{1,0:T(8,128)(2,1)S(1)}, bf16[128,1024]{1,0:T(8,128)(2,1)S(1)}, u32[]{:S(2)}, u32[]{:S(2)}) collective-permute-start(bf16[128,1024]{1,0:T(8,128)(2,1)S(1)} %shard_map.106), channel_id=1, source_target_pairs={{0,16},{4,20},{8,24},{12,28},{16,0},{20,4},{24,8},{28,12},{1,17},{... | collective-permute-start | bytes 786440 | tf_op jit(solution)/shard_map/ppermute | solution.py:162
  11.7 1.7 %collective-permute-start.8 = (bf16[128,1024]{1,0:T(8,128)(2,1)S(1)}, bf16[128,1024]{1,0:T(8,128)(2,1)S(1)}, u32[]{:S(2)}, u32[]{:S(2)}) collective-permute-start(bf16[128,1024]{1,0:T(8,128)(2,1)S(1)} %shard_map.108), channel_id=1, source_target_pairs={{0,24},{4,28},{8,16},{12,20},{16,8},{20,12},{24,0},{28,4},{1,25},{... | collective-permute-start | bytes 786440 | tf_op jit(solution)/shard_map/ppermute | solution.py:162
  13.5 2.7 %shard_map.103 = (f32[448,256]{1,0:T(8,128)S(1)}, bf16[448,256]{1,0:T(8,128)(2,1)S(1)}, bf16[128,512]{1,0:T(8,128)(2,1)S(1)}, bf16[128,512]{1,0:T(8,128)(2,1)S(1)}) custom-call(bf16[128,2048]{1,0:T(8,128)(2,1)S(1)} %bitcast.10, bf16[128,2048]{1,0:T(8,128)(2,1)S(1)} %bitcast.13, bf16[128,2048]{1,0:T(8,128)(2,1)S(1)} %collective-permute-done.refs_2_.refs_1_, ...), custom_call_target="tpu_custom_call" | custom-call | flops 11744051200 | tf_op jit(solution)/shard_map/pallas_call | solution.py:183
  16.2 1.0 %collective-permute-start.5 = (bf16[448,256]{1,0:T(8,128)(2,1)S(1)}, bf16[448,256]{1,0:T(8,128)(2,1)S(1)}, u32[]{:S(2)}, u32[]{:S(2)}) collective-permute-start(bf16[448,256]{1,0:T(8,128)(2,1)S(1)} %get-tuple-element.34), channel_id=1, source_target_pairs={{0,8},{4,12},{8,0},{12,4},{16,24},{20,28},{24,16},{28,20},{1,9},{5... | collective-permute-start | bytes 688136 | tf_op jit(solution)/shard_map/ppermute | solution.py:162
  17.2 0.7 %collective-permute-start.11 = (bf16[128,1024]{1,0:T(8,128)(2,1)S(1)}, bf16[128,1024]{1,0:T(8,128)(2,1)S(1)}, u32[]{:S(2)}, u32[]{:S(2)}) collective-permute-start(bf16[128,1024]{1,0:T(8,128)(2,1)S(1)} %get-tuple-element.49.refs_0_), channel_id=1, source_target_pairs={{0,4},{4,0},{8,12},{12,8},{16,20},{20,16},{24,28},{28,24},{1,5},{5... | collective-permute-start | bytes 786440 | tf_op jit(solution)/shard_map/ppermute | solution.py:162
  18.0 1.0 %collective-permute-done.6.refs_10_.refs_2_ = bf16[128,1024]{1,0:T(8,128)(2,1)S(1)} collective-permute-done((bf16[128,1024]{1,0:T(8,128)(2,1)S(1)}, bf16[128,1024]{1,0:T(8,128)(2,1)S(1)}, u32[]{:S(2)}, u32[]{:S(2)}) %collective-permute-start.6) | collective-permute-done | bytes 262176 | tf_op jit(solution)/shard_map/ppermute | solution.py:162
  19.0 2.7 %shard_map.107 = (f32[448,256]{1,0:T(8,128)S(1)}, bf16[448,256]{1,0:T(8,128)(2,1)S(1)}, bf16[128,512]{1,0:T(8,128)(2,1)S(1)}, bf16[128,512]{1,0:T(8,128)(2,1)S(1)}) custom-call(bf16[128,2048]{1,0:T(8,128)(2,1)S(1)} %bitcast.11, bf16[128,2048]{1,0:T(8,128)(2,1)S(1)} %bitcast.14, bf16[128,2048]{1,0:T(8,128)(2,1)S(1)} %collective-permute-done.refs_2_.refs_1_, ...), custom_call_target="tpu_custom_call" | custom-call | tf_op jit(solution)/shard_map/pallas_call | solution.py:183
  21.7 2.0 %collective-permute-start.9 = (bf16[448,256]{1,0:T(8,128)(2,1)S(1)}, bf16[448,256]{1,0:T(8,128)(2,1)S(1)}, u32[]{:S(2)}, u32[]{:S(2)}) collective-permute-start(bf16[448,256]{1,0:T(8,128)(2,1)S(1)} %get-tuple-element.41), channel_id=1, source_target_pairs={{0,8},{4,12},{8,0},{12,4},{16,24},{20,28},{24,16},{28,20},{1,9},{5... | collective-permute-start | bytes 688136 | tf_op jit(solution)/shard_map/ppermute | solution.py:162
  23.7 5.8 %collective-permute-done.5.refs_1_ = bf16[448,256]{1,0:T(8,128)(2,1)S(1)} collective-permute-done((bf16[448,256]{1,0:T(8,128)(2,1)S(1)}, bf16[448,256]{1,0:T(8,128)(2,1)S(1)}, u32[]{:S(2)}, u32[]{:S(2)}) %collective-permute-start.5) | collective-permute-done | bytes 229408 | tf_op jit(solution)/shard_map/ppermute | solution.py:162
  29.5 2.0 %collective-permute-start.16 = (bf16[448,256]{1,0:T(8,128)(2,1)S(1)}, bf16[448,256]{1,0:T(8,128)(2,1)S(1)}, u32[]{:S(2)}, u32[]{:S(2)}) collective-permute-start(bf16[448,256]{1,0:T(8,128)(2,1)S(1)} %shard_map.109.refs_0_.refs_9_), channel_id=1, source_target_pairs={{0,16},{4,20},{8,24},{12,28},{16,0},{20,4},{24,8},{28,12},{1,17},{... | collective-permute-start | bytes 688136 | tf_op jit(solution)/shard_map/ppermute | solution.py:162
  31.6 0.5 collective-permute-start.13
  32.2 1.9 %collective-permute-done.9.refs_1_ = bf16[448,256]{1,0:T(8,128)(2,1)S(1)} collective-permute-done((bf16[448,256]{1,0:T(8,128)(2,1)S(1)}, bf16[448,256]{1,0:T(8,128)(2,1)S(1)}, u32[]{:S(2)}, u32[]{:S(2)}) %collective-permute-start.9) | collective-permute-done | bytes 229408 | tf_op jit(solution)/shard_map/ppermute | solution.py:162
  34.2 1.9 %collective-permute-start.20 = (bf16[448,256]{1,0:T(8,128)(2,1)S(1)}, bf16[448,256]{1,0:T(8,128)(2,1)S(1)}, u32[]{:S(2)}, u32[]{:S(2)}) collective-permute-start(bf16[448,256]{1,0:T(8,128)(2,1)S(1)} %shard_map.110.refs_1_.refs_9_), channel_id=1, source_target_pairs={{0,16},{4,20},{8,24},{12,28},{16,0},{20,4},{24,8},{28,12},{1,17},{... | collective-permute-start | bytes 688136 | tf_op jit(solution)/shard_map/ppermute | solution.py:162
  36.1 0.6 %collective-permute-done.16.refs_10_ = bf16[448,256]{1,0:T(8,128)(2,1)S(1)} collective-permute-done((bf16[448,256]{1,0:T(8,128)(2,1)S(1)}, bf16[448,256]{1,0:T(8,128)(2,1)S(1)}, u32[]{:S(2)}, u32[]{:S(2)}) %collective-permute-start.16) | collective-permute-done | bytes 229408 | tf_op jit(solution)/shard_map/ppermute | solution.py:162
  36.7 0.8 %shard_map.113 = (f32[512,256]{1,0:T(8,128)S(1)}, bf16[512,256]{1,0:T(8,128)(2,1)S(1)}) custom-call(bf16[128,1024]{1,0:T(8,128)(2,1)S(1)} %get-tuple-element.49.refs_0_, bf16[128,1024]{1,0:T(8,128)(2,1)S(1)} %collective-permute-done.11.refs_1_, bf16[128,1024]{1,0:T(8,128)(2,1)S(1)} %collective-permute-done.6.refs_10_.refs_2_, ...), custom_call_target="tpu_custom_call" | custom-call | tf_op jit(solution)/shard_map/pallas_call | solution.py:183
  37.6 1.7 %collective-permute-start.17 = (bf16[512,256]{1,0:T(8,128)(2,1)S(1)}, bf16[512,256]{1,0:T(8,128)(2,1)S(1)}, u32[]{:S(2)}, u32[]{:S(2)}) collective-permute-start(bf16[512,256]{1,0:T(8,128)(2,1)S(1)} %get-tuple-element.51), channel_id=1, source_target_pairs={{0,1},{1,0},{2,3},{3,2},{4,5},{5,4},{6,7},{7,6},{8,9},{9,8},{10,11... | collective-permute-start | bytes 786440 | tf_op jit(solution)/shard_map/ppermute | solution.py:162
  39.3 3.1 %collective-permute-done.20.refs_10_ = bf16[448,256]{1,0:T(8,128)(2,1)S(1)} collective-permute-done((bf16[448,256]{1,0:T(8,128)(2,1)S(1)}, bf16[448,256]{1,0:T(8,128)(2,1)S(1)}, u32[]{:S(2)}, u32[]{:S(2)}) %collective-permute-start.20) | collective-permute-done | bytes 229408 | tf_op jit(solution)/shard_map/ppermute | solution.py:162
  42.3 0.8 %shard_map.116 = (f32[512,256]{1,0:T(8,128)S(1)}, bf16[512,256]{1,0:T(8,128)(2,1)S(1)}) custom-call(bf16[128,1024]{1,0:T(8,128)(2,1)S(1)} %get-tuple-element.49.refs_0_, bf16[128,1024]{1,0:T(8,128)(2,1)S(1)} %collective-permute-done.11.refs_1_, bf16[128,1024]{1,0:T(8,128)(2,1)S(1)} %collective-permute-done.6.refs_10_.refs_2_, ...), custom_call_target="tpu_custom_call" | custom-call | tf_op jit(solution)/shard_map/pallas_call | solution.py:183
  43.2 1.9 %collective-permute-start.21 = (bf16[512,256]{1,0:T(8,128)(2,1)S(1)}, bf16[512,256]{1,0:T(8,128)(2,1)S(1)}, u32[]{:S(2)}, u32[]{:S(2)}) collective-permute-start(bf16[512,256]{1,0:T(8,128)(2,1)S(1)} %get-tuple-element.55), channel_id=1, source_target_pairs={{0,1},{1,0},{2,3},{3,2},{4,5},{5,4},{6,7},{7,6},{8,9},{9,8},{10,11... | collective-permute-start | bytes 786440 | tf_op jit(solution)/shard_map/ppermute | solution.py:162
  45.5 2.7 %collective-permute-start.18 = (bf16[256,256]{1,0:T(8,128)(2,1)S(1)}, bf16[256,256]{1,0:T(8,128)(2,1)S(1)}, u32[]{:S(2)}, u32[]{:S(2)}) collective-permute-start(bf16[256,256]{1,0:T(8,128)(2,1)S(1)} %shard_map.114.refs_2_), channel_id=1, source_target_pairs={{0,2},{1,3},{2,0},{3,1},{4,6},{5,7},{6,4},{7,5},{8,10},{9,11},{10,... | collective-permute-start | bytes 393224 | tf_op jit(solution)/shard_map/ppermute | solution.py:162
  48.1 5.9 %collective-permute-done.21.refs_1_ = bf16[512,256]{1,0:T(8,128)(2,1)S(1)} collective-permute-done((bf16[512,256]{1,0:T(8,128)(2,1)S(1)}, bf16[512,256]{1,0:T(8,128)(2,1)S(1)}, u32[]{:S(2)}, u32[]{:S(2)}) %collective-permute-start.21) | collective-permute-done | bytes 262176 | tf_op jit(solution)/shard_map/ppermute | solution.py:162
  54.1 1.8 %collective-permute-start.22 = (bf16[256,256]{1,0:T(8,128)(2,1)S(1)}, bf16[256,256]{1,0:T(8,128)(2,1)S(1)}, u32[]{:S(2)}, u32[]{:S(2)}) collective-permute-start(bf16[256,256]{1,0:T(8,128)(2,1)S(1)} %shard_map.117), channel_id=1, source_target_pairs={{0,2},{1,3},{2,0},{3,1},{4,6},{5,7},{6,4},{7,5},{8,10},{9,11},{10,... | collective-permute-start | bytes 393224 | tf_op jit(solution)/shard_map/ppermute | solution.py:162
  56.1 6.1 %collective-permute-done.22.refs_2_ = bf16[256,256]{1,0:T(8,128)(2,1)S(1)} collective-permute-done((bf16[256,256]{1,0:T(8,128)(2,1)S(1)}, bf16[256,256]{1,0:T(8,128)(2,1)S(1)}, u32[]{:S(2)}, u32[]{:S(2)}) %collective-permute-start.22) | collective-permute-done | bytes 131104 | tf_op jit(solution)/shard_map/ppermute | solution.py:162
  62.3 1.0 %shard_map.112 = (bf16[128,2048]{1,0:T(8,128)(2,1)}, bf16[128,512]{1,0:T(8,128)(2,1)}, bf16[128,512]{1,0:T(8,128)(2,1)}) custom-call(bf16[128,512]{1,0:T(8,128)(2,1)S(1)} %get-tuple-element.44.refs_0_, bf16[128,1536]{1,0:T(8,128)(2,1)S(1)} %collective-permute-done.10.refs_1_, bf16[128,512]{1,0:T(8,128)(2,1)S(1)} %get-tuple-element.37.refs_12_.refs_2_, ...), custom_call_target="tpu_custom_call" | custom-call | tf_op jit(solution)/shard_map/pallas_call | solution.py:183
  63.6 0.9 %shard_map.119 = f32[128,1024]{1,0:T(8,128)} custom-call(f32[128,256]{1,0:T(8,128)S(1)} %get-tuple-element.52.refs_0_, f32[128,256]{1,0:T(8,128)S(1)} %collective-permute-done.19.refs_1_, f32[128,256]{1,0:T(8,128)S(1)} %get-tuple-element.56.refs_2_, f32[128,256]{1,0:T(8,128)S(1)} %collective-permute-done.23.refs_3_), custom_call_target="tpu_custom_call" | custom-call | tf_op jit(solution)/shard_map/pallas_call | solution.py:183
  (49 shorter events, 1.5 us)
Async XLA Ops:
  0.6 7.7 %collective-permute-start = (bf16[128,2048]{1,0:T(8,128)(2,1)}, bf16[128,2048]{1,0:T(8,128)(2,1)S(1)}, u32[]{:S(2)}, u32[]{:S(2)}) collective-permute-start(bf16[128,2048]{1,0:T(8,128)(2,1)} %bitcast.9), channel_id=1, source_target_pairs={{0,4},{4,0},{8,12},{12,8},{16,20},{20,16},{24,28},{28,24},{1,5},{5... | collective-permute-start | bytes 1572872 | tf_op jit(solution)/shard_map/ppermute | solution.py:162
  1.1 12.3 %collective-permute-start.1 = (bf16[128,2048]{1,0:T(8,128)(2,1)}, bf16[128,2048]{1,0:T(8,128)(2,1)S(1)}, u32[]{:S(2)}, u32[]{:S(2)}) collective-permute-start(bf16[128,2048]{1,0:T(8,128)(2,1)} %bitcast.12), channel_id=1, source_target_pairs={{0,4},{4,0},{8,12},{12,8},{16,20},{20,16},{24,28},{28,24},{1,5},{5... | collective-permute-start | bytes 1572872 | tf_op jit(solution)/shard_map/ppermute | solution.py:162
  2.9 7.2 %collective-permute-start.2 = (bf16[128,512]{1,0:T(8,128)(2,1)}, bf16[128,512]{1,0:T(8,128)(2,1)S(1)}, u32[]{:S(2)}, u32[]{:S(2)}) collective-permute-start(bf16[128,512]{1,0:T(8,128)(2,1)} %get-tuple-element.32), channel_id=1, source_target_pairs={{0,4},{4,0},{8,12},{12,8},{16,20},{20,16},{24,28},{28,24},{1,5},{5... | collective-permute-start | bytes 393224 | tf_op jit(solution)/shard_map/ppermute | solution.py:162
  3.4 8.3 %collective-permute-start.3 = (bf16[128,512]{1,0:T(8,128)(2,1)}, bf16[128,512]{1,0:T(8,128)(2,1)S(1)}, u32[]{:S(2)}, u32[]{:S(2)}) collective-permute-start(bf16[128,512]{1,0:T(8,128)(2,1)} %get-tuple-element.31.refs_4_.refs_1_), channel_id=1, source_target_pairs={{0,8},{4,12},{8,0},{12,4},{16,24},{20,28},{24,16},{28,20},{1,9},{5... | collective-permute-start | bytes 393224 | tf_op jit(solution)/shard_map/ppermute | solution.py:162
  6.0 7.5 %collective-permute-start.4 = (bf16[128,512]{1,0:T(8,128)(2,1)}, bf16[128,512]{1,0:T(8,128)(2,1)S(1)}, u32[]{:S(2)}, u32[]{:S(2)}) collective-permute-start(bf16[128,512]{1,0:T(8,128)(2,1)} %get-tuple-element.32), channel_id=1, source_target_pairs={{0,12},{4,8},{8,4},{12,0},{16,28},{20,24},{24,20},{28,16},{1,13},{... | collective-permute-start | bytes 393224 | tf_op jit(solution)/shard_map/ppermute | solution.py:162
  6.0 1.2 %copy-start = (bf16[1,128,4096]{2,1,0:T(8,128)(2,1)S(1)}, bf16[1,128,4096]{2,1,0:T(8,128)(2,1)}, u32[]{:S(2)}) copy-start(bf16[1,128,4096]{2,1,0:T(8,128)(2,1)} %param.11) | copy-start | bytes 3145732
  7.3 0.9 %copy-start.1 = (bf16[128,512]{1,0:T(8,128)(2,1)S(1)}, bf16[128,512]{1,0:T(8,128)(2,1)}, u32[]{:S(2)}) copy-start(bf16[128,512]{1,0:T(8,128)(2,1)} %get-tuple-element.31.refs_4_.refs_1_) | copy-start | bytes 393220
  8.3 10.6 %collective-permute-start.6 = (bf16[128,1024]{1,0:T(8,128)(2,1)S(1)}, bf16[128,1024]{1,0:T(8,128)(2,1)S(1)}, u32[]{:S(2)}, u32[]{:S(2)}) collective-permute-start(bf16[128,1024]{1,0:T(8,128)(2,1)S(1)} %shard_map.105), channel_id=1, source_target_pairs={{0,8},{4,12},{8,0},{12,4},{16,24},{20,28},{24,16},{28,20},{1,9},{5... | collective-permute-start | bytes 786440 | tf_op jit(solution)/shard_map/ppermute | solution.py:162
  10.1 3.3 %copy-start.4 = (bf16[1,128,2048]{2,1,0:T(8,128)(2,1)S(1)}, bf16[1,128,2048]{2,1,0:T(8,128)(2,1)}, u32[]{:S(2)}) copy-start(bf16[1,128,2048]{2,1,0:T(8,128)(2,1)} %param.10) | copy-start | bytes 1572868
  10.1 3.3 %copy-start.2 = (bf16[128,512]{1,0:T(8,128)(2,1)S(1)}, bf16[128,512]{1,0:T(8,128)(2,1)}, u32[]{:S(2)}) copy-start(bf16[128,512]{1,0:T(8,128)(2,1)} %get-tuple-element.31.refs_4_.refs_1_) | copy-start | bytes 393220
  10.1 3.3 %copy-start.3 = (bf16[1,128,2048]{2,1,0:T(8,128)(2,1)S(1)}, bf16[1,128,2048]{2,1,0:T(8,128)(2,1)}, u32[]{:S(2)}) copy-start(bf16[1,128,2048]{2,1,0:T(8,128)(2,1)} %param.7) | copy-start | bytes 1572868
  10.1 3.4 %copy-start.5 = (s32[2]{0:T(128)S(1)}, s32[2]{0:T(128)}, u32[]{:S(2)}) copy-start(s32[2]{0:T(128)} %refs_8_.3) | copy-start | bytes 28
  10.1 3.4 %copy-start.6 = (s32[2]{0:T(128)S(1)}, s32[2]{0:T(128)}, u32[]{:S(2)}) copy-start(s32[2]{0:T(128)} %refs_9_.3) | copy-start | bytes 28
  10.1 8.8 %collective-permute-start.7 = (bf16[128,1024]{1,0:T(8,128)(2,1)S(1)}, bf16[128,1024]{1,0:T(8,128)(2,1)S(1)}, u32[]{:S(2)}, u32[]{:S(2)}) collective-permute-start(bf16[128,1024]{1,0:T(8,128)(2,1)S(1)} %shard_map.106), channel_id=1, source_target_pairs={{0,16},{4,20},{8,24},{12,28},{16,0},{20,4},{24,8},{28,12},{1,17},{... | collective-permute-start | bytes 786440 | tf_op jit(solution)/shard_map/ppermute | solution.py:162
  11.7 17.8 %collective-permute-start.8 = (bf16[128,1024]{1,0:T(8,128)(2,1)S(1)}, bf16[128,1024]{1,0:T(8,128)(2,1)S(1)}, u32[]{:S(2)}, u32[]{:S(2)}) collective-permute-start(bf16[128,1024]{1,0:T(8,128)(2,1)S(1)} %shard_map.108), channel_id=1, source_target_pairs={{0,24},{4,28},{8,16},{12,20},{16,8},{20,12},{24,0},{28,4},{1,25},{... | collective-permute-start | bytes 786440 | tf_op jit(solution)/shard_map/ppermute | solution.py:162
  16.2 13.3 %collective-permute-start.5 = (bf16[448,256]{1,0:T(8,128)(2,1)S(1)}, bf16[448,256]{1,0:T(8,128)(2,1)S(1)}, u32[]{:S(2)}, u32[]{:S(2)}) collective-permute-start(bf16[448,256]{1,0:T(8,128)(2,1)S(1)} %get-tuple-element.34), channel_id=1, source_target_pairs={{0,8},{4,12},{8,0},{12,4},{16,24},{20,28},{24,16},{28,20},{1,9},{5... | collective-permute-start | bytes 688136 | tf_op jit(solution)/shard_map/ppermute | solution.py:162
  17.2 14.9 %collective-permute-start.11 = (bf16[128,1024]{1,0:T(8,128)(2,1)S(1)}, bf16[128,1024]{1,0:T(8,128)(2,1)S(1)}, u32[]{:S(2)}, u32[]{:S(2)}) collective-permute-start(bf16[128,1024]{1,0:T(8,128)(2,1)S(1)} %get-tuple-element.49.refs_0_), channel_id=1, source_target_pairs={{0,4},{4,0},{8,12},{12,8},{16,20},{20,16},{24,28},{28,24},{1,5},{5... | collective-permute-start | bytes 786440 | tf_op jit(solution)/shard_map/ppermute | solution.py:162
  21.7 12.5 %collective-permute-start.9 = (bf16[448,256]{1,0:T(8,128)(2,1)S(1)}, bf16[448,256]{1,0:T(8,128)(2,1)S(1)}, u32[]{:S(2)}, u32[]{:S(2)}) collective-permute-start(bf16[448,256]{1,0:T(8,128)(2,1)S(1)} %get-tuple-element.41), channel_id=1, source_target_pairs={{0,8},{4,12},{8,0},{12,4},{16,24},{20,28},{24,16},{28,20},{1,9},{5... | collective-permute-start | bytes 688136 | tf_op jit(solution)/shard_map/ppermute | solution.py:162
  29.5 7.2 %collective-permute-start.16 = (bf16[448,256]{1,0:T(8,128)(2,1)S(1)}, bf16[448,256]{1,0:T(8,128)(2,1)S(1)}, u32[]{:S(2)}, u32[]{:S(2)}) collective-permute-start(bf16[448,256]{1,0:T(8,128)(2,1)S(1)} %shard_map.109.refs_0_.refs_9_), channel_id=1, source_target_pairs={{0,16},{4,20},{8,24},{12,28},{16,0},{20,4},{24,8},{28,12},{1,17},{... | collective-permute-start | bytes 688136 | tf_op jit(solution)/shard_map/ppermute | solution.py:162
  31.6 5.1 %collective-permute-start.12 = (bf16[128,1024]{1,0:T(8,128)(2,1)S(1)}, bf16[128,1024]{1,0:T(8,128)(2,1)S(1)}, u32[]{:S(2)}, u32[]{:S(2)}) collective-permute-start(bf16[128,1024]{1,0:T(8,128)(2,1)S(1)} %collective-permute-done.6.refs_10_.refs_2_), channel_id=1, source_target_pairs={{0,4},{4,0},{8,12},{12,8},{16,20},{20,16},{24,28},{28,24},{1,5},{5... | collective-permute-start | bytes 786440 | tf_op jit(solution)/shard_map/ppermute | solution.py:162
  31.6 5.1 %collective-permute-start.13 = (bf16[128,1024]{1,0:T(8,128)(2,1)S(1)}, bf16[128,1024]{1,0:T(8,128)(2,1)S(1)}, u32[]{:S(2)}, u32[]{:S(2)}) collective-permute-start(bf16[128,1024]{1,0:T(8,128)(2,1)S(1)} %collective-permute-done.7.refs_11_.refs_4_), channel_id=1, source_target_pairs={{0,4},{4,0},{8,12},{12,8},{16,20},{20,16},{24,28},{28,24},{1,5},{5... | collective-permute-start | bytes 786440 | tf_op jit(solution)/shard_map/ppermute | solution.py:162
  32.1 2.1 %collective-permute-start.14 = (bf16[64,1024]{1,0:T(8,128)(2,1)S(1)}, bf16[64,1024]{1,0:T(8,128)(2,1)S(1)}, u32[]{:S(2)}, u32[]{:S(2)}) collective-permute-start(bf16[64,1024]{1,0:T(8,128)(2,1)S(1)} %get-tuple-element.59), channel_id=1, source_target_pairs={{0,4},{4,0},{8,12},{12,8},{16,20},{20,16},{24,28},{28,24},{1,5},{5... | collective-permute-start | bytes 393224 | tf_op jit(solution)/shard_map/ppermute | solution.py:162
  34.1 1.9 %collective-permute-start.15 = (bf16[64,1024]{1,0:T(8,128)(2,1)S(1)}, bf16[64,1024]{1,0:T(8,128)(2,1)S(1)}, u32[]{:S(2)}, u32[]{:S(2)}) collective-permute-start(bf16[64,1024]{1,0:T(8,128)(2,1)S(1)} %get-tuple-element.58), channel_id=1, source_target_pairs={{0,4},{4,0},{8,12},{12,8},{16,20},{20,16},{24,28},{28,24},{1,5},{5... | collective-permute-start | bytes 393224 | tf_op jit(solution)/shard_map/ppermute | solution.py:162
  34.2 8.1 %collective-permute-start.20 = (bf16[448,256]{1,0:T(8,128)(2,1)S(1)}, bf16[448,256]{1,0:T(8,128)(2,1)S(1)}, u32[]{:S(2)}, u32[]{:S(2)}) collective-permute-start(bf16[448,256]{1,0:T(8,128)(2,1)S(1)} %shard_map.110.refs_1_.refs_9_), channel_id=1, source_target_pairs={{0,16},{4,20},{8,24},{12,28},{16,0},{20,4},{24,8},{28,12},{1,17},{... | collective-permute-start | bytes 688136 | tf_op jit(solution)/shard_map/ppermute | solution.py:162
  37.6 7.9 %collective-permute-start.17 = (bf16[512,256]{1,0:T(8,128)(2,1)S(1)}, bf16[512,256]{1,0:T(8,128)(2,1)S(1)}, u32[]{:S(2)}, u32[]{:S(2)}) collective-permute-start(bf16[512,256]{1,0:T(8,128)(2,1)S(1)} %get-tuple-element.51), channel_id=1, source_target_pairs={{0,1},{1,0},{2,3},{3,2},{4,5},{5,4},{6,7},{7,6},{8,9},{9,8},{10,11... | collective-permute-start | bytes 786440 | tf_op jit(solution)/shard_map/ppermute | solution.py:162
  43.2 10.9 %collective-permute-start.21 = (bf16[512,256]{1,0:T(8,128)(2,1)S(1)}, bf16[512,256]{1,0:T(8,128)(2,1)S(1)}, u32[]{:S(2)}, u32[]{:S(2)}) collective-permute-start(bf16[512,256]{1,0:T(8,128)(2,1)S(1)} %get-tuple-element.55), channel_id=1, source_target_pairs={{0,1},{1,0},{2,3},{3,2},{4,5},{5,4},{6,7},{7,6},{8,9},{9,8},{10,11... | collective-permute-start | bytes 786440 | tf_op jit(solution)/shard_map/ppermute | solution.py:162
  45.1 17.2 %collective-permute-start.10 = (bf16[128,1536]{1,0:T(8,128)(2,1)S(1)}, bf16[128,1536]{1,0:T(8,128)(2,1)S(1)}, u32[]{:S(2)}, u32[]{:S(2)}) collective-permute-start(bf16[128,1536]{1,0:T(8,128)(2,1)S(1)} %get-tuple-element.45), channel_id=1, source_target_pairs={{0,4},{4,0},{8,12},{12,8},{16,20},{20,16},{24,28},{28,24},{1,5},{5... | collective-permute-start | bytes 1179656 | tf_op jit(solution)/shard_map/ppermute | solution.py:162
  45.5 10.5 %collective-permute-start.18 = (bf16[256,256]{1,0:T(8,128)(2,1)S(1)}, bf16[256,256]{1,0:T(8,128)(2,1)S(1)}, u32[]{:S(2)}, u32[]{:S(2)}) collective-permute-start(bf16[256,256]{1,0:T(8,128)(2,1)S(1)} %shard_map.114.refs_2_), channel_id=1, source_target_pairs={{0,2},{1,3},{2,0},{3,1},{4,6},{5,7},{6,4},{7,5},{8,10},{9,11},{10,... | collective-permute-start | bytes 393224 | tf_op jit(solution)/shard_map/ppermute | solution.py:162
  54.1 8.1 %collective-permute-start.22 = (bf16[256,256]{1,0:T(8,128)(2,1)S(1)}, bf16[256,256]{1,0:T(8,128)(2,1)S(1)}, u32[]{:S(2)}, u32[]{:S(2)}) collective-permute-start(bf16[256,256]{1,0:T(8,128)(2,1)S(1)} %shard_map.117), channel_id=1, source_target_pairs={{0,2},{1,3},{2,0},{3,1},{4,6},{5,7},{6,4},{7,5},{8,10},{9,11},{10,... | collective-permute-start | bytes 393224 | tf_op jit(solution)/shard_map/ppermute | solution.py:162
  56.0 7.3 %collective-permute-start.19 = (f32[128,256]{1,0:T(8,128)S(1)}, f32[128,256]{1,0:T(8,128)S(1)}, u32[]{:S(2)}, u32[]{:S(2)}) collective-permute-start(f32[128,256]{1,0:T(8,128)S(1)} %get-tuple-element.53), channel_id=1, source_target_pairs={{0,4},{4,0},{8,12},{12,8},{16,20},{20,16},{24,28},{28,24},{1,5},{5... | collective-permute-start | bytes 393224 | tf_op jit(solution)/shard_map/ppermute | solution.py:162
  62.2 1.4 %collective-permute-start.23 = (f32[128,256]{1,0:T(8,128)S(1)}, f32[128,256]{1,0:T(8,128)S(1)}, u32[]{:S(2)}, u32[]{:S(2)}) collective-permute-start(f32[128,256]{1,0:T(8,128)S(1)} %get-tuple-element.57), channel_id=1, source_target_pairs={{0,4},{4,0},{8,12},{12,8},{16,20},{20,16},{24,28},{28,24},{1,5},{5... | collective-permute-start | bytes 393224 | tf_op jit(solution)/shard_map/ppermute | solution.py:162

commit v3 on v2

--- a/solution.py
+++ b/solution.py
@@ -234,31 +234,11 @@
         me = lax.axis_index("seq")
         return me % 2, me % 4, me // 4
 
-    def split_pairs(key_ref, value_ref, kv_mine, kv_other, sems):
-        core, _, _ = place()
-        copy_all(
-            sems,
-            [
-                (ref.at[:, lanes(half * kv_width, kv_width)], out.at[:, pl.ds(part * kv_width, kv_width)])
-                for half, out in ((core, kv_mine), (1 - core, kv_other))
-                for part, ref in enumerate((key_ref, value_ref))
-            ],
-        )
-
-    kv_mine, kv_other = call(
-        split_pairs,
-        [((tokens, 2 * kv_width), BF16)] * 2,
-        (keys, values),
-        scratch=[pltpu.SemaphoreType.DMA((4,))],
-        place=pl.ANY,
-        vmem=60,
-    )
-    kv_far = swap(kv_mine, "seq", 2)
-    kv_cross = swap(kv_other, "seq", 3)
-
-    kv_pair = swap(kv_other, "seq", 1)
-    query_pair = swap(query, "seq", 1)
-    grad_pair = swap(out_grad, "seq", 1)
+    pairs = {0: (keys, values), 2: (swap(keys, "seq", 2), swap(values, "seq", 2))}
+    query_pair, grad_pair = swap(query, "seq", 1), swap(out_grad, "seq", 1)
+    for flip in (0, 2):
+        pairs[flip + 1] = tuple(swap(array, "seq", 1) for array in pairs[flip])
+    key_blocks, value_blocks = zip(*(pairs[flip] for flip in range(4)))
 
     def split_hidden(hidden_ref, *outs):
         *outs, sems = outs
@@ -274,9 +254,8 @@
     hidden_send = call(
         split_hidden,
         [((tokens, pair_rows), BF16)] * 4,
-        (hidden, kv_mine),
+        (hidden,),
         scratch=[pltpu.SemaphoreType.DMA((4,))],
-        held=1,
         place=pl.ANY,
     )
     hidden_core = {
@@ -286,13 +265,17 @@
         3: swap(after(hidden_send[3], query_pair), "seq", 6),
     }
 
-    def attention(head, query_ref, grad_ref, query_far, grad_far, kv0, kv1, kv2, kv3, start_ref, len_ref, part, part_low, mine, other, key_all, value_all):
+    hidden_pair = {flip: swap(hidden_core[flip], "seq", 1) for flip in (0, 1, 2)}
+
+    def attention(head, *refs):
+        query_ref, grad_ref, query_far, grad_far, *pair_refs = refs[:12]
+        start_ref, len_ref, part, part_low, mine, other, key_all, value_all = refs[12:]
         core, spot, seq_idx = place()
-        for flip, ref in enumerate((kv0, kv1, kv2, kv3)):
+        for flip in range(4):
             rows = pl.ds(pl.multiple_of(jnp.bitwise_xor(spot, flip) * tokens, tokens), tokens)
-            key_all[rows, :] = ref[:, head * HEAD_DIM : (head + 1) * HEAD_DIM]
-            first = kv_width + head * HEAD_DIM
-            value_all[rows, :] = ref[:, first : first + HEAD_DIM]
+            columns = lanes(core * kv_width + head * HEAD_DIM, HEAD_DIM)
+            key_all[rows, :] = pair_refs[flip][:, columns]
+            value_all[rows, :] = pair_refs[4 + flip][:, columns]
         key = key_all[:seen, :]
         value = value_all[:seen, :]
         start = start_ref[seq_idx]
@@ -363,7 +346,7 @@
     grads, query_parts, weight_parts = [], [], []
     sums = []
     for head in range(own_heads):
-        awaited = (hidden_core[1], hidden_core[2], query_parts[0][0]) if head else ()
+        awaited = (hidden_pair[1], hidden_pair[2], query_parts[0][0]) if head else ()
         part, part_low, query_mine, query_other = call(
             functools.partial(attention, head),
             [
@@ -372,23 +355,21 @@
                 ((tokens, group_width), BF16),
                 ((tokens, group_width), BF16),
             ],
-            (query, out_grad, query_pair, grad_pair, kv_mine, kv_pair, kv_far, kv_cross, q_start, q_len, *awaited),
+            (query, out_grad, query_pair, grad_pair, *key_blocks, *value_blocks, q_start, q_len, *awaited),
             scratch=[pltpu.VMEM((seq_len, HEAD_DIM), BF16)] * 2,
             smem=2,
             held=len(awaited),
             vmem=32,
-            flops=10 * seen * 2 * group_width * tokens * (0 if head else 20),
+            flops=10 * seen * 2 * group_width * tokens * (0 if head else 2),
         )
         query_parts.append((query_mine, query_other))
         if head:
             (grad,) = call(add_parts, [((seen, 2 * HEAD_DIM), BF16)], (*sums[0], query_mine, hidden_core[3]), held=2)
             sums[0] = (grad, swap(grad, "seq", 4))
         sums.append((part, swap(part_low, "seq", 2)))
-    hidden_blocks = []
-    for flip in range(4):
-        block = hidden_core[flip]
-        halves = (block[: tokens // 2], block[tokens // 2 :]) if flip == 3 else (block,)
-        hidden_blocks += [block, *[swap(half, "seq", 1) for half in halves]]
+    halves = [swap(half, "seq", 1) for half in (hidden_core[3][: tokens // 2], hidden_core[3][tokens // 2 :])]
+    hidden_blocks = [block for flip in (0, 1, 2) for block in (hidden_core[flip], hidden_pair[flip])]
+    hidden_blocks += [hidden_core[3], *halves]
     (grad,) = call(add_parts, [((seen, 2 * HEAD_DIM), BF16)], sums[1])
     sums[1] = (grad, swap(grad, "seq", 4))
     for head in range(own_heads):

time: 64.7 us -> 61.7 us (0.954)
  Pallas kernels: 11.1 us -> 9.45 us
  local copies, waits for them, and re-layouts: 2.17 us -> 1.26 us
  starting transfers between devices: 25.3 us -> 24.6 us
    pallas_call x15 -> x14, Pallas kernels: 11.1 us -> 9.45 us  [call(): pl.pallas_call(run, out_shape=shapes, in_specs=specs, out_specs=[pl.Block...]
    unnamed x14, local copies, waits for them, and re-layouts: 2.15 us -> 1.25 us
    ppermute x24 -> x27, starting transfers between devices: 25.3 us -> 24.6 us  [swap(): return lax.ppermute(array, axis, [(i, i ^ bit) for i in range(size)])]
    ppermute x24 -> x27, waiting for transfers between devices: 25.1 us -> 25.4 us  [swap(): return lax.ppermute(array, axis, [(i, i ^ bit) for i in range(size)])]
  transfers between devices with their start and end apart: 24 -> 27, of which waited for: 9 -> 12; matrix products, arithmetic and copies ran while one was open for 0% -> 0% of each run, Pallas kernels for 16% -> 14%
where the time goes in v3:
time: 61.7 us; the launch traced here: 61.6 us
  waiting for transfers between devices  25.4 us (41%)
  starting transfers between devices  24.6 us (40%)
  Pallas kernels  9.45 us (15%)
  local copies, waits for them, and re-layouts  1.26 us (2%)
  between operations  0.84 us (1%)
    ppermute x27, waiting for transfers between devices, swap(): return lax.ppermute(array, axis, [(i, i ^ bit) for i in range(size)])  25.4 us
    ppermute x27, starting transfers between devices, swap(): return lax.ppermute(array, axis, [(i, i ^ bit) for i in range(size)])  24.6 us
    pallas_call x14, Pallas kernels, call(): pl.pallas_call(run, out_shape=shapes, in_specs=specs, out_specs=[pl.Block...  9.45 us
    unnamed x14, local copies, waits for them, and re-layouts  1.25 us
  transfers between devices with their start and end apart: 27, of which 12 were waited for; matrix products, arithmetic and copies ran while one was open for 0% of the time, Pallas kernels for 14%

profile of v3, /device:TPU:0, one launch (start us, length us, event | category | flops | bytes accessed | tf_op | source)
XLA Modules:
  0.0 61.6 jit_solution(14927682007522522961)
XLA Ops:
  0.6 0.5 collective-permute-start
  1.2 2.9 %collective-permute-start.3 = (bf16[128,512]{1,0:T(8,128)(2,1)}, bf16[128,512]{1,0:T(8,128)(2,1)S(1)}, u32[]{:S(2)}, u32[]{:S(2)}) collective-permute-start(bf16[128,512]{1,0:T(8,128)(2,1)} %bitcast.15), channel_id=1, source_target_pairs={{0,8},{4,12},{8,0},{12,4},{16,24},{20,28},{24,16},{28,20},{1,9},{5... | collective-permute-start | bytes 393224 | tf_op jit(solution)/shard_map/ppermute | solution.py:162
  4.2 1.2 %copy-done = bf16[1,128,4096]{2,1,0:T(8,128)(2,1)S(1)} copy-done((bf16[1,128,4096]{2,1,0:T(8,128)(2,1)S(1)}, bf16[1,128,4096]{2,1,0:T(8,128)(2,1)}, u32[]{:S(2)}) %copy-start) | copy-done | bytes 1048600
  5.6 2.1 %collective-permute-start.9 = (bf16[128,1024]{1,0:T(8,128)(2,1)S(1)}, bf16[128,1024]{1,0:T(8,128)(2,1)S(1)}, u32[]{:S(2)}, u32[]{:S(2)}) collective-permute-start(bf16[128,1024]{1,0:T(8,128)(2,1)S(1)} %shard_map.104), channel_id=1, source_target_pairs={{0,8},{4,12},{8,0},{12,4},{16,24},{20,28},{24,16},{28,20},{1,9},{5... | collective-permute-start | bytes 786440 | tf_op jit(solution)/shard_map/ppermute | solution.py:162
  7.6 1.0 %collective-permute-done.3.refs_6_ = bf16[128,512]{1,0:T(8,128)(2,1)S(1)} collective-permute-done((bf16[128,512]{1,0:T(8,128)(2,1)}, bf16[128,512]{1,0:T(8,128)(2,1)S(1)}, u32[]{:S(2)}, u32[]{:S(2)}) %collective-permute-start.3) | collective-permute-done | bytes 131104 | tf_op jit(solution)/shard_map/ppermute | solution.py:162
  8.6 2.1 %collective-permute-start.11 = (bf16[128,1024]{1,0:T(8,128)(2,1)S(1)}, bf16[128,1024]{1,0:T(8,128)(2,1)S(1)}, u32[]{:S(2)}, u32[]{:S(2)}) collective-permute-start(bf16[128,1024]{1,0:T(8,128)(2,1)S(1)} %shard_map.105), channel_id=1, source_target_pairs={{0,16},{4,20},{8,24},{12,28},{16,0},{20,4},{24,8},{28,12},{1,17},{... | collective-permute-start | bytes 786440 | tf_op jit(solution)/shard_map/ppermute | solution.py:162
  10.7 0.7 %collective-permute-done.6.refs_10_ = bf16[128,512]{1,0:T(8,128)(2,1)S(1)} collective-permute-done((bf16[128,512]{1,0:T(8,128)(2,1)}, bf16[128,512]{1,0:T(8,128)(2,1)S(1)}, u32[]{:S(2)}, u32[]{:S(2)}) %collective-permute-start.6) | collective-permute-done | bytes 131104 | tf_op jit(solution)/shard_map/ppermute | solution.py:162
  11.5 0.5 collective-permute-start.4
  12.0 0.8 %collective-permute-done.5.refs_9_ = bf16[128,512]{1,0:T(8,128)(2,1)S(1)} collective-permute-done((bf16[128,512]{1,0:T(8,128)(2,1)S(1)}, bf16[128,512]{1,0:T(8,128)(2,1)S(1)}, u32[]{:S(2)}, u32[]{:S(2)}) %collective-permute-start.5) | collective-permute-done | bytes 131104 | tf_op jit(solution)/shard_map/ppermute | solution.py:162
  13.0 3.1 %collective-permute-start.13 = (bf16[128,1024]{1,0:T(8,128)(2,1)S(1)}, bf16[128,1024]{1,0:T(8,128)(2,1)S(1)}, u32[]{:S(2)}, u32[]{:S(2)}) collective-permute-start(bf16[128,1024]{1,0:T(8,128)(2,1)S(1)} %shard_map.107), channel_id=1, source_target_pairs={{0,24},{4,28},{8,16},{12,20},{16,8},{20,12},{24,0},{28,4},{1,25},{... | collective-permute-start | bytes 786440 | tf_op jit(solution)/shard_map/ppermute | solution.py:162
  16.5 0.5 collective-permute-start.12
  17.1 2.8 %shard_map.102 = (f32[448,256]{1,0:T(8,128)S(1)}, bf16[448,256]{1,0:T(8,128)(2,1)S(1)}, bf16[128,512]{1,0:T(8,128)(2,1)S(1)}, bf16[128,512]{1,0:T(8,128)(2,1)S(1)}) custom-call(bf16[128,2048]{1,0:T(8,128)(2,1)S(1)} %bitcast.10, bf16[128,2048]{1,0:T(8,128)(2,1)S(1)} %bitcast.13, bf16[128,2048]{1,0:T(8,128)(2,1)S(1)} %collective-permute-done.refs_2_.refs_1_, ...), custom_call_target="tpu_custom_call" | custom-call | flops 1174405120 | tf_op jit(solution)/shard_map/pallas_call | solution.py:183
  19.8 1.8 %collective-permute-start.8 = (bf16[448,256]{1,0:T(8,128)(2,1)S(1)}, bf16[448,256]{1,0:T(8,128)(2,1)S(1)}, u32[]{:S(2)}, u32[]{:S(2)}) collective-permute-start(bf16[448,256]{1,0:T(8,128)(2,1)S(1)} %get-tuple-element.30), channel_id=1, source_target_pairs={{0,8},{4,12},{8,0},{12,4},{16,24},{20,28},{24,16},{28,20},{1,9},{5... | collective-permute-start | bytes 688136 | tf_op jit(solution)/shard_map/ppermute | solution.py:162
  21.7 2.7 %shard_map.106 = (f32[448,256]{1,0:T(8,128)S(1)}, bf16[448,256]{1,0:T(8,128)(2,1)S(1)}, bf16[128,512]{1,0:T(8,128)(2,1)S(1)}, bf16[128,512]{1,0:T(8,128)(2,1)S(1)}) custom-call(bf16[128,2048]{1,0:T(8,128)(2,1)S(1)} %bitcast.11, bf16[128,2048]{1,0:T(8,128)(2,1)S(1)} %bitcast.14, bf16[128,2048]{1,0:T(8,128)(2,1)S(1)} %collective-permute-done.refs_2_.refs_1_, ...), custom_call_target="tpu_custom_call" | custom-call | tf_op jit(solution)/shard_map/pallas_call | solution.py:183
  24.8 3.7 %collective-permute-done.8.refs_1_ = bf16[448,256]{1,0:T(8,128)(2,1)S(1)} collective-permute-done((bf16[448,256]{1,0:T(8,128)(2,1)S(1)}, bf16[448,256]{1,0:T(8,128)(2,1)S(1)}, u32[]{:S(2)}, u32[]{:S(2)}) %collective-permute-start.8) | collective-permute-done | bytes 229408 | tf_op jit(solution)/shard_map/ppermute | solution.py:162
  28.5 1.4 %collective-permute-start.19 = (bf16[448,256]{1,0:T(8,128)(2,1)S(1)}, bf16[448,256]{1,0:T(8,128)(2,1)S(1)}, u32[]{:S(2)}, u32[]{:S(2)}) collective-permute-start(bf16[448,256]{1,0:T(8,128)(2,1)S(1)} %shard_map.108.refs_0_.refs_9_), channel_id=1, source_target_pairs={{0,16},{4,20},{8,24},{12,28},{16,0},{20,4},{24,8},{28,12},{1,17},{... | collective-permute-start | bytes 688136 | tf_op jit(solution)/shard_map/ppermute | solution.py:162
  30.1 0.5 collective-permute-start.18
  30.6 2.4 %collective-permute-done.14.refs_1_ = bf16[448,256]{1,0:T(8,128)(2,1)S(1)} collective-permute-done((bf16[448,256]{1,0:T(8,128)(2,1)S(1)}, bf16[448,256]{1,0:T(8,128)(2,1)S(1)}, u32[]{:S(2)}, u32[]{:S(2)}) %collective-permute-start.14) | collective-permute-done | bytes 229408 | tf_op jit(solution)/shard_map/ppermute | solution.py:162
  33.0 1.6 %collective-permute-start.23 = (bf16[448,256]{1,0:T(8,128)(2,1)S(1)}, bf16[448,256]{1,0:T(8,128)(2,1)S(1)}, u32[]{:S(2)}, u32[]{:S(2)}) collective-permute-start(bf16[448,256]{1,0:T(8,128)(2,1)S(1)} %shard_map.109.refs_1_.refs_9_), channel_id=1, source_target_pairs={{0,16},{4,20},{8,24},{12,28},{16,0},{20,4},{24,8},{28,12},{1,17},{... | collective-permute-start | bytes 688136 | tf_op jit(solution)/shard_map/ppermute | solution.py:162
  34.7 0.6 collective-permute-done.19.refs_10_
  35.2 0.9 %shard_map.112 = (f32[512,256]{1,0:T(8,128)S(1)}, bf16[512,256]{1,0:T(8,128)(2,1)S(1)}) custom-call(bf16[128,1024]{1,0:T(8,128)(2,1)S(1)} %get-tuple-element.45.refs_0_, bf16[128,1024]{1,0:T(8,128)(2,1)S(1)} %collective-permute-done.16.refs_1_, bf16[128,1024]{1,0:T(8,128)(2,1)S(1)} %collective-permute-done.9.refs_2_, ...), custom_call_target="tpu_custom_call" | custom-call | tf_op jit(solution)/shard_map/pallas_call | solution.py:183
  36.1 1.6 %collective-permute-start.20 = (bf16[512,256]{1,0:T(8,128)(2,1)S(1)}, bf16[512,256]{1,0:T(8,128)(2,1)S(1)}, u32[]{:S(2)}, u32[]{:S(2)}) collective-permute-start(bf16[512,256]{1,0:T(8,128)(2,1)S(1)} %get-tuple-element.47), channel_id=1, source_target_pairs={{0,1},{1,0},{2,3},{3,2},{4,5},{5,4},{6,7},{7,6},{8,9},{9,8},{10,11... | collective-permute-start | bytes 786440 | tf_op jit(solution)/shard_map/ppermute | solution.py:162
  37.7 2.6 %collective-permute-done.23.refs_10_ = bf16[448,256]{1,0:T(8,128)(2,1)S(1)} collective-permute-done((bf16[448,256]{1,0:T(8,128)(2,1)S(1)}, bf16[448,256]{1,0:T(8,128)(2,1)S(1)}, u32[]{:S(2)}, u32[]{:S(2)}) %collective-permute-start.23) | collective-permute-done | bytes 229408 | tf_op jit(solution)/shard_map/ppermute | solution.py:162
  40.3 0.9 %shard_map.115 = (f32[512,256]{1,0:T(8,128)S(1)}, bf16[512,256]{1,0:T(8,128)(2,1)S(1)}) custom-call(bf16[128,1024]{1,0:T(8,128)(2,1)S(1)} %get-tuple-element.45.refs_0_, bf16[128,1024]{1,0:T(8,128)(2,1)S(1)} %collective-permute-done.16.refs_1_, bf16[128,1024]{1,0:T(8,128)(2,1)S(1)} %collective-permute-done.9.refs_2_, ...), custom_call_target="tpu_custom_call" | custom-call | tf_op jit(solution)/shard_map/pallas_call | solution.py:183
  41.2 1.6 %collective-permute-start.24 = (bf16[512,256]{1,0:T(8,128)(2,1)S(1)}, bf16[512,256]{1,0:T(8,128)(2,1)S(1)}, u32[]{:S(2)}, u32[]{:S(2)}) collective-permute-start(bf16[512,256]{1,0:T(8,128)(2,1)S(1)} %get-tuple-element.51), channel_id=1, source_target_pairs={{0,1},{1,0},{2,3},{3,2},{4,5},{5,4},{6,7},{7,6},{8,9},{9,8},{10,11... | collective-permute-start | bytes 786440 | tf_op jit(solution)/shard_map/ppermute | solution.py:162
  43.0 1.1 %collective-permute-done.20.refs_1_ = bf16[512,256]{1,0:T(8,128)(2,1)S(1)} collective-permute-done((bf16[512,256]{1,0:T(8,128)(2,1)S(1)}, bf16[512,256]{1,0:T(8,128)(2,1)S(1)}, u32[]{:S(2)}, u32[]{:S(2)}) %collective-permute-start.20) | collective-permute-done | bytes 262176 | tf_op jit(solution)/shard_map/ppermute | solution.py:162
  44.1 2.2 %collective-permute-start.21 = (bf16[256,256]{1,0:T(8,128)(2,1)S(1)}, bf16[256,256]{1,0:T(8,128)(2,1)S(1)}, u32[]{:S(2)}, u32[]{:S(2)}) collective-permute-start(bf16[256,256]{1,0:T(8,128)(2,1)S(1)} %shard_map.113.refs_2_), channel_id=1, source_target_pairs={{0,2},{1,3},{2,0},{3,1},{4,6},{5,7},{6,4},{7,5},{8,10},{9,11},{10,... | collective-permute-start | bytes 393224 | tf_op jit(solution)/shard_map/ppermute | solution.py:162
  46.3 5.5 %collective-permute-done.24.refs_1_ = bf16[512,256]{1,0:T(8,128)(2,1)S(1)} collective-permute-done((bf16[512,256]{1,0:T(8,128)(2,1)S(1)}, bf16[512,256]{1,0:T(8,128)(2,1)S(1)}, u32[]{:S(2)}, u32[]{:S(2)}) %collective-permute-start.24) | collective-permute-done | bytes 262176 | tf_op jit(solution)/shard_map/ppermute | solution.py:162
  51.9 1.2 %collective-permute-start.25 = (bf16[256,256]{1,0:T(8,128)(2,1)S(1)}, bf16[256,256]{1,0:T(8,128)(2,1)S(1)}, u32[]{:S(2)}, u32[]{:S(2)}) collective-permute-start(bf16[256,256]{1,0:T(8,128)(2,1)S(1)} %shard_map.116), channel_id=1, source_target_pairs={{0,2},{1,3},{2,0},{3,1},{4,6},{5,7},{6,4},{7,5},{8,10},{9,11},{10,... | collective-permute-start | bytes 393224 | tf_op jit(solution)/shard_map/ppermute | solution.py:162
  53.2 6.1 %collective-permute-done.25.refs_2_ = bf16[256,256]{1,0:T(8,128)(2,1)S(1)} collective-permute-done((bf16[256,256]{1,0:T(8,128)(2,1)S(1)}, bf16[256,256]{1,0:T(8,128)(2,1)S(1)}, u32[]{:S(2)}, u32[]{:S(2)}) %collective-permute-start.25) | collective-permute-done | bytes 131104 | tf_op jit(solution)/shard_map/ppermute | solution.py:162
  59.4 1.0 %shard_map.111 = (bf16[128,2048]{1,0:T(8,128)(2,1)}, bf16[128,512]{1,0:T(8,128)(2,1)}, bf16[128,512]{1,0:T(8,128)(2,1)}) custom-call(bf16[128,512]{1,0:T(8,128)(2,1)S(1)} %get-tuple-element.40.refs_0_, bf16[128,1536]{1,0:T(8,128)(2,1)S(1)} %collective-permute-done.15.refs_1_, bf16[128,512]{1,0:T(8,128)(2,1)S(1)} %get-tuple-element.33.refs_16_.refs_2_, ...), custom_call_target="tpu_custom_call" | custom-call | tf_op jit(solution)/shard_map/pallas_call | solution.py:183
  60.7 0.9 %shard_map.118 = f32[128,1024]{1,0:T(8,128)} custom-call(f32[128,256]{1,0:T(8,128)S(1)} %get-tuple-element.48.refs_0_, f32[128,256]{1,0:T(8,128)S(1)} %collective-permute-done.22.refs_1_, f32[128,256]{1,0:T(8,128)S(1)} %get-tuple-element.52.refs_2_, f32[128,256]{1,0:T(8,128)S(1)} %collective-permute-done.26.refs_3_), custom_call_target="tpu_custom_call" | custom-call | tf_op jit(solution)/shard_map/pallas_call | solution.py:183
  (54 shorter events, 2.3 us)
Async XLA Ops:
  0.6 4.9 %collective-permute-start = (bf16[128,2048]{1,0:T(8,128)(2,1)}, bf16[128,2048]{1,0:T(8,128)(2,1)S(1)}, u32[]{:S(2)}, u32[]{:S(2)}) collective-permute-start(bf16[128,2048]{1,0:T(8,128)(2,1)} %bitcast.9), channel_id=1, source_target_pairs={{0,4},{4,0},{8,12},{12,8},{16,20},{20,16},{24,28},{28,24},{1,5},{5... | collective-permute-start | bytes 1572872 | tf_op jit(solution)/shard_map/ppermute | solution.py:162
  1.1 15.9 %collective-permute-start.1 = (bf16[128,2048]{1,0:T(8,128)(2,1)}, bf16[128,2048]{1,0:T(8,128)(2,1)S(1)}, u32[]{:S(2)}, u32[]{:S(2)}) collective-permute-start(bf16[128,2048]{1,0:T(8,128)(2,1)} %bitcast.12), channel_id=1, source_target_pairs={{0,4},{4,0},{8,12},{12,8},{16,20},{20,16},{24,28},{28,24},{1,5},{5... | collective-permute-start | bytes 1572872 | tf_op jit(solution)/shard_map/ppermute | solution.py:162
  1.2 7.4 %collective-permute-start.3 = (bf16[128,512]{1,0:T(8,128)(2,1)}, bf16[128,512]{1,0:T(8,128)(2,1)S(1)}, u32[]{:S(2)}, u32[]{:S(2)}) collective-permute-start(bf16[128,512]{1,0:T(8,128)(2,1)} %bitcast.15), channel_id=1, source_target_pairs={{0,8},{4,12},{8,0},{12,4},{16,24},{20,28},{24,16},{28,20},{1,9},{5... | collective-permute-start | bytes 393224 | tf_op jit(solution)/shard_map/ppermute | solution.py:162
  4.1 7.3 %collective-permute-start.6 = (bf16[128,512]{1,0:T(8,128)(2,1)}, bf16[128,512]{1,0:T(8,128)(2,1)S(1)}, u32[]{:S(2)}, u32[]{:S(2)}) collective-permute-start(bf16[128,512]{1,0:T(8,128)(2,1)} %bitcast.19), channel_id=1, source_target_pairs={{0,8},{4,12},{8,0},{12,4},{16,24},{20,28},{24,16},{28,20},{1,9},{5... | collective-permute-start | bytes 393224 | tf_op jit(solution)/shard_map/ppermute | solution.py:162
  4.2 7.3 %collective-permute-start.2 = (bf16[128,512]{1,0:T(8,128)(2,1)}, bf16[128,512]{1,0:T(8,128)(2,1)S(1)}, u32[]{:S(2)}, u32[]{:S(2)}) collective-permute-start(bf16[128,512]{1,0:T(8,128)(2,1)} %bitcast.16), channel_id=1, source_target_pairs={{0,4},{4,0},{8,12},{12,8},{16,20},{20,16},{24,28},{28,24},{1,5},{5... | collective-permute-start | bytes 393224 | tf_op jit(solution)/shard_map/ppermute | solution.py:162
  5.6 11.0 %collective-permute-start.9 = (bf16[128,1024]{1,0:T(8,128)(2,1)S(1)}, bf16[128,1024]{1,0:T(8,128)(2,1)S(1)}, u32[]{:S(2)}, u32[]{:S(2)}) collective-permute-start(bf16[128,1024]{1,0:T(8,128)(2,1)S(1)} %shard_map.104), channel_id=1, source_target_pairs={{0,8},{4,12},{8,0},{12,4},{16,24},{20,28},{24,16},{28,20},{1,9},{5... | collective-permute-start | bytes 786440 | tf_op jit(solution)/shard_map/ppermute | solution.py:162
  7.6 9.4 %copy-start.3 = (bf16[1,128,512]{2,1,0:T(8,128)(2,1)S(1)}, bf16[1,128,512]{2,1,0:T(8,128)(2,1)}, u32[]{:S(2)}) copy-start(bf16[1,128,512]{2,1,0:T(8,128)(2,1)} %param.8) | copy-start | bytes 393220
  7.6 9.4 %copy-start.5 = (s32[2]{0:T(128)S(1)}, s32[2]{0:T(128)}, u32[]{:S(2)}) copy-start(s32[2]{0:T(128)} %refs_12_.3) | copy-start | bytes 28
  7.6 9.4 %copy-start.6 = (s32[2]{0:T(128)S(1)}, s32[2]{0:T(128)}, u32[]{:S(2)}) copy-start(s32[2]{0:T(128)} %refs_13_.3) | copy-start | bytes 28
  8.6 7.9 %collective-permute-start.11 = (bf16[128,1024]{1,0:T(8,128)(2,1)S(1)}, bf16[128,1024]{1,0:T(8,128)(2,1)S(1)}, u32[]{:S(2)}, u32[]{:S(2)}) collective-permute-start(bf16[128,1024]{1,0:T(8,128)(2,1)S(1)} %shard_map.105), channel_id=1, source_target_pairs={{0,16},{4,20},{8,24},{12,28},{16,0},{20,4},{24,8},{28,12},{1,17},{... | collective-permute-start | bytes 786440 | tf_op jit(solution)/shard_map/ppermute | solution.py:162
  11.5 1.3 %collective-permute-start.5 = (bf16[128,512]{1,0:T(8,128)(2,1)S(1)}, bf16[128,512]{1,0:T(8,128)(2,1)S(1)}, u32[]{:S(2)}, u32[]{:S(2)}) collective-permute-start(bf16[128,512]{1,0:T(8,128)(2,1)S(1)} %bitcast.20), channel_id=1, source_target_pairs={{0,4},{4,0},{8,12},{12,8},{16,20},{20,16},{24,28},{28,24},{1,5},{5... | collective-permute-start | bytes 393224 | tf_op jit(solution)/shard_map/ppermute | solution.py:162
  11.5 1.5 %collective-permute-start.4 = (bf16[128,512]{1,0:T(8,128)(2,1)S(1)}, bf16[128,512]{1,0:T(8,128)(2,1)S(1)}, u32[]{:S(2)}, u32[]{:S(2)}) collective-permute-start(bf16[128,512]{1,0:T(8,128)(2,1)S(1)} %collective-permute-done.3.refs_6_), channel_id=1, source_target_pairs={{0,4},{4,0},{8,12},{12,8},{16,20},{20,16},{24,28},{28,24},{1,5},{5... | collective-permute-start | bytes 393224 | tf_op jit(solution)/shard_map/ppermute | solution.py:162
  12.8 4.2 %collective-permute-start.7 = (bf16[128,512]{1,0:T(8,128)(2,1)S(1)}, bf16[128,512]{1,0:T(8,128)(2,1)S(1)}, u32[]{:S(2)}, u32[]{:S(2)}) collective-permute-start(bf16[128,512]{1,0:T(8,128)(2,1)S(1)} %collective-permute-done.6.refs_10_), channel_id=1, source_target_pairs={{0,4},{4,0},{8,12},{12,8},{16,20},{20,16},{24,28},{28,24},{1,5},{5... | collective-permute-start | bytes 393224 | tf_op jit(solution)/shard_map/ppermute | solution.py:162
  13.0 4.1 %copy-start.1 = (bf16[1,128,2048]{2,1,0:T(8,128)(2,1)S(1)}, bf16[1,128,2048]{2,1,0:T(8,128)(2,1)}, u32[]{:S(2)}) copy-start(bf16[1,128,2048]{2,1,0:T(8,128)(2,1)} %param.7) | copy-start | bytes 1572868
  13.0 4.1 %copy-start.2 = (bf16[1,128,2048]{2,1,0:T(8,128)(2,1)S(1)}, bf16[1,128,2048]{2,1,0:T(8,128)(2,1)}, u32[]{:S(2)}) copy-start(bf16[1,128,2048]{2,1,0:T(8,128)(2,1)} %param.10) | copy-start | bytes 1572868
  13.0 15.5 %collective-permute-start.13 = (bf16[128,1024]{1,0:T(8,128)(2,1)S(1)}, bf16[128,1024]{1,0:T(8,128)(2,1)S(1)}, u32[]{:S(2)}, u32[]{:S(2)}) collective-permute-start(bf16[128,1024]{1,0:T(8,128)(2,1)S(1)} %shard_map.107), channel_id=1, source_target_pairs={{0,24},{4,28},{8,16},{12,20},{16,8},{20,12},{24,0},{28,4},{1,25},{... | collective-permute-start | bytes 786440 | tf_op jit(solution)/shard_map/ppermute | solution.py:162
  16.5 5.1 %collective-permute-start.10 = (bf16[128,1024]{1,0:T(8,128)(2,1)S(1)}, bf16[128,1024]{1,0:T(8,128)(2,1)S(1)}, u32[]{:S(2)}, u32[]{:S(2)}) collective-permute-start(bf16[128,1024]{1,0:T(8,128)(2,1)S(1)} %collective-permute-done.9.refs_2_), channel_id=1, source_target_pairs={{0,4},{4,0},{8,12},{12,8},{16,20},{20,16},{24,28},{28,24},{1,5},{5... | collective-permute-start | bytes 786440 | tf_op jit(solution)/shard_map/ppermute | solution.py:162
  16.5 5.1 %collective-permute-start.12 = (bf16[128,1024]{1,0:T(8,128)(2,1)S(1)}, bf16[128,1024]{1,0:T(8,128)(2,1)S(1)}, u32[]{:S(2)}, u32[]{:S(2)}) collective-permute-start(bf16[128,1024]{1,0:T(8,128)(2,1)S(1)} %collective-permute-done.11.refs_4_), channel_id=1, source_target_pairs={{0,4},{4,0},{8,12},{12,8},{16,20},{20,16},{24,28},{28,24},{1,5},{5... | collective-permute-start | bytes 786440 | tf_op jit(solution)/shard_map/ppermute | solution.py:162
  19.8 8.6 %collective-permute-start.8 = (bf16[448,256]{1,0:T(8,128)(2,1)S(1)}, bf16[448,256]{1,0:T(8,128)(2,1)S(1)}, u32[]{:S(2)}, u32[]{:S(2)}) collective-permute-start(bf16[448,256]{1,0:T(8,128)(2,1)S(1)} %get-tuple-element.30), channel_id=1, source_target_pairs={{0,8},{4,12},{8,0},{12,4},{16,24},{20,28},{24,16},{28,20},{1,9},{5... | collective-permute-start | bytes 688136 | tf_op jit(solution)/shard_map/ppermute | solution.py:162
  21.7 13.0 %collective-permute-start.16 = (bf16[128,1024]{1,0:T(8,128)(2,1)S(1)}, bf16[128,1024]{1,0:T(8,128)(2,1)S(1)}, u32[]{:S(2)}, u32[]{:S(2)}) collective-permute-start(bf16[128,1024]{1,0:T(8,128)(2,1)S(1)} %get-tuple-element.45.refs_0_), channel_id=1, source_target_pairs={{0,4},{4,0},{8,12},{12,8},{16,20},{20,16},{24,28},{28,24},{1,5},{5... | collective-permute-start | bytes 786440 | tf_op jit(solution)/shard_map/ppermute | solution.py:162
  24.4 8.6 %collective-permute-start.14 = (bf16[448,256]{1,0:T(8,128)(2,1)S(1)}, bf16[448,256]{1,0:T(8,128)(2,1)S(1)}, u32[]{:S(2)}, u32[]{:S(2)}) collective-permute-start(bf16[448,256]{1,0:T(8,128)(2,1)S(1)} %get-tuple-element.37), channel_id=1, source_target_pairs={{0,8},{4,12},{8,0},{12,4},{16,24},{20,28},{24,16},{28,20},{1,9},{5... | collective-permute-start | bytes 688136 | tf_op jit(solution)/shard_map/ppermute | solution.py:162
  28.5 6.7 %collective-permute-start.19 = (bf16[448,256]{1,0:T(8,128)(2,1)S(1)}, bf16[448,256]{1,0:T(8,128)(2,1)S(1)}, u32[]{:S(2)}, u32[]{:S(2)}) collective-permute-start(bf16[448,256]{1,0:T(8,128)(2,1)S(1)} %shard_map.108.refs_0_.refs_9_), channel_id=1, source_target_pairs={{0,16},{4,20},{8,24},{12,28},{16,0},{20,4},{24,8},{28,12},{1,17},{... | collective-permute-start | bytes 688136 | tf_op jit(solution)/shard_map/ppermute | solution.py:162
  30.0 4.7 %collective-permute-start.17 = (bf16[64,1024]{1,0:T(8,128)(2,1)S(1)}, bf16[64,1024]{1,0:T(8,128)(2,1)S(1)}, u32[]{:S(2)}, u32[]{:S(2)}) collective-permute-start(bf16[64,1024]{1,0:T(8,128)(2,1)S(1)} %get-tuple-element.55), channel_id=1, source_target_pairs={{0,4},{4,0},{8,12},{12,8},{16,20},{20,16},{24,28},{28,24},{1,5},{5... | collective-permute-start | bytes 393224 | tf_op jit(solution)/shard_map/ppermute | solution.py:162
  30.1 4.6 %collective-permute-start.18 = (bf16[64,1024]{1,0:T(8,128)(2,1)S(1)}, bf16[64,1024]{1,0:T(8,128)(2,1)S(1)}, u32[]{:S(2)}, u32[]{:S(2)}) collective-permute-start(bf16[64,1024]{1,0:T(8,128)(2,1)S(1)} %get-tuple-element.54), channel_id=1, source_target_pairs={{0,4},{4,0},{8,12},{12,8},{16,20},{20,16},{24,28},{28,24},{1,5},{5... | collective-permute-start | bytes 393224 | tf_op jit(solution)/shard_map/ppermute | solution.py:162
  33.0 7.3 %collective-permute-start.23 = (bf16[448,256]{1,0:T(8,128)(2,1)S(1)}, bf16[448,256]{1,0:T(8,128)(2,1)S(1)}, u32[]{:S(2)}, u32[]{:S(2)}) collective-permute-start(bf16[448,256]{1,0:T(8,128)(2,1)S(1)} %shard_map.109.refs_1_.refs_9_), channel_id=1, source_target_pairs={{0,16},{4,20},{8,24},{12,28},{16,0},{20,4},{24,8},{28,12},{1,17},{... | collective-permute-start | bytes 688136 | tf_op jit(solution)/shard_map/ppermute | solution.py:162
  36.1 8.0 %collective-permute-start.20 = (bf16[512,256]{1,0:T(8,128)(2,1)S(1)}, bf16[512,256]{1,0:T(8,128)(2,1)S(1)}, u32[]{:S(2)}, u32[]{:S(2)}) collective-permute-start(bf16[512,256]{1,0:T(8,128)(2,1)S(1)} %get-tuple-element.47), channel_id=1, source_target_pairs={{0,1},{1,0},{2,3},{3,2},{4,5},{5,4},{6,7},{7,6},{8,9},{9,8},{10,11... | collective-permute-start | bytes 786440 | tf_op jit(solution)/shard_map/ppermute | solution.py:162
  41.2 10.7 %collective-permute-start.24 = (bf16[512,256]{1,0:T(8,128)(2,1)S(1)}, bf16[512,256]{1,0:T(8,128)(2,1)S(1)}, u32[]{:S(2)}, u32[]{:S(2)}) collective-permute-start(bf16[512,256]{1,0:T(8,128)(2,1)S(1)} %get-tuple-element.51), channel_id=1, source_target_pairs={{0,1},{1,0},{2,3},{3,2},{4,5},{5,4},{6,7},{7,6},{8,9},{9,8},{10,11... | collective-permute-start | bytes 786440 | tf_op jit(solution)/shard_map/ppermute | solution.py:162
  42.9 16.5 %collective-permute-start.15 = (bf16[128,1536]{1,0:T(8,128)(2,1)S(1)}, bf16[128,1536]{1,0:T(8,128)(2,1)S(1)}, u32[]{:S(2)}, u32[]{:S(2)}) collective-permute-start(bf16[128,1536]{1,0:T(8,128)(2,1)S(1)} %get-tuple-element.41), channel_id=1, source_target_pairs={{0,4},{4,0},{8,12},{12,8},{16,20},{20,16},{24,28},{28,24},{1,5},{5... | collective-permute-start | bytes 1179656 | tf_op jit(solution)/shard_map/ppermute | solution.py:162
  44.1 8.9 %collective-permute-start.21 = (bf16[256,256]{1,0:T(8,128)(2,1)S(1)}, bf16[256,256]{1,0:T(8,128)(2,1)S(1)}, u32[]{:S(2)}, u32[]{:S(2)}) collective-permute-start(bf16[256,256]{1,0:T(8,128)(2,1)S(1)} %shard_map.113.refs_2_), channel_id=1, source_target_pairs={{0,2},{1,3},{2,0},{3,1},{4,6},{5,7},{6,4},{7,5},{8,10},{9,11},{10,... | collective-permute-start | bytes 393224 | tf_op jit(solution)/shard_map/ppermute | solution.py:162
  51.9 7.4 %collective-permute-start.25 = (bf16[256,256]{1,0:T(8,128)(2,1)S(1)}, bf16[256,256]{1,0:T(8,128)(2,1)S(1)}, u32[]{:S(2)}, u32[]{:S(2)}) collective-permute-start(bf16[256,256]{1,0:T(8,128)(2,1)S(1)} %shard_map.116), channel_id=1, source_target_pairs={{0,2},{1,3},{2,0},{3,1},{4,6},{5,7},{6,4},{7,5},{8,10},{9,11},{10,... | collective-permute-start | bytes 393224 | tf_op jit(solution)/shard_map/ppermute | solution.py:162
  53.1 7.2 %collective-permute-start.22 = (f32[128,256]{1,0:T(8,128)S(1)}, f32[128,256]{1,0:T(8,128)S(1)}, u32[]{:S(2)}, u32[]{:S(2)}) collective-permute-start(f32[128,256]{1,0:T(8,128)S(1)} %get-tuple-element.49), channel_id=1, source_target_pairs={{0,4},{4,0},{8,12},{12,8},{16,20},{20,16},{24,28},{28,24},{1,5},{5... | collective-permute-start | bytes 393224 | tf_op jit(solution)/shard_map/ppermute | solution.py:162
  59.3 1.4 %collective-permute-start.26 = (f32[128,256]{1,0:T(8,128)S(1)}, f32[128,256]{1,0:T(8,128)S(1)}, u32[]{:S(2)}, u32[]{:S(2)}) collective-permute-start(f32[128,256]{1,0:T(8,128)S(1)} %get-tuple-element.53), channel_id=1, source_target_pairs={{0,4},{4,0},{8,12},{12,8},{16,20},{20,16},{24,28},{28,24},{1,5},{5... | collective-permute-start | bytes 393224 | tf_op jit(solution)/shard_map/ppermute | solution.py:162
  (2 other events, 5.1 us)

commit v4 on v3

--- a/solution.py
+++ b/solution.py
@@ -295,7 +295,7 @@
             scores = dot(key, query_rows, ((1,), (1,)))
             scores = jnp.where(key_pos < limit, scores, -jnp.inf)
             row_max = jnp.max(scores, axis=0, keepdims=True)
-            exponent = jnp.exp((scores - row_max) * score_scale)
+            exponent = jnp.exp2((scores - row_max) * (score_scale * math.log2(math.e)))
             probability = exponent * (1.0 / jnp.sum(exponent, axis=0, keepdims=True))
             dprob = dot(value, grad_rows, ((1,), (1,)))
             row_delta = jnp.sum(probability * dprob, axis=0, keepdims=True)
@@ -364,7 +364,7 @@
         )
         query_parts.append((query_mine, query_other))
         if head:
-            (grad,) = call(add_parts, [((seen, 2 * HEAD_DIM), BF16)], (*sums[0], query_mine, hidden_core[3]), held=2)
+            (grad,) = call(add_parts, [((seen, 2 * HEAD_DIM), BF16)], (*sums[0], query_mine), held=1, flops=0)
             sums[0] = (grad, swap(grad, "seq", 4))
         sums.append((part, swap(part_low, "seq", 2)))
     halves = [swap(half, "seq", 1) for half in (hidden_core[3][: tokens // 2], hidden_core[3][tokens // 2 :])]

time: 61.7 us -> 61.6 us (level)
  no operation moved by 1% of the time
where the time goes in v4:
time: 61.6 us; the launch traced here: 61.5 us
  waiting for transfers between devices  25.7 us (42%)
  starting transfers between devices  24.4 us (40%)
  Pallas kernels  9.3 us (15%)
  local copies, waits for them, and re-layouts  1.26 us (2%)
  between operations  0.84 us (1%)
    ppermute x27, waiting for transfers between devices, swap(): return lax.ppermute(array, axis, [(i, i ^ bit) for i in range(size)])  25.7 us
    ppermute x27, starting transfers between devices, swap(): return lax.ppermute(array, axis, [(i, i ^ bit) for i in range(size)])  24.4 us
    pallas_call x14, Pallas kernels, call(): pl.pallas_call(run, out_shape=shapes, in_specs=specs, out_specs=[pl.Block...  9.3 us
    unnamed x14, local copies, waits for them, and re-layouts  1.25 us
  transfers between devices with their start and end apart: 27, of which 12 were waited for; matrix products, arithmetic and copies ran while one was open for 0% of the time, Pallas kernels for 14%

profile of v4, /device:TPU:0, one launch (start us, length us, event | category | flops | bytes accessed | tf_op | source)
XLA Modules:
  0.0 61.5 jit_solution(6403113450476136250)
XLA Ops:
  0.6 0.5 collective-permute-start
  1.2 2.9 %collective-permute-start.3 = (bf16[128,512]{1,0:T(8,128)(2,1)}, bf16[128,512]{1,0:T(8,128)(2,1)S(1)}, u32[]{:S(2)}, u32[]{:S(2)}) collective-permute-start(bf16[128,512]{1,0:T(8,128)(2,1)} %bitcast.15), channel_id=1, source_target_pairs={{0,8},{4,12},{8,0},{12,4},{16,24},{20,28},{24,16},{28,20},{1,9},{5... | collective-permute-start | bytes 393224 | tf_op jit(solution)/shard_map/ppermute | solution.py:162
  4.2 1.2 %copy-done = bf16[1,128,4096]{2,1,0:T(8,128)(2,1)S(1)} copy-done((bf16[1,128,4096]{2,1,0:T(8,128)(2,1)S(1)}, bf16[1,128,4096]{2,1,0:T(8,128)(2,1)}, u32[]{:S(2)}) %copy-start) | copy-done | bytes 1048600
  5.6 2.1 %collective-permute-start.9 = (bf16[128,1024]{1,0:T(8,128)(2,1)S(1)}, bf16[128,1024]{1,0:T(8,128)(2,1)S(1)}, u32[]{:S(2)}, u32[]{:S(2)}) collective-permute-start(bf16[128,1024]{1,0:T(8,128)(2,1)S(1)} %shard_map.104), channel_id=1, source_target_pairs={{0,8},{4,12},{8,0},{12,4},{16,24},{20,28},{24,16},{28,20},{1,9},{5... | collective-permute-start | bytes 786440 | tf_op jit(solution)/shard_map/ppermute | solution.py:162
  7.6 1.0 %collective-permute-done.3.refs_6_ = bf16[128,512]{1,0:T(8,128)(2,1)S(1)} collective-permute-done((bf16[128,512]{1,0:T(8,128)(2,1)}, bf16[128,512]{1,0:T(8,128)(2,1)S(1)}, u32[]{:S(2)}, u32[]{:S(2)}) %collective-permute-start.3) | collective-permute-done | bytes 131104 | tf_op jit(solution)/shard_map/ppermute | solution.py:162
  8.6 2.1 %collective-permute-start.11 = (bf16[128,1024]{1,0:T(8,128)(2,1)S(1)}, bf16[128,1024]{1,0:T(8,128)(2,1)S(1)}, u32[]{:S(2)}, u32[]{:S(2)}) collective-permute-start(bf16[128,1024]{1,0:T(8,128)(2,1)S(1)} %shard_map.105), channel_id=1, source_target_pairs={{0,16},{4,20},{8,24},{12,28},{16,0},{20,4},{24,8},{28,12},{1,17},{... | collective-permute-start | bytes 786440 | tf_op jit(solution)/shard_map/ppermute | solution.py:162
  10.7 0.7 %collective-permute-done.6.refs_10_ = bf16[128,512]{1,0:T(8,128)(2,1)S(1)} collective-permute-done((bf16[128,512]{1,0:T(8,128)(2,1)}, bf16[128,512]{1,0:T(8,128)(2,1)S(1)}, u32[]{:S(2)}, u32[]{:S(2)}) %collective-permute-start.6) | collective-permute-done | bytes 131104 | tf_op jit(solution)/shard_map/ppermute | solution.py:162
  11.5 0.5 collective-permute-start.4
  12.0 0.8 %collective-permute-done.5.refs_9_ = bf16[128,512]{1,0:T(8,128)(2,1)S(1)} collective-permute-done((bf16[128,512]{1,0:T(8,128)(2,1)S(1)}, bf16[128,512]{1,0:T(8,128)(2,1)S(1)}, u32[]{:S(2)}, u32[]{:S(2)}) %collective-permute-start.5) | collective-permute-done | bytes 131104 | tf_op jit(solution)/shard_map/ppermute | solution.py:162
  13.0 3.1 %collective-permute-start.16 = (bf16[128,1024]{1,0:T(8,128)(2,1)S(1)}, bf16[128,1024]{1,0:T(8,128)(2,1)S(1)}, u32[]{:S(2)}, u32[]{:S(2)}) collective-permute-start(bf16[128,1024]{1,0:T(8,128)(2,1)S(1)} %shard_map.111), channel_id=1, source_target_pairs={{0,24},{4,28},{8,16},{12,20},{16,8},{20,12},{24,0},{28,4},{1,25},{... | collective-permute-start | bytes 786440 | tf_op jit(solution)/shard_map/ppermute | solution.py:162
  16.5 0.5 collective-permute-start.12
  17.1 2.7 %shard_map.102 = (f32[448,256]{1,0:T(8,128)S(1)}, bf16[448,256]{1,0:T(8,128)(2,1)S(1)}, bf16[128,512]{1,0:T(8,128)(2,1)S(1)}, bf16[128,512]{1,0:T(8,128)(2,1)S(1)}) custom-call(bf16[128,2048]{1,0:T(8,128)(2,1)S(1)} %bitcast.10, bf16[128,2048]{1,0:T(8,128)(2,1)S(1)} %bitcast.13, bf16[128,2048]{1,0:T(8,128)(2,1)S(1)} %collective-permute-done.refs_2_.refs_1_, ...), custom_call_target="tpu_custom_call" | custom-call | flops 1174405120 | tf_op jit(solution)/shard_map/pallas_call | solution.py:183
  19.8 1.8 %collective-permute-start.8 = (bf16[448,256]{1,0:T(8,128)(2,1)S(1)}, bf16[448,256]{1,0:T(8,128)(2,1)S(1)}, u32[]{:S(2)}, u32[]{:S(2)}) collective-permute-start(bf16[448,256]{1,0:T(8,128)(2,1)S(1)} %get-tuple-element.30), channel_id=1, source_target_pairs={{0,8},{4,12},{8,0},{12,4},{16,24},{20,28},{24,16},{28,20},{1,9},{5... | collective-permute-start | bytes 688136 | tf_op jit(solution)/shard_map/ppermute | solution.py:162
  21.6 2.7 %shard_map.106 = (f32[448,256]{1,0:T(8,128)S(1)}, bf16[448,256]{1,0:T(8,128)(2,1)S(1)}, bf16[128,512]{1,0:T(8,128)(2,1)S(1)}, bf16[128,512]{1,0:T(8,128)(2,1)S(1)}) custom-call(bf16[128,2048]{1,0:T(8,128)(2,1)S(1)} %bitcast.11, bf16[128,2048]{1,0:T(8,128)(2,1)S(1)} %bitcast.14, bf16[128,2048]{1,0:T(8,128)(2,1)S(1)} %collective-permute-done.refs_2_.refs_1_, ...), custom_call_target="tpu_custom_call" | custom-call | tf_op jit(solution)/shard_map/pallas_call | solution.py:183
  24.6 4.0 %collective-permute-done.8.refs_1_ = bf16[448,256]{1,0:T(8,128)(2,1)S(1)} collective-permute-done((bf16[448,256]{1,0:T(8,128)(2,1)S(1)}, bf16[448,256]{1,0:T(8,128)(2,1)S(1)}, u32[]{:S(2)}, u32[]{:S(2)}) %collective-permute-start.8) | collective-permute-done | bytes 229408 | tf_op jit(solution)/shard_map/ppermute | solution.py:162
  28.7 1.3 %collective-permute-start.19 = (bf16[448,256]{1,0:T(8,128)(2,1)S(1)}, bf16[448,256]{1,0:T(8,128)(2,1)S(1)}, u32[]{:S(2)}, u32[]{:S(2)}) collective-permute-start(bf16[448,256]{1,0:T(8,128)(2,1)S(1)} %shard_map.107.refs_0_.refs_9_), channel_id=1, source_target_pairs={{0,16},{4,20},{8,24},{12,28},{16,0},{20,4},{24,8},{28,12},{1,17},{... | collective-permute-start | bytes 688136 | tf_op jit(solution)/shard_map/ppermute | solution.py:162
  30.0 0.5 collective-permute-start.18
  30.5 2.4 %collective-permute-done.13.refs_1_ = bf16[448,256]{1,0:T(8,128)(2,1)S(1)} collective-permute-done((bf16[448,256]{1,0:T(8,128)(2,1)S(1)}, bf16[448,256]{1,0:T(8,128)(2,1)S(1)}, u32[]{:S(2)}, u32[]{:S(2)}) %collective-permute-start.13) | collective-permute-done | bytes 229408 | tf_op jit(solution)/shard_map/ppermute | solution.py:162
  33.0 1.5 %collective-permute-start.23 = (bf16[448,256]{1,0:T(8,128)(2,1)S(1)}, bf16[448,256]{1,0:T(8,128)(2,1)S(1)}, u32[]{:S(2)}, u32[]{:S(2)}) collective-permute-start(bf16[448,256]{1,0:T(8,128)(2,1)S(1)} %shard_map.108.refs_1_.refs_9_), channel_id=1, source_target_pairs={{0,16},{4,20},{8,24},{12,28},{16,0},{20,4},{24,8},{28,12},{1,17},{... | collective-permute-start | bytes 688136 | tf_op jit(solution)/shard_map/ppermute | solution.py:162
  34.6 0.6 %collective-permute-done.19.refs_10_ = bf16[448,256]{1,0:T(8,128)(2,1)S(1)} collective-permute-done((bf16[448,256]{1,0:T(8,128)(2,1)S(1)}, bf16[448,256]{1,0:T(8,128)(2,1)S(1)}, u32[]{:S(2)}, u32[]{:S(2)}) %collective-permute-start.19) | collective-permute-done | bytes 229408 | tf_op jit(solution)/shard_map/ppermute | solution.py:162
  35.2 0.9 %shard_map.112 = (f32[512,256]{1,0:T(8,128)S(1)}, bf16[512,256]{1,0:T(8,128)(2,1)S(1)}) custom-call(bf16[128,1024]{1,0:T(8,128)(2,1)S(1)} %get-tuple-element.44.refs_0_, bf16[128,1024]{1,0:T(8,128)(2,1)S(1)} %collective-permute-done.15.refs_1_, bf16[128,1024]{1,0:T(8,128)(2,1)S(1)} %collective-permute-done.9.refs_2_, ...), custom_call_target="tpu_custom_call" | custom-call | tf_op jit(solution)/shard_map/pallas_call | solution.py:183
  36.1 1.7 %collective-permute-start.20 = (bf16[512,256]{1,0:T(8,128)(2,1)S(1)}, bf16[512,256]{1,0:T(8,128)(2,1)S(1)}, u32[]{:S(2)}, u32[]{:S(2)}) collective-permute-start(bf16[512,256]{1,0:T(8,128)(2,1)S(1)} %get-tuple-element.47), channel_id=1, source_target_pairs={{0,1},{1,0},{2,3},{3,2},{4,5},{5,4},{6,7},{7,6},{8,9},{9,8},{10,11... | collective-permute-start | bytes 786440 | tf_op jit(solution)/shard_map/ppermute | solution.py:162
  37.8 2.4 %collective-permute-done.23.refs_10_ = bf16[448,256]{1,0:T(8,128)(2,1)S(1)} collective-permute-done((bf16[448,256]{1,0:T(8,128)(2,1)S(1)}, bf16[448,256]{1,0:T(8,128)(2,1)S(1)}, u32[]{:S(2)}, u32[]{:S(2)}) %collective-permute-start.23) | collective-permute-done | bytes 229408 | tf_op jit(solution)/shard_map/ppermute | solution.py:162
  40.1 0.9 %shard_map.115 = (f32[512,256]{1,0:T(8,128)S(1)}, bf16[512,256]{1,0:T(8,128)(2,1)S(1)}) custom-call(bf16[128,1024]{1,0:T(8,128)(2,1)S(1)} %get-tuple-element.44.refs_0_, bf16[128,1024]{1,0:T(8,128)(2,1)S(1)} %collective-permute-done.15.refs_1_, bf16[128,1024]{1,0:T(8,128)(2,1)S(1)} %collective-permute-done.9.refs_2_, ...), custom_call_target="tpu_custom_call" | custom-call | tf_op jit(solution)/shard_map/pallas_call | solution.py:183
  41.0 1.7 %collective-permute-start.24 = (bf16[512,256]{1,0:T(8,128)(2,1)S(1)}, bf16[512,256]{1,0:T(8,128)(2,1)S(1)}, u32[]{:S(2)}, u32[]{:S(2)}) collective-permute-start(bf16[512,256]{1,0:T(8,128)(2,1)S(1)} %get-tuple-element.51), channel_id=1, source_target_pairs={{0,1},{1,0},{2,3},{3,2},{4,5},{5,4},{6,7},{7,6},{8,9},{9,8},{10,11... | collective-permute-start | bytes 786440 | tf_op jit(solution)/shard_map/ppermute | solution.py:162
  42.8 1.3 %collective-permute-done.20.refs_1_ = bf16[512,256]{1,0:T(8,128)(2,1)S(1)} collective-permute-done((bf16[512,256]{1,0:T(8,128)(2,1)S(1)}, bf16[512,256]{1,0:T(8,128)(2,1)S(1)}, u32[]{:S(2)}, u32[]{:S(2)}) %collective-permute-start.20) | collective-permute-done | bytes 262176 | tf_op jit(solution)/shard_map/ppermute | solution.py:162
  44.2 2.2 %collective-permute-start.21 = (bf16[256,256]{1,0:T(8,128)(2,1)S(1)}, bf16[256,256]{1,0:T(8,128)(2,1)S(1)}, u32[]{:S(2)}, u32[]{:S(2)}) collective-permute-start(bf16[256,256]{1,0:T(8,128)(2,1)S(1)} %shard_map.113.refs_2_), channel_id=1, source_target_pairs={{0,2},{1,3},{2,0},{3,1},{4,6},{5,7},{6,4},{7,5},{8,10},{9,11},{10,... | collective-permute-start | bytes 393224 | tf_op jit(solution)/shard_map/ppermute | solution.py:162
  46.4 5.3 %collective-permute-done.24.refs_1_ = bf16[512,256]{1,0:T(8,128)(2,1)S(1)} collective-permute-done((bf16[512,256]{1,0:T(8,128)(2,1)S(1)}, bf16[512,256]{1,0:T(8,128)(2,1)S(1)}, u32[]{:S(2)}, u32[]{:S(2)}) %collective-permute-start.24) | collective-permute-done | bytes 262176 | tf_op jit(solution)/shard_map/ppermute | solution.py:162
  51.7 1.1 %collective-permute-start.25 = (bf16[256,256]{1,0:T(8,128)(2,1)S(1)}, bf16[256,256]{1,0:T(8,128)(2,1)S(1)}, u32[]{:S(2)}, u32[]{:S(2)}) collective-permute-start(bf16[256,256]{1,0:T(8,128)(2,1)S(1)} %shard_map.116), channel_id=1, source_target_pairs={{0,2},{1,3},{2,0},{3,1},{4,6},{5,7},{6,4},{7,5},{8,10},{9,11},{10,... | collective-permute-start | bytes 393224 | tf_op jit(solution)/shard_map/ppermute | solution.py:162
  53.0 6.2 %collective-permute-done.25.refs_2_ = bf16[256,256]{1,0:T(8,128)(2,1)S(1)} collective-permute-done((bf16[256,256]{1,0:T(8,128)(2,1)S(1)}, bf16[256,256]{1,0:T(8,128)(2,1)S(1)}, u32[]{:S(2)}, u32[]{:S(2)}) %collective-permute-start.25) | collective-permute-done | bytes 131104 | tf_op jit(solution)/shard_map/ppermute | solution.py:162
  59.3 1.0 %shard_map.110 = (bf16[128,2048]{1,0:T(8,128)(2,1)}, bf16[128,512]{1,0:T(8,128)(2,1)}, bf16[128,512]{1,0:T(8,128)(2,1)}) custom-call(bf16[128,512]{1,0:T(8,128)(2,1)S(1)} %get-tuple-element.39.refs_0_, bf16[128,1536]{1,0:T(8,128)(2,1)S(1)} %collective-permute-done.14.refs_1_, bf16[128,512]{1,0:T(8,128)(2,1)S(1)} %get-tuple-element.33.refs_16_.refs_2_, ...), custom_call_target="tpu_custom_call" | custom-call | tf_op jit(solution)/shard_map/pallas_call | solution.py:183
  60.6 0.9 %shard_map.118 = f32[128,1024]{1,0:T(8,128)} custom-call(f32[128,256]{1,0:T(8,128)S(1)} %get-tuple-element.48.refs_0_, f32[128,256]{1,0:T(8,128)S(1)} %collective-permute-done.22.refs_1_, f32[128,256]{1,0:T(8,128)S(1)} %get-tuple-element.52.refs_2_, f32[128,256]{1,0:T(8,128)S(1)} %collective-permute-done.26.refs_3_), custom_call_target="tpu_custom_call" | custom-call | tf_op jit(solution)/shard_map/pallas_call | solution.py:183
  (54 shorter events, 2.2 us)
Async XLA Ops:
  0.6 4.9 %collective-permute-start = (bf16[128,2048]{1,0:T(8,128)(2,1)}, bf16[128,2048]{1,0:T(8,128)(2,1)S(1)}, u32[]{:S(2)}, u32[]{:S(2)}) collective-permute-start(bf16[128,2048]{1,0:T(8,128)(2,1)} %bitcast.9), channel_id=1, source_target_pairs={{0,4},{4,0},{8,12},{12,8},{16,20},{20,16},{24,28},{28,24},{1,5},{5... | collective-permute-start | bytes 1572872 | tf_op jit(solution)/shard_map/ppermute | solution.py:162
  1.1 15.9 %collective-permute-start.1 = (bf16[128,2048]{1,0:T(8,128)(2,1)}, bf16[128,2048]{1,0:T(8,128)(2,1)S(1)}, u32[]{:S(2)}, u32[]{:S(2)}) collective-permute-start(bf16[128,2048]{1,0:T(8,128)(2,1)} %bitcast.12), channel_id=1, source_target_pairs={{0,4},{4,0},{8,12},{12,8},{16,20},{20,16},{24,28},{28,24},{1,5},{5... | collective-permute-start | bytes 1572872 | tf_op jit(solution)/shard_map/ppermute | solution.py:162
  1.2 7.4 %collective-permute-start.3 = (bf16[128,512]{1,0:T(8,128)(2,1)}, bf16[128,512]{1,0:T(8,128)(2,1)S(1)}, u32[]{:S(2)}, u32[]{:S(2)}) collective-permute-start(bf16[128,512]{1,0:T(8,128)(2,1)} %bitcast.15), channel_id=1, source_target_pairs={{0,8},{4,12},{8,0},{12,4},{16,24},{20,28},{24,16},{28,20},{1,9},{5... | collective-permute-start | bytes 393224 | tf_op jit(solution)/shard_map/ppermute | solution.py:162
  4.1 7.3 %collective-permute-start.6 = (bf16[128,512]{1,0:T(8,128)(2,1)}, bf16[128,512]{1,0:T(8,128)(2,1)S(1)}, u32[]{:S(2)}, u32[]{:S(2)}) collective-permute-start(bf16[128,512]{1,0:T(8,128)(2,1)} %bitcast.19), channel_id=1, source_target_pairs={{0,8},{4,12},{8,0},{12,4},{16,24},{20,28},{24,16},{28,20},{1,9},{5... | collective-permute-start | bytes 393224 | tf_op jit(solution)/shard_map/ppermute | solution.py:162
  4.2 7.3 %collective-permute-start.2 = (bf16[128,512]{1,0:T(8,128)(2,1)}, bf16[128,512]{1,0:T(8,128)(2,1)S(1)}, u32[]{:S(2)}, u32[]{:S(2)}) collective-permute-start(bf16[128,512]{1,0:T(8,128)(2,1)} %bitcast.16), channel_id=1, source_target_pairs={{0,4},{4,0},{8,12},{12,8},{16,20},{20,16},{24,28},{28,24},{1,5},{5... | collective-permute-start | bytes 393224 | tf_op jit(solution)/shard_map/ppermute | solution.py:162
  5.6 11.0 %collective-permute-start.9 = (bf16[128,1024]{1,0:T(8,128)(2,1)S(1)}, bf16[128,1024]{1,0:T(8,128)(2,1)S(1)}, u32[]{:S(2)}, u32[]{:S(2)}) collective-permute-start(bf16[128,1024]{1,0:T(8,128)(2,1)S(1)} %shard_map.104), channel_id=1, source_target_pairs={{0,8},{4,12},{8,0},{12,4},{16,24},{20,28},{24,16},{28,20},{1,9},{5... | collective-permute-start | bytes 786440 | tf_op jit(solution)/shard_map/ppermute | solution.py:162
  7.6 9.4 %copy-start.3 = (bf16[1,128,512]{2,1,0:T(8,128)(2,1)S(1)}, bf16[1,128,512]{2,1,0:T(8,128)(2,1)}, u32[]{:S(2)}) copy-start(bf16[1,128,512]{2,1,0:T(8,128)(2,1)} %param.8) | copy-start | bytes 393220
  7.6 9.4 %copy-start.5 = (s32[2]{0:T(128)S(1)}, s32[2]{0:T(128)}, u32[]{:S(2)}) copy-start(s32[2]{0:T(128)} %refs_12_.3) | copy-start | bytes 28
  7.6 9.4 %copy-start.6 = (s32[2]{0:T(128)S(1)}, s32[2]{0:T(128)}, u32[]{:S(2)}) copy-start(s32[2]{0:T(128)} %refs_13_.3) | copy-start | bytes 28
  8.6 7.9 %collective-permute-start.11 = (bf16[128,1024]{1,0:T(8,128)(2,1)S(1)}, bf16[128,1024]{1,0:T(8,128)(2,1)S(1)}, u32[]{:S(2)}, u32[]{:S(2)}) collective-permute-start(bf16[128,1024]{1,0:T(8,128)(2,1)S(1)} %shard_map.105), channel_id=1, source_target_pairs={{0,16},{4,20},{8,24},{12,28},{16,0},{20,4},{24,8},{28,12},{1,17},{... | collective-permute-start | bytes 786440 | tf_op jit(solution)/shard_map/ppermute | solution.py:162
  11.5 1.3 %collective-permute-start.5 = (bf16[128,512]{1,0:T(8,128)(2,1)S(1)}, bf16[128,512]{1,0:T(8,128)(2,1)S(1)}, u32[]{:S(2)}, u32[]{:S(2)}) collective-permute-start(bf16[128,512]{1,0:T(8,128)(2,1)S(1)} %bitcast.20), channel_id=1, source_target_pairs={{0,4},{4,0},{8,12},{12,8},{16,20},{20,16},{24,28},{28,24},{1,5},{5... | collective-permute-start | bytes 393224 | tf_op jit(solution)/shard_map/ppermute | solution.py:162
  11.5 1.5 %collective-permute-start.4 = (bf16[128,512]{1,0:T(8,128)(2,1)S(1)}, bf16[128,512]{1,0:T(8,128)(2,1)S(1)}, u32[]{:S(2)}, u32[]{:S(2)}) collective-permute-start(bf16[128,512]{1,0:T(8,128)(2,1)S(1)} %collective-permute-done.3.refs_6_), channel_id=1, source_target_pairs={{0,4},{4,0},{8,12},{12,8},{16,20},{20,16},{24,28},{28,24},{1,5},{5... | collective-permute-start | bytes 393224 | tf_op jit(solution)/shard_map/ppermute | solution.py:162
  12.8 4.2 %collective-permute-start.7 = (bf16[128,512]{1,0:T(8,128)(2,1)S(1)}, bf16[128,512]{1,0:T(8,128)(2,1)S(1)}, u32[]{:S(2)}, u32[]{:S(2)}) collective-permute-start(bf16[128,512]{1,0:T(8,128)(2,1)S(1)} %collective-permute-done.6.refs_10_), channel_id=1, source_target_pairs={{0,4},{4,0},{8,12},{12,8},{16,20},{20,16},{24,28},{28,24},{1,5},{5... | collective-permute-start | bytes 393224 | tf_op jit(solution)/shard_map/ppermute | solution.py:162
  13.0 4.1 %copy-start.1 = (bf16[1,128,2048]{2,1,0:T(8,128)(2,1)S(1)}, bf16[1,128,2048]{2,1,0:T(8,128)(2,1)}, u32[]{:S(2)}) copy-start(bf16[1,128,2048]{2,1,0:T(8,128)(2,1)} %param.7) | copy-start | bytes 1572868
  13.0 4.1 %copy-start.2 = (bf16[1,128,2048]{2,1,0:T(8,128)(2,1)S(1)}, bf16[1,128,2048]{2,1,0:T(8,128)(2,1)}, u32[]{:S(2)}) copy-start(bf16[1,128,2048]{2,1,0:T(8,128)(2,1)} %param.10) | copy-start | bytes 1572868
  13.0 16.9 %collective-permute-start.16 = (bf16[128,1024]{1,0:T(8,128)(2,1)S(1)}, bf16[128,1024]{1,0:T(8,128)(2,1)S(1)}, u32[]{:S(2)}, u32[]{:S(2)}) collective-permute-start(bf16[128,1024]{1,0:T(8,128)(2,1)S(1)} %shard_map.111), channel_id=1, source_target_pairs={{0,24},{4,28},{8,16},{12,20},{16,8},{20,12},{24,0},{28,4},{1,25},{... | collective-permute-start | bytes 786440 | tf_op jit(solution)/shard_map/ppermute | solution.py:162
  16.5 5.1 %collective-permute-start.10 = (bf16[128,1024]{1,0:T(8,128)(2,1)S(1)}, bf16[128,1024]{1,0:T(8,128)(2,1)S(1)}, u32[]{:S(2)}, u32[]{:S(2)}) collective-permute-start(bf16[128,1024]{1,0:T(8,128)(2,1)S(1)} %collective-permute-done.9.refs_2_), channel_id=1, source_target_pairs={{0,4},{4,0},{8,12},{12,8},{16,20},{20,16},{24,28},{28,24},{1,5},{5... | collective-permute-start | bytes 786440 | tf_op jit(solution)/shard_map/ppermute | solution.py:162
  16.5 5.1 %collective-permute-start.12 = (bf16[128,1024]{1,0:T(8,128)(2,1)S(1)}, bf16[128,1024]{1,0:T(8,128)(2,1)S(1)}, u32[]{:S(2)}, u32[]{:S(2)}) collective-permute-start(bf16[128,1024]{1,0:T(8,128)(2,1)S(1)} %collective-permute-done.11.refs_4_), channel_id=1, source_target_pairs={{0,4},{4,0},{8,12},{12,8},{16,20},{20,16},{24,28},{28,24},{1,5},{5... | collective-permute-start | bytes 786440 | tf_op jit(solution)/shard_map/ppermute | solution.py:162
  19.8 8.8 %collective-permute-start.8 = (bf16[448,256]{1,0:T(8,128)(2,1)S(1)}, bf16[448,256]{1,0:T(8,128)(2,1)S(1)}, u32[]{:S(2)}, u32[]{:S(2)}) collective-permute-start(bf16[448,256]{1,0:T(8,128)(2,1)S(1)} %get-tuple-element.30), channel_id=1, source_target_pairs={{0,8},{4,12},{8,0},{12,4},{16,24},{20,28},{24,16},{28,20},{1,9},{5... | collective-permute-start | bytes 688136 | tf_op jit(solution)/shard_map/ppermute | solution.py:162
  21.6 13.0 %collective-permute-start.15 = (bf16[128,1024]{1,0:T(8,128)(2,1)S(1)}, bf16[128,1024]{1,0:T(8,128)(2,1)S(1)}, u32[]{:S(2)}, u32[]{:S(2)}) collective-permute-start(bf16[128,1024]{1,0:T(8,128)(2,1)S(1)} %get-tuple-element.44.refs_0_), channel_id=1, source_target_pairs={{0,4},{4,0},{8,12},{12,8},{16,20},{20,16},{24,28},{28,24},{1,5},{5... | collective-permute-start | bytes 786440 | tf_op jit(solution)/shard_map/ppermute | solution.py:162
  24.3 8.7 %collective-permute-start.13 = (bf16[448,256]{1,0:T(8,128)(2,1)S(1)}, bf16[448,256]{1,0:T(8,128)(2,1)S(1)}, u32[]{:S(2)}, u32[]{:S(2)}) collective-permute-start(bf16[448,256]{1,0:T(8,128)(2,1)S(1)} %get-tuple-element.36), channel_id=1, source_target_pairs={{0,8},{4,12},{8,0},{12,4},{16,24},{20,28},{24,16},{28,20},{1,9},{5... | collective-permute-start | bytes 688136 | tf_op jit(solution)/shard_map/ppermute | solution.py:162
  28.7 6.6 %collective-permute-start.19 = (bf16[448,256]{1,0:T(8,128)(2,1)S(1)}, bf16[448,256]{1,0:T(8,128)(2,1)S(1)}, u32[]{:S(2)}, u32[]{:S(2)}) collective-permute-start(bf16[448,256]{1,0:T(8,128)(2,1)S(1)} %shard_map.107.refs_0_.refs_9_), channel_id=1, source_target_pairs={{0,16},{4,20},{8,24},{12,28},{16,0},{20,4},{24,8},{28,12},{1,17},{... | collective-permute-start | bytes 688136 | tf_op jit(solution)/shard_map/ppermute | solution.py:162
  30.0 4.6 %collective-permute-start.17 = (bf16[64,1024]{1,0:T(8,128)(2,1)S(1)}, bf16[64,1024]{1,0:T(8,128)(2,1)S(1)}, u32[]{:S(2)}, u32[]{:S(2)}) collective-permute-start(bf16[64,1024]{1,0:T(8,128)(2,1)S(1)} %get-tuple-element.55), channel_id=1, source_target_pairs={{0,4},{4,0},{8,12},{12,8},{16,20},{20,16},{24,28},{28,24},{1,5},{5... | collective-permute-start | bytes 393224 | tf_op jit(solution)/shard_map/ppermute | solution.py:162
  30.0 4.5 %collective-permute-start.18 = (bf16[64,1024]{1,0:T(8,128)(2,1)S(1)}, bf16[64,1024]{1,0:T(8,128)(2,1)S(1)}, u32[]{:S(2)}, u32[]{:S(2)}) collective-permute-start(bf16[64,1024]{1,0:T(8,128)(2,1)S(1)} %get-tuple-element.54), channel_id=1, source_target_pairs={{0,4},{4,0},{8,12},{12,8},{16,20},{20,16},{24,28},{28,24},{1,5},{5... | collective-permute-start | bytes 393224 | tf_op jit(solution)/shard_map/ppermute | solution.py:162
  33.0 7.1 %collective-permute-start.23 = (bf16[448,256]{1,0:T(8,128)(2,1)S(1)}, bf16[448,256]{1,0:T(8,128)(2,1)S(1)}, u32[]{:S(2)}, u32[]{:S(2)}) collective-permute-start(bf16[448,256]{1,0:T(8,128)(2,1)S(1)} %shard_map.108.refs_1_.refs_9_), channel_id=1, source_target_pairs={{0,16},{4,20},{8,24},{12,28},{16,0},{20,4},{24,8},{28,12},{1,17},{... | collective-permute-start | bytes 688136 | tf_op jit(solution)/shard_map/ppermute | solution.py:162
  36.1 8.1 %collective-permute-start.20 = (bf16[512,256]{1,0:T(8,128)(2,1)S(1)}, bf16[512,256]{1,0:T(8,128)(2,1)S(1)}, u32[]{:S(2)}, u32[]{:S(2)}) collective-permute-start(bf16[512,256]{1,0:T(8,128)(2,1)S(1)} %get-tuple-element.47), channel_id=1, source_target_pairs={{0,1},{1,0},{2,3},{3,2},{4,5},{5,4},{6,7},{7,6},{8,9},{9,8},{10,11... | collective-permute-start | bytes 786440 | tf_op jit(solution)/shard_map/ppermute | solution.py:162
  41.0 10.7 %collective-permute-start.24 = (bf16[512,256]{1,0:T(8,128)(2,1)S(1)}, bf16[512,256]{1,0:T(8,128)(2,1)S(1)}, u32[]{:S(2)}, u32[]{:S(2)}) collective-permute-start(bf16[512,256]{1,0:T(8,128)(2,1)S(1)} %get-tuple-element.51), channel_id=1, source_target_pairs={{0,1},{1,0},{2,3},{3,2},{4,5},{5,4},{6,7},{7,6},{8,9},{9,8},{10,11... | collective-permute-start | bytes 786440 | tf_op jit(solution)/shard_map/ppermute | solution.py:162
  42.8 16.5 %collective-permute-start.14 = (bf16[128,1536]{1,0:T(8,128)(2,1)S(1)}, bf16[128,1536]{1,0:T(8,128)(2,1)S(1)}, u32[]{:S(2)}, u32[]{:S(2)}) collective-permute-start(bf16[128,1536]{1,0:T(8,128)(2,1)S(1)} %get-tuple-element.40), channel_id=1, source_target_pairs={{0,4},{4,0},{8,12},{12,8},{16,20},{20,16},{24,28},{28,24},{1,5},{5... | collective-permute-start | bytes 1179656 | tf_op jit(solution)/shard_map/ppermute | solution.py:162
  44.2 8.7 %collective-permute-start.21 = (bf16[256,256]{1,0:T(8,128)(2,1)S(1)}, bf16[256,256]{1,0:T(8,128)(2,1)S(1)}, u32[]{:S(2)}, u32[]{:S(2)}) collective-permute-start(bf16[256,256]{1,0:T(8,128)(2,1)S(1)} %shard_map.113.refs_2_), channel_id=1, source_target_pairs={{0,2},{1,3},{2,0},{3,1},{4,6},{5,7},{6,4},{7,5},{8,10},{9,11},{10,... | collective-permute-start | bytes 393224 | tf_op jit(solution)/shard_map/ppermute | solution.py:162
  51.7 7.4 %collective-permute-start.25 = (bf16[256,256]{1,0:T(8,128)(2,1)S(1)}, bf16[256,256]{1,0:T(8,128)(2,1)S(1)}, u32[]{:S(2)}, u32[]{:S(2)}) collective-permute-start(bf16[256,256]{1,0:T(8,128)(2,1)S(1)} %shard_map.116), channel_id=1, source_target_pairs={{0,2},{1,3},{2,0},{3,1},{4,6},{5,7},{6,4},{7,5},{8,10},{9,11},{10,... | collective-permute-start | bytes 393224 | tf_op jit(solution)/shard_map/ppermute | solution.py:162
  52.9 7.3 %collective-permute-start.22 = (f32[128,256]{1,0:T(8,128)S(1)}, f32[128,256]{1,0:T(8,128)S(1)}, u32[]{:S(2)}, u32[]{:S(2)}) collective-permute-start(f32[128,256]{1,0:T(8,128)S(1)} %get-tuple-element.49), channel_id=1, source_target_pairs={{0,4},{4,0},{8,12},{12,8},{16,20},{20,16},{24,28},{28,24},{1,5},{5... | collective-permute-start | bytes 393224 | tf_op jit(solution)/shard_map/ppermute | solution.py:162
  59.2 1.4 %collective-permute-start.26 = (f32[128,256]{1,0:T(8,128)S(1)}, f32[128,256]{1,0:T(8,128)S(1)}, u32[]{:S(2)}, u32[]{:S(2)}) collective-permute-start(f32[128,256]{1,0:T(8,128)S(1)} %get-tuple-element.53), channel_id=1, source_target_pairs={{0,4},{4,0},{8,12},{12,8},{16,20},{20,16},{24,28},{28,24},{1,5},{5... | collective-permute-start | bytes 393224 | tf_op jit(solution)/shard_map/ppermute | solution.py:162
  (2 other events, 5.1 us)
